TPU v7x, 32 devices: a whole 2x2x4 slice. The times are simulated.
32 devices in a mesh: segment: 2 (over core), dom: 8 (over z, y), rep: 2 (over x).
Axes of the slice: x: 2, y: 2, z: 4, core: 2. Of those that a mesh axis runs over, the one named last changes fastest.
Arguments:
- node_latent: bfloat16 [4, 1024, 512], P('rep', 'dom'), may hold values from -6 to 6
- edge_latent: bfloat16 [4, 3072, 512], P('rep', 'dom'), may hold values from -6 to 6
- node_cot: bfloat16 [4, 1024, 512], P('rep', 'dom'), may hold values from -6 to 6
- edge_src: int32 [3072], P('dom'), may hold values from 0 to 191, as said below
- edge_dst: int32 [3072], P('dom'), may hold values from 0 to 127
- edge_count: int32 [8], P('dom'), may hold values from 192 to 384, as said below
- send_index: int32 [8, 4, 16], P('dom'), may hold values from 0 to 127, as said below
- w_edge_in: bfloat16 [2, 1536, 512], P('segment'), may hold values from -0.15625 to 0.15625
- w_edge_out: bfloat16 [2, 512, 512], P('segment'), may hold values from -0.25 to 0.25
- w_node_in: bfloat16 [2, 1024, 512], P('segment'), may hold values from -0.1875 to 0.1875
- w_node_out: bfloat16 [2, 512, 512], P('segment'), may hold values from -0.25 to 0.25
- gain_edge: float32 [2, 512], P('segment'), may hold values from 0.1 to 1.9
- gain_node: float32 [2, 512], P('segment'), may hold values from 0.1 to 1.9
Outputs:
- node_pair: bfloat16 [2, 4, 1024, 512], P('segment', 'rep', 'dom')
- edge_pair: bfloat16 [2, 4, 3072, 512], P('segment', 'rep', 'dom')
- grad_edge_in: float32 [2, 1536, 512], P('segment', ('dom', 'rep'))
- grad_edge_out: float32 [2, 512, 512], P('segment', ('dom', 'rep'))
- grad_node_in: float32 [2, 1024, 512], P('segment', ('dom', 'rep'))
- grad_node_out: float32 [2, 512, 512], P('segment', ('dom', 'rep'))
- grad_gain_edge: float32 [2, 512], P('segment', ('dom', 'rep'))
- grad_gain_node: float32 [2, 512], P('segment', ('dom', 'rep'))
Inputs may be any that keep to these rules, and one draw needn't show every extreme that they name: `edge_src`: each value is below 192; a value 128 + j * 16 + k of partition p refers to round j only where partition p - o_j exists. `edge_count`: some partition has all 384 slots live. `send_index`: the 16 rows of one partition and round are distinct.
All inputs are finite; a program needn't handle non-finite values.
Results may differ from a plain program's by a relative error of at most 0.039.
Values may be sent and summed in bfloat16 or wider, within the bound.
No kernel may reach another device: no remote copies, remote signals or barrier semaphores. Data moves between devices by JAX's collectives and lax.ppermute only.
A program may use at most 128 MiB of HBM per device.

v0:
```python
import jax
import jax.numpy as jnp
from jax import lax
from jax.sharding import PartitionSpec as P

NODE_DEV = 128


OFFSETS = (1, -1, 2, -2)
EPS = 1e-05


def shifted(block, axis, distance):
    devices = range(lax.axis_size(axis))
    route = [(i - distance, i) for i in devices if i - distance in devices]
    return lax.ppermute(block, axis, route)


def norm_rows(values, gain):
    center = values - jnp.mean(values, axis=-1, keepdims=True)
    spread = jnp.mean(center * center, axis=-1, keepdims=True)
    return center * lax.rsqrt(spread + EPS) * gain


def layer(table, edges, weights, src, dst, live):
    w_ein, w_eout, w_nin, w_nout, g_edge, g_node = weights
    own = table[:NODE_DEV]
    sender = jnp.take(table, src, axis=0)
    receiver = jnp.take(table, dst, axis=0)
    joined = jnp.concatenate([edges, sender, receiver], axis=1)
    pre = jnp.dot(joined, w_ein.astype(jnp.bfloat16), preferred_element_type=jnp.float32)
    middle = jax.nn.silu(pre).astype(jnp.bfloat16)
    outer = jnp.dot(middle, w_eout.astype(jnp.bfloat16), preferred_element_type=jnp.float32)
    moved = edges.astype(jnp.float32)
    edge_new = jnp.where(live[:, None], moved + norm_rows(outer, g_edge), moved).astype(
        jnp.bfloat16
    )
    owners = jnp.arange(NODE_DEV, dtype=jnp.int32)
    incidence = ((dst[None, :] == owners[:, None]) & live[None, :]).astype(jnp.bfloat16)
    summed = jnp.dot(incidence, edge_new, preferred_element_type=jnp.float32).astype(jnp.bfloat16)
    node_in = jnp.concatenate([own, summed], axis=1)
    pre_node = jnp.dot(node_in, w_nin.astype(jnp.bfloat16), preferred_element_type=jnp.float32)
    mid_node = jax.nn.silu(pre_node).astype(jnp.bfloat16)
    out_node = jnp.dot(mid_node, w_nout.astype(jnp.bfloat16), preferred_element_type=jnp.float32)
    node_new = (own.astype(jnp.float32) + norm_rows(out_node, g_node)).astype(jnp.bfloat16)
    return (node_new, edge_new)


def build_table(own, rounds):
    parts = [own]
    for j, step in enumerate(OFFSETS):
        sent = jnp.take(own, rounds[j], axis=0)
        parts.append(shifted(sent, "dom", step))
    return jnp.concatenate(parts, axis=0)


def return_halo(d_table, rounds):
    halo = rounds.shape[1]
    d_own = d_table[:NODE_DEV].astype(jnp.float32)
    owners = jnp.arange(NODE_DEV, dtype=jnp.int32)
    for j, step in enumerate(OFFSETS):
        piece = d_table[NODE_DEV + j * halo : NODE_DEV + (j + 1) * halo]
        back = shifted(piece, "dom", -step)
        incidence = (rounds[j][None, :] == owners[:, None]).astype(jnp.bfloat16)
        d_own = d_own + jnp.dot(incidence, back, preferred_element_type=jnp.float32)
    return d_own.astype(jnp.bfloat16)


def body(
    node_latent,
    edge_latent,
    node_cot,
    edge_src,
    edge_dst,
    edge_count,
    send_index,
    w_edge_in,
    w_edge_out,
    w_node_in,
    w_node_out,
    gain_edge,
    gain_node,
):
    micro = node_latent.shape[0]
    edge_rows = edge_latent.shape[1]
    first = lax.axis_index("segment") == 0
    weights = (
        w_edge_in[0].astype(jnp.float32),
        w_edge_out[0].astype(jnp.float32),
        w_node_in[0].astype(jnp.float32),
        w_node_out[0].astype(jnp.float32),
        gain_edge[0],
        gain_node[0],
    )
    live = jnp.arange(edge_rows, dtype=jnp.int32) < edge_count[0]
    rounds = send_index[0]
    inbound_node = jnp.zeros_like(node_latent[0])
    inbound_edge = jnp.zeros_like(edge_latent[0])
    saved_tables, saved_edges, outs_node, outs_edge = ([], [], [], [])
    for tick in range(micro + 1):
        pick = min(tick, micro - 1)
        enter_node = jnp.where(first, node_latent[pick], inbound_node)
        enter_edge = jnp.where(first, edge_latent[pick], inbound_edge)
        table = build_table(enter_node, rounds)
        node_new, edge_new = layer(table, enter_edge, weights, edge_src, edge_dst, live)
        saved_tables.append(table)
        saved_edges.append(enter_edge)
        outs_node.append(node_new)
        outs_edge.append(edge_new)
        if tick < micro:
            inbound_node, inbound_edge = shifted((node_new, edge_new), "segment", 1)
    factor = float(micro * lax.axis_size("rep") * NODE_DEV * lax.axis_size("dom")) ** (-0.5)
    total = jax.tree.map(jnp.zeros_like, weights)
    shares = None
    back_node = jnp.zeros_like(node_latent[0])
    back_edge = jnp.zeros_like(edge_latent[0])
    grad_nodes = [None] * micro
    grad_edges = [None] * micro
    for tick in range(micro + 1):
        late = min(tick + 1, micro)
        early = max(tick - 1, 0)
        table = jnp.where(first, saved_tables[early], saved_tables[late])
        edges = jnp.where(first, saved_edges[early], saved_edges[late])
        valid = jnp.where(first, tick >= 1, tick < micro)
        cot_node = jnp.where(first, back_node, node_cot[min(tick, micro - 1)])
        cot_edge = jnp.where(first, back_edge, jnp.zeros_like(back_edge))
        _, pull = jax.vjp(
            lambda a, b, w: layer(a, b, w, edge_src, edge_dst, live), table, edges, weights
        )
        d_table, d_edges, d_weights = pull((cot_node, cot_edge))
        d_own = return_halo(d_table, rounds)
        term = jax.tree.map(lambda g: jnp.where(valid, g, 0.0), d_weights)
        total = jax.tree.map(lambda x, y: x + y, total, term)
        if tick >= 1:
            grad_nodes[tick - 1] = d_own
            grad_edges[tick - 1] = d_edges
        if tick < micro:
            back_node, back_edge = shifted((d_own, d_edges), "segment", -1)
    shares = lax.psum_scatter(tuple(total), ("dom", "rep"), scatter_dimension=0, tiled=True)
    node_out = jnp.stack([jnp.where(first, grad_nodes[m], outs_node[m + 1]) for m in range(micro)])[
        None
    ]
    edge_out = jnp.stack([jnp.where(first, grad_edges[m], outs_edge[m + 1]) for m in range(micro)])[
        None
    ]
    scaled = [(piece * factor)[None] for piece in shares]
    return (node_out, edge_out, scaled[0], scaled[1], scaled[2], scaled[3], scaled[4], scaled[5])


def solution(mesh):
    placed = (
        P("rep", "dom", None),
        P("rep", "dom", None),
        P("rep", "dom", None),
        P("dom"),
        P("dom"),
        P("dom"),
        P("dom", None, None),
        P("segment", None, None),
        P("segment", None, None),
        P("segment", None, None),
        P("segment", None, None),
        P("segment", None),
        P("segment", None),
    )
    return jax.shard_map(
        body,
        mesh=mesh,
        in_specs=placed,
        out_specs=(
            P("segment", "rep", "dom", None),
            P("segment", "rep", "dom", None),
            P("segment", ("dom", "rep"), None),
            P("segment", ("dom", "rep"), None),
            P("segment", ("dom", "rep"), None),
            P("segment", ("dom", "rep"), None),
            P("segment", ("dom", "rep")),
            P("segment", ("dom", "rep")),
        ),
        check_vma=False,
    )
```

profile of v0, /device:TPU:0, one launch (start us, length us, event | category | flops | bytes accessed | tf_op | source)
XLA Modules:
  0.0 613.8 jit_solution(12364113593664068911)
XLA Ops:
  9.8 4.9 collective-permute-start
  17.4 5.5 collective-permute-start.2
  30.5 2.1 gather_fusion.5
  32.6 2.1 gather_fusion.4
  34.9 3.1 fusion.390
  39.5 2.3 fusion.96
  47.7 2.1 collective-permute-start.5
  54.8 2.5 collective-permute-start.6
  59.3 7.5 %collective-permute-start.8 = (bf16[16,512]{1,0:T(8,128)(2,1)S(1)}, bf16[16,512]{1,0:T(8,128)(2,1)S(1)}, u32[]{:S(2)}, u32[]{:S(2)}) collective-permute-start(bf16[16,512]{1,0:T(8,128)(2,1)S(1)} %broadcast_select_fusion.22), channel_id=1, source_target_pairs={{0,4},{2,6},{4,8},{6,10},{8,12},{10,14},{1,5},{3,7},{5,9},{7,11},{... | collective-permute-start | bytes 49160 | tf_op jit(solution)/shard_map/ppermute | solution.py:16
  68.2 4.2 collective-permute-done.9
  72.4 2.6 gather_fusion.11
  75.0 2.1 gather_fusion.10
  81.4 4.0 fusion.400
  87.5 2.2 fusion.97
  90.9 2.2 fusion.405
  106.3 6.9 %collective-permute-start.13 = (bf16[16,512]{1,0:T(8,128)(2,1)S(1)}, bf16[16,512]{1,0:T(8,128)(2,1)S(1)}, u32[]{:S(2)}, u32[]{:S(2)}) collective-permute-start(bf16[16,512]{1,0:T(8,128)(2,1)S(1)} %broadcast_select_fusion.21), channel_id=1, source_target_pairs={{0,4},{2,6},{4,8},{6,10},{8,12},{10,14},{1,5},{3,7},{5,9},{7,11},{... | collective-permute-start | bytes 49160 | tf_op jit(solution)/shard_map/ppermute | solution.py:16
  115.0 3.8 collective-permute-done.14
  119.6 2.6 gather_fusion.18
  124.2 2.1 gather_fusion.21
  126.3 2.6 gather_fusion.20
  130.9 2.6 gather_fusion.16
  133.5 2.6 gather_fusion.23
  136.1 2.6 gather_fusion.22
  138.6 2.6 broadcast_select_fusion
  155.8 3.6 scatter_custom_fusion.1
  159.4 3.4 scatter_custom_fusion
  162.8 3.0 fusion.21
  170.7 6.9 %collective-permute-start.19 = (bf16[16,512]{1,0:T(8,128)(2,1)S(1)}, bf16[16,512]{1,0:T(8,128)(2,1)S(1)}, u32[]{:S(2)}, u32[]{:S(2)}) collective-permute-start(bf16[16,512]{1,0:T(8,128)(2,1)S(1)} %get-tuple-element.94), channel_id=1, source_target_pairs={{0,4},{2,6},{4,8},{6,10},{8,12},{10,14},{1,5},{3,7},{5,9},{7,11},{... | collective-permute-start | bytes 49160 | tf_op jit(solution)/shard_map/ppermute | solution.py:16
  180.4 2.8 collective-permute-done.18
  204.2 4.2 scatter_custom_fusion.3
  208.4 4.0 scatter_custom_fusion.2
  216.9 6.1 collective-permute-start.25
  225.0 3.5 collective-permute-done.24
  232.6 2.2 select_bitcast_fusion
  239.9 2.3 fusion.19
  243.4 2.2 fusion.95
  253.9 2.5 convolution_convert_fusion.1
  259.2 3.0 select_add_fusion
  264.1 3.9 fusion.416
  277.6 4.0 scatter_custom_fusion.5
  281.6 4.0 scatter_custom_fusion.4
  291.2 38.8 %all-reduce.5 = (f32[512]{0:T(512)}, f32[512]{0:T(512)}) all-reduce(f32[512]{0:T(512)} %select_add_fusion.5, f32[512]{0:T(512)} %select_add_fusion.4), channel_id=6, replica_groups=mesh['segment'=2,'dom'=8,'rep'=2] {'dom','rep'}, use_global_device_ids=true, to_apply=%region_49.53.clone | all-reduce | flops 1024 | bytes 8192
  331.3 2.5 fusion.174
  334.7 2.4 fusion.421
  346.0 3.5 collective-permute-done.30
  352.3 41.1 %reduce-scatter.7.cloned.1.call-done = f32[32,512]{1,0:T(8,128)} async-done(((f32[512,512]{1,0:T(8,128)}), f32[32,512]{1,0:T(8,128)}) %reduce-scatter.7.cloned.1.call-update) | async-done | bytes 65552 | tf_op jit(solution)/shard_map/reduce_scatter | solution.py:139
  394.9 77.6 %reduce-scatter.9.cloned.1.call-done = f32[64,512]{1,0:T(8,128)} async-done(((f32[1024,512]{1,0:T(8,128)}), f32[64,512]{1,0:T(8,128)}) %reduce-scatter.9.cloned.1.call-update) | async-done | bytes 131088 | tf_op jit(solution)/shard_map/reduce_scatter | solution.py:139
  474.1 131.1 %reduce-scatter.5.cloned.1.call-done = f32[96,512]{1,0:T(8,128)} async-done(((f32[1536,512]{1,0:T(8,128)}), f32[96,512]{1,0:T(8,128)}) %reduce-scatter.5.cloned.1.call-update) | async-done | bytes 196624 | tf_op jit(solution)/shard_map/reduce_scatter | solution.py:139
  (546 shorter events, 159.8 us)
Async XLA Ops:
  7.2 27.8 %copy-start = (bf16[1,1536,512]{2,1,0:T(8,128)(2,1)S(1)}, bf16[1,1536,512]{2,1,0:T(8,128)(2,1)}, u32[]{:S(2)}) copy-start(bf16[1,1536,512]{2,1,0:T(8,128)(2,1)} %param.26) | copy-start | bytes 4718596
  7.2 343.6 %reduce-scatter.11.cloned.1.call-start = ((), (), s32[]{:S(2)}) async-start(), calls=%async_computation.7 | async-start | bytes 1114112 | tf_op jit(solution)/shard_map/reduce_scatter | solution.py:139
  8.1 22.3 %copy-start.87 = (pred[16]{0:T(512)(128)(4,1)}, pred[16]{0:T(512)(128)(4,1)S(1)}, u32[]{:S(2)}) copy-start(pred[16]{0:T(512)(128)(4,1)S(1)} %get-tuple-element.106) | copy-start | bytes 52
  8.1 22.3 %copy-start.89 = (pred[16]{0:T(512)(128)(4,1)}, pred[16]{0:T(512)(128)(4,1)S(1)}, u32[]{:S(2)}) copy-start(pred[16]{0:T(512)(128)(4,1)S(1)} %get-tuple-element.108) | copy-start | bytes 52
  9.8 20.6 %collective-permute-start = (bf16[16,512]{1,0:T(8,128)(2,1)S(1)}, bf16[16,512]{1,0:T(8,128)(2,1)S(1)}, u32[]{:S(2)}, u32[]{:S(2)}) collective-permute-start(bf16[16,512]{1,0:T(8,128)(2,1)S(1)} %broadcast_select_fusion.29), channel_id=1, source_target_pairs={{0,2},{2,4},{4,6},{6,8},{8,10},{10,12},{12,14},{1,3},{3,5},{5,7},{... | collective-permute-start | bytes 49160 | tf_op jit(solution)/shard_map/ppermute | solution.py:16
  15.3 15.1 %collective-permute-start.1 = (bf16[16,512]{1,0:T(8,128)(2,1)S(1)}, bf16[16,512]{1,0:T(8,128)(2,1)S(1)}, u32[]{:S(2)}, u32[]{:S(2)}) collective-permute-start(bf16[16,512]{1,0:T(8,128)(2,1)S(1)} %broadcast_select_fusion.26), channel_id=1, source_target_pairs={{2,0},{4,2},{6,4},{8,6},{10,8},{12,10},{14,12},{3,1},{5,3},{7,5},{... | collective-permute-start | bytes 49160 | tf_op jit(solution)/shard_map/ppermute | solution.py:16
  17.4 13.1 %collective-permute-start.2 = (bf16[16,512]{1,0:T(8,128)(2,1)S(1)}, bf16[16,512]{1,0:T(8,128)(2,1)S(1)}, u32[]{:S(2)}, u32[]{:S(2)}) collective-permute-start(bf16[16,512]{1,0:T(8,128)(2,1)S(1)} %broadcast_select_fusion.23), channel_id=1, source_target_pairs={{0,4},{2,6},{4,8},{6,10},{8,12},{10,14},{1,5},{3,7},{5,9},{7,11},{... | collective-permute-start | bytes 49160 | tf_op jit(solution)/shard_map/ppermute | solution.py:16
  23.6 6.9 %collective-permute-start.3 = (bf16[16,512]{1,0:T(8,128)(2,1)S(1)}, bf16[16,512]{1,0:T(8,128)(2,1)S(1)}, u32[]{:S(2)}, u32[]{:S(2)}) collective-permute-start(bf16[16,512]{1,0:T(8,128)(2,1)S(1)} %broadcast_select_fusion.20), channel_id=1, source_target_pairs={{4,0},{6,2},{8,4},{10,6},{12,8},{14,10},{5,1},{7,3},{9,5},{11,7},{... | collective-permute-start | bytes 49160 | tf_op jit(solution)/shard_map/ppermute | solution.py:16
  46.4 3.4 collective-permute-start.4
  47.7 32.9 %collective-permute-start.5 = (bf16[384,512]{1,0:T(8,128)(2,1)}, bf16[384,512]{1,0:T(8,128)(2,1)}, u32[]{:S(2)}, u32[]{:S(2)}) collective-permute-start(bf16[384,512]{1,0:T(8,128)(2,1)} %fusion.96), channel_id=1, source_target_pairs={{0,16},{1,17},{2,18},{3,19},{4,20},{5,21},{6,22},{7,23},{8,24},{9,... | collective-permute-start | bytes 1179656 | tf_op jit(solution)/shard_map/ppermute | solution.py:16
  54.8 13.3 %collective-permute-start.6 = (bf16[16,512]{1,0:T(8,128)(2,1)S(1)}, bf16[16,512]{1,0:T(8,128)(2,1)S(1)}, u32[]{:S(2)}, u32[]{:S(2)}) collective-permute-start(bf16[16,512]{1,0:T(8,128)(2,1)S(1)} %broadcast_select_fusion.28), channel_id=1, source_target_pairs={{0,2},{2,4},{4,6},{6,8},{8,10},{10,12},{12,14},{1,3},{3,5},{5,7},{... | collective-permute-start | bytes 49160 | tf_op jit(solution)/shard_map/ppermute | solution.py:16
  58.0 10.1 %collective-permute-start.7 = (bf16[16,512]{1,0:T(8,128)(2,1)S(1)}, bf16[16,512]{1,0:T(8,128)(2,1)S(1)}, u32[]{:S(2)}, u32[]{:S(2)}) collective-permute-start(bf16[16,512]{1,0:T(8,128)(2,1)S(1)} %broadcast_select_fusion.25), channel_id=1, source_target_pairs={{2,0},{4,2},{6,4},{8,6},{10,8},{12,10},{14,12},{3,1},{5,3},{7,5},{... | collective-permute-start | bytes 49160 | tf_op jit(solution)/shard_map/ppermute | solution.py:16
  59.3 8.9 %collective-permute-start.8 = (bf16[16,512]{1,0:T(8,128)(2,1)S(1)}, bf16[16,512]{1,0:T(8,128)(2,1)S(1)}, u32[]{:S(2)}, u32[]{:S(2)}) collective-permute-start(bf16[16,512]{1,0:T(8,128)(2,1)S(1)} %broadcast_select_fusion.22), channel_id=1, source_target_pairs={{0,4},{2,6},{4,8},{6,10},{8,12},{10,14},{1,5},{3,7},{5,9},{7,11},{... | collective-permute-start | bytes 49160 | tf_op jit(solution)/shard_map/ppermute | solution.py:16
  66.8 5.6 collective-permute-start.9
  94.0 24.8 %copy-start.39 = (bf16[128,512]{1,0:T(8,128)(2,1)}, bf16[128,512]{1,0:T(8,128)(2,1)S(1)}, u32[]{:S(2)}) copy-start(bf16[128,512]{1,0:T(8,128)(2,1)S(1)} %add_convert_fusion.2) | copy-start | bytes 393220
  94.1 4.8 collective-permute-start.10
  96.8 88.5 %collective-permute-start.21 = (bf16[384,512]{1,0:T(8,128)(2,1)}, bf16[384,512]{1,0:T(8,128)(2,1)}, u32[]{:S(2)}, u32[]{:S(2)}) collective-permute-start(bf16[384,512]{1,0:T(8,128)(2,1)} %fusion.97), channel_id=1, source_target_pairs={{0,16},{1,17},{2,18},{3,19},{4,20},{5,21},{6,22},{7,23},{8,24},{9,... | collective-permute-start | bytes 1179656 | tf_op jit(solution)/shard_map/ppermute | solution.py:16
  102.9 12.1 %collective-permute-start.11 = (bf16[16,512]{1,0:T(8,128)(2,1)S(1)}, bf16[16,512]{1,0:T(8,128)(2,1)S(1)}, u32[]{:S(2)}, u32[]{:S(2)}) collective-permute-start(bf16[16,512]{1,0:T(8,128)(2,1)S(1)} %broadcast_select_fusion.27), channel_id=1, source_target_pairs={{0,2},{2,4},{4,6},{6,8},{8,10},{10,12},{12,14},{1,3},{3,5},{5,7},{... | collective-permute-start | bytes 49160 | tf_op jit(solution)/shard_map/ppermute | solution.py:16
  105.0 10.0 %collective-permute-start.12 = (bf16[16,512]{1,0:T(8,128)(2,1)S(1)}, bf16[16,512]{1,0:T(8,128)(2,1)S(1)}, u32[]{:S(2)}, u32[]{:S(2)}) collective-permute-start(bf16[16,512]{1,0:T(8,128)(2,1)S(1)} %broadcast_select_fusion.24), channel_id=1, source_target_pairs={{2,0},{4,2},{6,4},{8,6},{10,8},{12,10},{14,12},{3,1},{5,3},{7,5},{... | collective-permute-start | bytes 49160 | tf_op jit(solution)/shard_map/ppermute | solution.py:16
  106.3 8.7 %collective-permute-start.13 = (bf16[16,512]{1,0:T(8,128)(2,1)S(1)}, bf16[16,512]{1,0:T(8,128)(2,1)S(1)}, u32[]{:S(2)}, u32[]{:S(2)}) collective-permute-start(bf16[16,512]{1,0:T(8,128)(2,1)S(1)} %broadcast_select_fusion.21), channel_id=1, source_target_pairs={{0,4},{2,6},{4,8},{6,10},{8,12},{10,14},{1,5},{3,7},{5,9},{7,11},{... | collective-permute-start | bytes 49160 | tf_op jit(solution)/shard_map/ppermute | solution.py:16
  113.2 5.6 collective-permute-start.14
  165.8 17.4 %copy-start.99 = (s32[16]{0:T(128)S(1)}, s32[16]{0:T(128)}, u32[]{:S(2)}) copy-start(s32[16]{0:T(128)} %get-tuple-element.103) | copy-start | bytes 196
  165.9 17.5 %copy-start.97 = (s32[16]{0:T(128)S(1)}, s32[16]{0:T(128)}, u32[]{:S(2)}) copy-start(s32[16]{0:T(128)} %get-tuple-element.102) | copy-start | bytes 196
  165.9 17.7 %copy-start.95 = (s32[16]{0:T(128)S(1)}, s32[16]{0:T(128)}, u32[]{:S(2)}) copy-start(s32[16]{0:T(128)} %get-tuple-element.100) | copy-start | bytes 196
  165.9 13.0 %collective-permute-start.17 = (bf16[16,512]{1,0:T(8,128)(2,1)S(1)}, bf16[16,512]{1,0:T(8,128)(2,1)S(1)}, u32[]{:S(2)}, u32[]{:S(2)}) collective-permute-start(bf16[16,512]{1,0:T(8,128)(2,1)S(1)} %get-tuple-element.96), channel_id=1, source_target_pairs={{0,2},{2,4},{4,6},{6,8},{8,10},{10,12},{12,14},{1,3},{3,5},{5,7},{... | collective-permute-start | bytes 49160 | tf_op jit(solution)/shard_map/ppermute | solution.py:16
  169.2 16.1 %copy-start.4 = (bf16[2,384,512]{2,1,0:T(8,128)(2,1)S(1)}, bf16[2,384,512]{2,1,0:T(8,128)(2,1)}, u32[]{:S(2)}) copy-start(bf16[2,384,512]{2,1,0:T(8,128)(2,1)} %param.20) | copy-start | bytes 2359300
  169.2 16.1 %copy-start.7 = (bf16[384,512]{1,0:T(8,128)(2,1)S(1)}, bf16[384,512]{1,0:T(8,128)(2,1)}, u32[]{:S(2)}) copy-start(bf16[384,512]{1,0:T(8,128)(2,1)} %copy-done.6) | copy-start | bytes 1179652
  169.2 19.1 %copy-start.21 = (bf16[128,512]{1,0:T(8,128)(2,1)}, bf16[128,512]{1,0:T(8,128)(2,1)S(1)}, u32[]{:S(2)}) copy-start(bf16[128,512]{1,0:T(8,128)(2,1)S(1)} %slice.199) | copy-start | bytes 393220
  169.2 22.9 %copy-start.22 = (bf16[128,512]{1,0:T(8,128)(2,1)}, bf16[128,512]{1,0:T(8,128)(2,1)S(1)}, u32[]{:S(2)}) copy-start(bf16[128,512]{1,0:T(8,128)(2,1)S(1)} %slice.193) | copy-start | bytes 393220
  169.3 14.3 %collective-permute-start.16 = (bf16[16,512]{1,0:T(8,128)(2,1)S(1)}, bf16[16,512]{1,0:T(8,128)(2,1)S(1)}, u32[]{:S(2)}, u32[]{:S(2)}) collective-permute-start(bf16[16,512]{1,0:T(8,128)(2,1)S(1)} %get-tuple-element.93), channel_id=1, source_target_pairs={{2,0},{4,2},{6,4},{8,6},{10,8},{12,10},{14,12},{3,1},{5,3},{7,5},{... | collective-permute-start | bytes 49160 | tf_op jit(solution)/shard_map/ppermute | solution.py:16
  170.7 12.7 %collective-permute-start.19 = (bf16[16,512]{1,0:T(8,128)(2,1)S(1)}, bf16[16,512]{1,0:T(8,128)(2,1)S(1)}, u32[]{:S(2)}, u32[]{:S(2)}) collective-permute-start(bf16[16,512]{1,0:T(8,128)(2,1)S(1)} %get-tuple-element.94), channel_id=1, source_target_pairs={{0,4},{2,6},{4,8},{6,10},{8,12},{10,14},{1,5},{3,7},{5,9},{7,11},{... | collective-permute-start | bytes 49160 | tf_op jit(solution)/shard_map/ppermute | solution.py:16
  177.6 5.6 collective-permute-start.18
  178.9 19.4 %collective-permute-start.15 = (bf16[384,512]{1,0:T(8,128)(2,1)S(1)}, bf16[384,512]{1,0:T(8,128)(2,1)S(1)}, u32[]{:S(2)}, u32[]{:S(2)}) collective-permute-start(bf16[384,512]{1,0:T(8,128)(2,1)S(1)} %fusion.168), channel_id=1, source_target_pairs={{16,0},{17,1},{18,2},{19,3},{20,4},{21,5},{22,6},{23,7},{24,8},{25... | collective-permute-start | bytes 1179656 | tf_op jit(solution)/shard_map/ppermute | solution.py:16
  183.8 9.9 %collective-permute-start.20 = (bf16[128,512]{1,0:T(8,128)(2,1)S(1)}, bf16[128,512]{1,0:T(8,128)(2,1)S(1)}, u32[]{:S(2)}, u32[]{:S(2)}) collective-permute-start(bf16[128,512]{1,0:T(8,128)(2,1)S(1)} %fusion.57), channel_id=1, source_target_pairs={{16,0},{17,1},{18,2},{19,3},{20,4},{21,5},{22,6},{23,7},{24,8},{25... | collective-permute-start | bytes 393224 | tf_op jit(solution)/shard_map/ppermute | solution.py:16
  212.4 20.1 %copy-start.16 = (bf16[384,512]{1,0:T(8,128)(2,1)S(1)}, bf16[384,512]{1,0:T(8,128)(2,1)}, u32[]{:S(2)}) copy-start(bf16[384,512]{1,0:T(8,128)(2,1)} %copy-done.15) | copy-start | bytes 1179652
  213.6 10.6 %collective-permute-start.23 = (bf16[16,512]{1,0:T(8,128)(2,1)S(1)}, bf16[16,512]{1,0:T(8,128)(2,1)S(1)}, u32[]{:S(2)}, u32[]{:S(2)}) collective-permute-start(bf16[16,512]{1,0:T(8,128)(2,1)S(1)} %get-tuple-element.92), channel_id=1, source_target_pairs={{0,2},{2,4},{4,6},{6,8},{8,10},{10,12},{12,14},{1,3},{3,5},{5,7},{... | collective-permute-start | bytes 49160 | tf_op jit(solution)/shard_map/ppermute | solution.py:16
  215.6 14.7 %collective-permute-start.22 = (bf16[16,512]{1,0:T(8,128)(2,1)S(1)}, bf16[16,512]{1,0:T(8,128)(2,1)S(1)}, u32[]{:S(2)}, u32[]{:S(2)}) collective-permute-start(bf16[16,512]{1,0:T(8,128)(2,1)S(1)} %get-tuple-element.89), channel_id=1, source_target_pairs={{2,0},{4,2},{6,4},{8,6},{10,8},{12,10},{14,12},{3,1},{5,3},{7,5},{... | collective-permute-start | bytes 49160 | tf_op jit(solution)/shard_map/ppermute | solution.py:16
  216.9 12.6 %collective-permute-start.25 = (bf16[16,512]{1,0:T(8,128)(2,1)S(1)}, bf16[16,512]{1,0:T(8,128)(2,1)S(1)}, u32[]{:S(2)}, u32[]{:S(2)}) collective-permute-start(bf16[16,512]{1,0:T(8,128)(2,1)S(1)} %get-tuple-element.90), channel_id=1, source_target_pairs={{0,4},{2,6},{4,8},{6,10},{8,12},{10,14},{1,5},{3,7},{5,9},{7,11},{... | collective-permute-start | bytes 49160 | tf_op jit(solution)/shard_map/ppermute | solution.py:16
  222.9 5.6 collective-permute-start.24
  231.1 5.1 collective-permute-start.27
  234.8 8.4 %collective-permute-start.26 = (bf16[384,512]{1,0:T(8,128)(2,1)}, bf16[384,512]{1,0:T(8,128)(2,1)}, u32[]{:S(2)}, u32[]{:S(2)}) collective-permute-start(bf16[384,512]{1,0:T(8,128)(2,1)} %get-tuple-element.49), channel_id=1, source_target_pairs={{16,0},{17,1},{18,2},{19,3},{20,4},{21,5},{22,6},{23,7},{24,8},{25... | collective-permute-start | bytes 1179656 | tf_op jit(solution)/shard_map/ppermute | solution.py:16
  239.8 153.7 %reduce-scatter.7.cloned.1.call-start = ((), (), s32[]{:S(2)}) async-start(), calls=%async_computation.5 | async-start | bytes 1114112 | tf_op jit(solution)/shard_map/reduce_scatter | solution.py:139
  248.5 224.0 %reduce-scatter.9.cloned.1.call-start = ((), (), s32[]{:S(2)}) async-start(), calls=%async_computation.6 | async-start | bytes 2228224 | tf_op jit(solution)/shard_map/reduce_scatter | solution.py:139
  253.6 351.6 %reduce-scatter.5.cloned.1.call-start = ((), (), s32[]{:S(2)}) async-start(), calls=%async_computation.4 | async-start | bytes 3342336 | tf_op jit(solution)/shard_map/reduce_scatter | solution.py:139
  288.1 57.0 %collective-permute-start.29 = (bf16[16,512]{1,0:T(8,128)(2,1)}, bf16[16,512]{1,0:T(8,128)(2,1)}, u32[]{:S(2)}, u32[]{:S(2)}) collective-permute-start(bf16[16,512]{1,0:T(8,128)(2,1)} %get-tuple-element.88), channel_id=1, source_target_pairs={{0,2},{2,4},{4,6},{6,8},{8,10},{10,12},{12,14},{1,3},{3,5},{5,7},{... | collective-permute-start | bytes 49160 | tf_op jit(solution)/shard_map/ppermute | solution.py:16
  340.6 9.2 %collective-permute-start.28 = (bf16[16,512]{1,0:T(8,128)(2,1)S(1)}, bf16[16,512]{1,0:T(8,128)(2,1)S(1)}, u32[]{:S(2)}, u32[]{:S(2)}) collective-permute-start(bf16[16,512]{1,0:T(8,128)(2,1)S(1)} %copy-done.84), channel_id=1, source_target_pairs={{2,0},{4,2},{6,4},{8,6},{10,8},{12,10},{14,12},{3,1},{5,3},{7,5},{... | collective-permute-start | bytes 49160 | tf_op jit(solution)/shard_map/ppermute | solution.py:16
  341.9 7.7 %collective-permute-start.31 = (bf16[16,512]{1,0:T(8,128)(2,1)S(1)}, bf16[16,512]{1,0:T(8,128)(2,1)S(1)}, u32[]{:S(2)}, u32[]{:S(2)}) collective-permute-start(bf16[16,512]{1,0:T(8,128)(2,1)S(1)} %copy-done.85), channel_id=1, source_target_pairs={{0,4},{2,6},{4,8},{6,10},{8,12},{10,14},{1,5},{3,7},{5,9},{7,11},{... | collective-permute-start | bytes 49160 | tf_op jit(solution)/shard_map/ppermute | solution.py:16
  343.8 5.7 collective-permute-start.30
  (131 other events, 469.1 us)
Sparse Core Ops, SparseCore 0:
  239.9 76.5 reduce-scatter.10
  318.9 74.5 reduce-scatter.6
  395.7 76.7 reduce-scatter.8
  477.3 127.7 reduce-scatter.4
where the time goes:
time: 624 us; the launch traced here: 614 us
  waiting for transfers between devices  268 us (43%)
  other arithmetic  89 us (14%)
  starting transfers between devices  78 us (12%)
  matrix products  68.6 us (11%)
  local copies, waits for them, and re-layouts  53.4 us (9%)
  blocking collectives  38.8 us (6%)
  between operations  18 us (3%)
    reduce_scatter x4, waiting for transfers between devices, body(): lax.psum_scatter(tuple(total), ('dom', 'rep'), scatter_dimension=0, tiled...  250 us
    ppermute x32, starting transfers between devices, shifted(): return lax.ppermute(block, axis, route)  77.6 us
    unnamed x1, blocking collectives  38.8 us
    dot_general x12, matrix products, layer(): jnp.dot(middle, w_eout.astype(jnp.bfloat16), preferred_element_type=jnp.f...  20.9 us
    ppermute x32, waiting for transfers between devices, shifted(): return lax.ppermute(block, axis, route)  18.1 us
    gather x6, local copies, waits for them, and re-layouts, layer(): receiver = jnp.take(table, dst, axis=0)  14.9 us
    unnamed x296, local copies, waits for them, and re-layouts  14.8 us
    dot_general x9, matrix products, layer(): jnp.dot(joined, w_ein.astype(jnp.bfloat16), preferred_element_type=jnp.fl...  14.4 us
  transfers between devices with their start and end apart: 36, of which 9 were waited for; matrix products, arithmetic and copies ran while one was open for 24% of the time, Pallas kernels for 0%

commit v1 on v0

v1 whole, which is shorter than its diff:
```python
import functools

import jax
import jax.numpy as jnp
from jax import lax
from jax.experimental import pallas as pl
from jax.experimental.pallas import tpu as pltpu
from jax.sharding import PartitionSpec as P

NODE_DEV = 128
HALO = 16
ROUNDS = 4
D = 512
EPS = 1e-05
CHUNK = 128
BF = jnp.bfloat16
F32 = jnp.float32
VMEM_LIMIT = 60 * 1024 * 1024

ROWS = {"ein": 3 * D, "eout": D, "nin": 2 * D, "nout": D}
GROUPS = {"node": ("nin", "nout"), "edge": ("ein", "eout")}
SEQUENCE = {"node": (0, 1, 2, 3), "edge": (1, 0, 2, 3)}


def mm(a, b):
    return lax.dot_general(a, b, (((1,), (0,)), ((), ())), preferred_element_type=F32)


def mm_t(a, b):
    return lax.dot_general(a, b, (((1,), (1,)), ((), ())), preferred_element_type=F32)


def t_mm(a, b):
    return lax.dot_general(a, b, (((0,), (0,)), ((), ())), preferred_element_type=F32)


def one_hot(rows, index):
    where = lax.broadcasted_iota(jnp.int32, (rows, index.shape[1]), 0) == index
    return jnp.where(where, 1.0, 0.0).astype(BF)


def incidence(dst, count):
    edges = dst.shape[1]
    hit = lax.broadcasted_iota(jnp.int32, (NODE_DEV, edges), 0) == dst
    live = lax.broadcasted_iota(jnp.int32, (NODE_DEV, edges), 1) < count
    return jnp.where(hit & live, 1.0, 0.0).astype(BF)


def normed(values):
    center = values - jnp.mean(values, axis=-1, keepdims=True)
    spread = jnp.mean(center * center, axis=-1, keepdims=True)
    return center, lax.rsqrt(spread + EPS)


def silu_pair(pre):
    gate = lax.logistic(pre)
    return pre * gate, gate * (1.0 + pre * (1.0 - gate))


def norm_back(cot, hat, rate, gain):
    scaled = cot * gain
    first = jnp.mean(scaled, axis=-1, keepdims=True)
    second = jnp.mean(scaled * hat, axis=-1, keepdims=True)
    return rate * (scaled - first - hat * second)


def forward(own, edges, table, src, dst, count, weights, waits, gains, res):
    w_ein, w_eout, w_nin, w_nout = weights
    g_edge, g_node = gains
    rows = edges.shape[0]
    hot_src = one_hot(table.shape[0], src[...])
    hot_dst = one_hot(NODE_DEV, dst[...])
    waits[0]()
    waits[1]()
    for at in range(0, rows, CHUNK):
        part = slice(at, at + CHUNK)
        edge = edges[part]
        sender = t_mm(hot_src[:, part], table[...]).astype(BF)
        receiver = t_mm(hot_dst[:, part], own[...]).astype(BF)
        pre = mm(edge, w_ein[:D]) + mm(sender, w_ein[D : 2 * D]) + mm(receiver, w_ein[2 * D :])
        middle, slope = silu_pair(pre)
        middle = middle.astype(BF)
        center, rate = normed(mm(middle, w_eout[...]))
        live = lax.broadcasted_iota(jnp.int32, (CHUNK, 1), 0) + at < count
        rate = jnp.where(live, rate, 0.0)
        hat = center * rate
        res["edge_new"][part] = (edge.astype(F32) + hat * g_edge).astype(BF)
        res["edge_mid"][part] = middle
        res["edge_slope"][part] = slope.astype(BF)
        res["edge_hat"][part] = hat.astype(BF)
        res["edge_rate"][part] = jnp.broadcast_to(rate, (CHUNK, 128))
    agg = mm(incidence(dst[...], count), res["edge_new"][...]).astype(BF)
    waits[2]()
    waits[3]()
    pre = mm(own[...], w_nin[:D]) + mm(agg, w_nin[D:])
    middle, slope = silu_pair(pre)
    middle = middle.astype(BF)
    center, rate = normed(mm(middle, w_nout[...]))
    hat = center * rate
    res["node_new"][...] = (own[...].astype(F32) + hat * g_node).astype(BF)
    res["agg"][...] = agg
    res["node_mid"][...] = middle
    res["node_slope"][...] = slope.astype(BF)
    res["node_hat"][...] = hat.astype(BF)
    res["node_rate"][...] = jnp.broadcast_to(rate, (NODE_DEV, 128))


def slot_of(shard, me, shards, sequence):
    if shards == 1:
        return 0
    apart = jnp.bitwise_xor(jnp.int32(shard), me)
    slot = jnp.int32(0)
    for bit in sequence:
        slot = slot * 2 + jnp.bitwise_and(lax.shift_right_logical(apart, jnp.int32(bit)), 1)
    return slot


def emit(value, name, first_row, group, store, core, slots):
    shards = store.shape[1]
    half = ROWS[name] // shards // 2
    base = 0
    for other in GROUPS[group]:
        if other == name:
            break
        base += ROWS[other] // shards // 2
    value = value.astype(BF)
    last_row = first_row + value.shape[0]
    for piece in range(2 * shards):
        low, high = max(piece * half, first_row), min((piece + 1) * half, last_row)
        if low < high:
            keep = jnp.bitwise_xor(core, piece % 2)
            to = base + low - piece * half
            store[keep, slots[piece // 2], to : to + high - low, :] = value[
                low - first_row : high - first_row
            ]


def backward(
    cot_node, cot_edge, own, edges, table, src, dst, count, weights, gains, res, core, me, stores,
    outs, work, ready,
):
    w_ein, w_eout, w_nin, w_nout = weights
    g_edge, g_node = gains
    d_own_out, d_edges_out, halo_out, gain_out = outs
    d_outer, d_pre = work
    rows = edges.shape[0]
    shards = stores["node"].shape[1]
    slots = {
        g: [slot_of(i, me, shards, SEQUENCE[g]) for i in range(shards)] for g in GROUPS
    }

    def put(value, name, first_row):
        group = "node" if name in GROUPS["node"] else "edge"
        emit(value, name, first_row, group, stores[group], core, slots[group])

    hat = res["node_hat"][...].astype(F32)
    gain_node = jnp.sum(cot_node * hat, axis=0, keepdims=True)
    d_out = norm_back(cot_node, hat, res["node_rate"][:, :1], g_node).astype(BF)
    put(t_mm(res["node_mid"][...], d_out), "nout", 0)
    d_pre_node = (mm_t(d_out, w_nout[...]) * res["node_slope"][...].astype(F32)).astype(BF)
    put(t_mm(own[...], d_pre_node), "nin", 0)
    put(t_mm(res["agg"][...], d_pre_node), "nin", D)
    ready("node")
    d_own = cot_node + mm_t(d_pre_node, w_nin[:D])
    d_agg = mm_t(d_pre_node, w_nin[D:]).astype(BF)

    joins = incidence(dst[...], count)
    gain_edge = jnp.zeros((1, D), F32)
    for at in range(0, rows, CHUNK):
        part = slice(at, at + CHUNK)
        cot = t_mm(joins[:, part], d_agg)
        if cot_edge is not None:
            cot = cot + cot_edge[part].astype(F32)
        hat = res["edge_hat"][part].astype(F32)
        gain_edge = gain_edge + jnp.sum(cot * hat, axis=0, keepdims=True)
        outer = norm_back(cot, hat, res["edge_rate"][part, :1], g_edge).astype(BF)
        d_outer[part] = outer
        pre = (mm_t(outer, w_eout[...]) * res["edge_slope"][part].astype(F32)).astype(BF)
        d_pre[part] = pre
        d_edges_out[part] = (cot + mm_t(pre, w_ein[:D])).astype(BF)
    put(t_mm(res["edge_mid"][...], d_outer[...]), "eout", 0)
    put(t_mm(edges[...], d_pre[...]), "ein", 0)
    to_src = mm(one_hot(table.shape[0], src[...]), d_pre[...]).astype(BF)
    to_dst = mm(one_hot(NODE_DEV, dst[...]), d_pre[...]).astype(BF)
    put(t_mm(table[...], to_src), "ein", D)
    put(t_mm(own[...], to_dst), "ein", 2 * D)
    ready("edge")
    d_table = mm_t(to_src, w_ein[D : 2 * D])
    d_own = d_own + d_table[:NODE_DEV] + mm_t(to_dst, w_ein[2 * D :])
    d_own_out[...] = d_own
    halo_out[...] = d_table[NODE_DEV:].astype(BF)
    gain_out[...] = jnp.concatenate([gain_edge, gain_node, jnp.zeros((6, D), F32)], axis=0)


SAVED = (
    ("edge_mid", None),
    ("edge_slope", None),
    ("edge_hat", None),
    ("agg", NODE_DEV),
    ("node_mid", NODE_DEV),
    ("node_slope", NODE_DEV),
    ("node_hat", NODE_DEV),
)


def saved_rows(rows):
    return sum(h or rows for _, h in SAVED)


def views(rows, held, rates):
    out, at = {}, 0
    for name, height in SAVED:
        out[name] = held.at[at : at + (height or rows)]
        at += height or rows
    out["edge_rate"] = rates.at[:rows]
    out["node_rate"] = rates.at[rows : rows + NODE_DEV]
    return out


class Copies:
    def __init__(self, sems):
        self.sems, self.used, self.out = sems, 0, []

    def start(self, source, target):
        copy = pltpu.make_async_copy(source, target, self.sems.at[self.used])
        self.used += 1
        copy.start()
        return copy

    def send(self, source, target):
        self.out.append(self.start(source, target))

    def either(self, choice, yes, no, targets):
        sems = [self.sems.at[self.used + i] for i in range(len(targets))]
        self.used += len(targets)

        def start(refs):
            for ref, to, sem in zip(refs, targets, sems):
                pltpu.make_async_copy(ref, to, sem).start()

        pl.when(choice)(lambda: start(yes))
        pl.when(jnp.logical_not(choice))(lambda: start(no))
        return [
            pltpu.make_async_copy(ref, to, sem).wait for ref, to, sem in zip(yes, targets, sems)
        ]

    def finish(self):
        for copy in self.out:
            copy.wait()


def shard_number(shards):
    if shards == 1:
        return jnp.int32(0)
    return lax.axis_index("dom") * lax.axis_size("rep") + lax.axis_index("rep")


def first_rows(refs):
    return [ref.at[0] for ref in refs]


def halo_rows(table):
    return [table.at[NODE_DEV + j * HALO : NODE_DEV + (j + 1) * HALO] for j in range(ROUNDS)]


def send_rows(copies, held, outs):
    for j in range(ROUNDS):
        copies.send(held.at[j * HALO : (j + 1) * HALO], outs[j])


def lists_of(ints):
    rows = ints.shape[1]
    return ints.at[0:1, :rows], ints.at[1:2, :rows], ints[2:3, : ROUNDS * HALO]


def pick_kernel(ints, nodes, *rest):
    sent, (own, rows, sems) = rest[:ROUNDS], rest[ROUNDS:]
    copies = Copies(sems)
    copy = copies.start(nodes.at[lax.axis_index("segment")], own)
    hot = one_hot(NODE_DEV, lists_of(ints)[2])
    copy.wait()
    rows[...] = t_mm(hot, own[...]).astype(BF)
    send_rows(copies, rows, sent)
    copies.finish()


def first_kernel(count, ints, g_mine, g_other, nodes, latents, *rest):
    halo, mine, other, rest = rest[:4], rest[4:8], rest[8:12], rest[12:]
    (node_out, edge_out, saved_out, rate_out), sent, rest = rest[:4], rest[4:8], rest[8:]
    held, rest = rest[:4], rest[4:]
    table, edges, saved, rates, node_new, edge_new, rows, sems = rest
    core = lax.axis_index("segment")
    own = table.at[:NODE_DEV]
    copies = Copies(sems)
    coming = [copies.start(nodes.at[core], own), copies.start(latents.at[core], edges)]
    coming += [copies.start(ref, to) for ref, to in zip(halo, halo_rows(table))]
    waits = copies.either(core == 0, first_rows(mine), first_rows(other), held)
    src, dst, send_idx = lists_of(ints)
    gains = jnp.where(core == 0, g_mine[...], g_other[...])
    res = views(edges.shape[0], saved, rates)
    res.update(node_new=node_new, edge_new=edge_new)
    for copy in coming:
        copy.wait()
    forward(
        own, edges, table, src, dst, count[0], held, waits, (gains[:1], gains[1:2]), res
    )
    rows[...] = t_mm(one_hot(NODE_DEV, send_idx), node_new[...]).astype(BF)
    send_rows(copies, rows, sent)
    for source, target in zip(
        (node_new, edge_new, saved, rates), (node_out, edge_out, saved_out, rate_out)
    ):
        copies.send(source, target)
    copies.finish()


def back_outs(copies, stores, outs, work):
    d_own, d_edges, halo, gain, keeps, sends = outs
    d_own_s, d_edges_s, halo_s, gain_s = work

    def ready(group):
        i = 0 if group == "node" else 1
        copies.send(stores[group].at[1], sends[i])
        copies.send(stores[group].at[0], keeps[i])

    def finish():
        send_rows(copies, halo_s, halo)
        for source, target in ((d_own_s, d_own), (d_edges_s, d_edges), (gain_s, gain)):
            copies.send(source, target)
        copies.finish()

    return ready, finish


def second_kernel(count, ints, g_mine, g_other, nodes, latents, cots, *rest):
    halo, mine, other, rest = rest[:4], rest[4:8], rest[8:12], rest[12:]
    (node_out, edge_out), rest = rest[:2], rest[2:]
    outs, rest = (*rest[:2], rest[2:6], rest[6], rest[7:9], rest[9:11]), rest[11:]
    held, rest = rest[:4], rest[4:]
    table, edges, saved, rates, node_new, edge_new, cot, rest = *rest[:7], rest[7:]
    d_outer, d_pre, store_node, store_edge, *work, sems = rest
    core, me = lax.axis_index("segment"), shard_number(store_node.shape[1])
    own = table.at[:NODE_DEV]
    copies = Copies(sems)
    coming = [copies.start(nodes, own), copies.start(latents, edges)]
    coming += [copies.start(ref, to) for ref, to in zip(halo, halo_rows(table))]
    waits = copies.either(core == 1, first_rows(mine), first_rows(other), held)
    cot_copy = copies.start(cots.at[core], cot)
    src, dst, _ = lists_of(ints)
    gains = jnp.where(core == 1, g_mine[...], g_other[...])
    gains = (gains[:1], gains[1:2])
    res = views(edges.shape[0], saved, rates)
    res.update(node_new=node_new, edge_new=edge_new)
    for copy in coming:
        copy.wait()
    forward(own, edges, table, src, dst, count[0], held, waits, gains, res)
    copies.send(node_new, node_out)
    copies.send(edge_new, edge_out)
    cot_copy.wait()
    stores = {"node": store_node, "edge": store_edge}
    ready, finish = back_outs(copies, stores, outs, work)
    backward(
        cot[...].astype(F32), None, own, edges, table, src, dst, count[0], held, gains, res,
        core, me, stores, work, (d_outer, d_pre), ready,
    )
    finish()


def third_kernel(
    count, ints, g_mine, g_other, nodes, latents, d_own_in, d_edges_in, saved_in, rate_in, *rest
):
    halo, back, mine, other, rest = rest[:4], rest[4:8], rest[8:12], rest[12:16], rest[16:]
    outs, rest = (*rest[:2], rest[2:6], rest[6], rest[7:9], rest[9:11]), rest[11:]
    held, rest = rest[:4], rest[4:]
    table, edges, saved, rates, cot_own, cot_edge, got, rest = *rest[:7], rest[7:]
    d_outer, d_pre, store_node, store_edge, *work, sems = rest
    core, me = lax.axis_index("segment"), shard_number(store_node.shape[1])
    own = table.at[:NODE_DEV]
    copies = Copies(sems)
    coming = [
        copies.start(ref, got.at[j * HALO : (j + 1) * HALO]) for j, ref in enumerate(back)
    ]
    coming += [copies.start(d_own_in, cot_own), copies.start(rate_in, rates)]
    coming += [copies.start(saved_in, saved), copies.start(nodes.at[core], own)]
    coming += [copies.start(ref, to) for ref, to in zip(halo, halo_rows(table))]
    waits = copies.either(core == 0, first_rows(mine), first_rows(other), held)
    coming += [copies.start(d_edges_in, cot_edge), copies.start(latents.at[core], edges)]
    src, dst, send_idx = lists_of(ints)
    gains = jnp.where(core == 0, g_mine[...], g_other[...])
    gains = (gains[:1], gains[1:2])
    res = views(edges.shape[0], saved, rates)
    hot = one_hot(NODE_DEV, send_idx)
    for copy in coming:
        copy.wait()
    cot = (cot_own[...] + mm(hot, got[...])).astype(BF).astype(F32)
    for wait in waits:
        wait()
    stores = {"node": store_node, "edge": store_edge}
    ready, finish = back_outs(copies, stores, outs, work)
    backward(
        cot, cot_edge, own, edges, table, src, dst, count[0], held, gains, res,
        core, me, stores, work, (d_outer, d_pre), ready,
    )
    finish()


def last_kernel(ints, d_own, b0, b1, b2, b3, out):
    back = jnp.concatenate([b0[...], b1[...], b2[...], b3[...]], axis=0)
    out[...] = (d_own[...] + mm(one_hot(NODE_DEV, lists_of(ints)[2]), back)).astype(BF)


def weight_scratch():
    return [pltpu.VMEM((r, D), BF) for r in ROWS.values()]


SMEM = pl.BlockSpec(memory_space=pltpu.SMEM)
VMEM = pl.BlockSpec(memory_space=pltpu.VMEM)
ANY = pl.BlockSpec(memory_space=pl.ANY)


def shape(dims, dtype):
    return jax.ShapeDtypeStruct(tuple(dims), dtype)


def call(kernel, in_specs, outs, out_specs, scratch, flops, traffic):
    return pl.pallas_call(
        kernel,
        in_specs=in_specs,
        out_shape=outs,
        out_specs=out_specs,
        scratch_shapes=scratch,
        compiler_params=pltpu.CompilerParams(vmem_limit_bytes=VMEM_LIMIT),
        cost_estimate=pl.CostEstimate(flops=flops, bytes_accessed=traffic, transcendentals=0),
    )


def swap_pairs(size, distance):
    even, odd = [], []
    for p in range(size - distance):
        pair = [(p, p + distance), (p + distance, p)]
        (even if p % (2 * distance) < distance else odd).extend(pair)
    return even, odd


def exchange(pieces):
    size = lax.axis_size("dom")
    routes = swap_pairs(size, 1) + swap_pairs(size, 2)
    return [lax.ppermute(piece, "dom", route) for piece, route in zip(pieces, routes)]


def other_core(value):
    return lax.ppermute(value, "segment", [(0, 1), (1, 0)])


def across(value, bit):
    if bit == 0:
        return lax.ppermute(value, "rep", [(0, 1), (1, 0)])
    step = 1 << (bit - 1)
    return lax.ppermute(value, "dom", [(p, p ^ step) for p in range(lax.axis_size("dom"))])


def added(pieces):
    total = pieces[0].astype(F32)
    for piece in pieces[1:]:
        total = total + piece.astype(F32)
    return total


def tied(values, others):
    return lax.optimization_barrier((list(values), list(others)))[0]


class Halving:
    def __init__(self, keep, got):
        self.terms = [keep, got]

    def gone(self):
        slots = self.terms[0].shape[0] // 2
        value = added([t[slots:] for t in self.terms]).astype(BF)
        self.terms = [t[:slots] for t in self.terms]
        return value

    def sum(self):
        return added(self.terms)[0]


def body(
    node_latent,
    edge_latent,
    node_cot,
    edge_src,
    edge_dst,
    edge_count,
    send_index,
    w_edge_in,
    w_edge_out,
    w_node_in,
    w_node_out,
    gain_edge,
    gain_node,
):
    micro, _, _ = node_latent.shape
    rows = edge_latent.shape[1]
    assert micro == lax.axis_size("segment") == 2
    doms, reps = lax.axis_size("dom"), lax.axis_size("rep")
    core, part, rep = (lax.axis_index(a) for a in ("segment", "dom", "rep"))
    shards = doms * reps if doms * reps == 16 else 1
    first = core == 0

    odd_one, odd_two = part % 2 == 1, (part // 2) % 2 == 1
    flip = jnp.where(jnp.bitwise_and(edge_src, 2 * HALO) != 0, ~odd_two, ~odd_one)
    src = jnp.where(flip & (edge_src >= NODE_DEV), jnp.bitwise_xor(edge_src, HALO), edge_src)
    lists = send_index[0]
    order = [
        jnp.where(odd_one, lists[1], lists[0]),
        jnp.where(odd_one, lists[0], lists[1]),
        jnp.where(odd_two, lists[3], lists[2]),
        jnp.where(odd_two, lists[2], lists[3]),
    ]
    send_idx = jnp.pad(jnp.concatenate(order), (0, rows - ROUNDS * HALO))
    ints = jnp.stack([src, edge_dst, send_idx])

    dma = pltpu.SemaphoreType.DMA
    halo_shapes = [shape((HALO, D), BF)] * ROUNDS
    node_s, edge_s = pltpu.VMEM((NODE_DEV, D), BF), pltpu.VMEM((rows, D), BF)
    sent_s = pltpu.VMEM((ROUNDS * HALO, D), BF)
    sent = call(
        pick_kernel,
        [VMEM, ANY],
        halo_shapes,
        [ANY] * ROUNDS,
        [node_s, sent_s, dma((8,))],
        10**7,
        10**6,
    )(ints, node_latent)
    halo_zero = exchange(sent)
    mine = (w_edge_in, w_edge_out, w_node_in, w_node_out)
    other = tuple(other_core(w) for w in mine)
    g_mine = jnp.concatenate([gain_edge, gain_node], axis=0)
    small = (edge_count, ints, g_mine, other_core(g_mine))
    small_specs = [SMEM, VMEM, VMEM, VMEM]

    table_s = pltpu.VMEM((NODE_DEV + ROUNDS * HALO, D), BF)
    saved_dims, rate_dims = (saved_rows(rows), D), (rows + NODE_DEV, 128)
    layer_s = [
        *weight_scratch(),
        table_s,
        edge_s,
        pltpu.VMEM(saved_dims, BF),
        pltpu.VMEM(rate_dims, F32),
    ]
    node_one, edge_one, saved, rates, *sent = call(
        first_kernel,
        small_specs + [ANY] * (2 + 4 + 8),
        [
            shape((NODE_DEV, D), BF),
            shape((rows, D), BF),
            shape(saved_dims, BF),
            shape(rate_dims, F32),
            *halo_shapes,
        ],
        [ANY] * 8,
        [*layer_s, node_s, edge_s, sent_s, dma((20,))],
        11 * 10**8,
        8 * 10**6,
    )(*small, node_latent, edge_latent, *halo_zero, *mine, *other)
    halo_one = exchange(sent)

    sizes = [sum(ROWS[n] for n in names) // shards // 2 for names in GROUPS.values()]
    share = [shape((shards, size, D), BF) for size in sizes]
    back_shapes = [
        shape((NODE_DEV, D), F32),
        shape((rows, D), BF),
        *halo_shapes,
        shape((8, D), F32),
        *share,
        *share,
    ]
    back_s = [
        edge_s,
        edge_s,
        *[pltpu.VMEM((2, shards, size, D), BF) for size in sizes],
        pltpu.VMEM((NODE_DEV, D), F32),
        edge_s,
        sent_s,
        pltpu.VMEM((8, D), F32),
        dma((40,)),
    ]
    done = call(
        second_kernel,
        small_specs + [ANY] * (3 + 4 + 8),
        [shape((NODE_DEV, D), BF), shape((rows, D), BF)] + back_shapes,
        [ANY] * (2 + len(back_shapes)),
        [*layer_s, node_s, edge_s, node_s, *back_s],
        28 * 10**8,
        14 * 10**6,
    )(*small, node_one, edge_one, node_cot, *halo_one, *mine, *other)
    node_two, edge_two, d_own, d_edges = done[:4]
    gain_one, keep_one, send_one = done[8], done[9:11], done[11:13]
    back = exchange(done[4:8])
    got_one = [other_core(v) for v in send_one]
    if shards > 1:
        one = [Halving(k, g) for k, g in zip(keep_one, got_one)]
        gone = [h.gone() for h in one]
        back = tied(back, gone)
        one[0].terms.append(across(gone[0], 0))
        one[1].terms.append(across(gone[1], 1))

    done = call(
        third_kernel,
        small_specs + [ANY] * (6 + 8 + 8),
        back_shapes,
        [ANY] * len(back_shapes),
        [*layer_s, pltpu.VMEM((NODE_DEV, D), F32), edge_s, sent_s, *back_s],
        18 * 10**8,
        14 * 10**6,
    )(
        *small, node_latent, edge_latent, d_own, d_edges, saved, rates, *halo_zero, *back,
        *mine, *other,
    )
    d_own, d_edges = done[:2]
    gain_zero, keep_zero, send_zero = done[6], done[7:9], done[9:11]
    got_zero = [other_core(v) for v in send_zero]
    back = exchange(done[2:6])
    sums = jnp.where(first, gain_zero, gain_one)[:2]
    sums = sums + other_core(jnp.where(first, gain_one, gain_zero)[:2])

    if shards > 1:
        zero = [Halving(k, g) for k, g in zip(keep_zero, got_zero)]

        def step(bits, halves, after):
            gone = [h.gone() for h in halves]
            if after:
                gone = tied(gone, after)
            got = [across(v, bit) for v, bit in zip(gone, bits)]
            for h, v in zip(halves, got):
                h.terms.append(v)
            return got

        def joint(bit, halves, after):
            gone = [h.gone() for h in halves]
            if after:
                gone = tied(gone, after)
            got = across(jnp.concatenate(gone, axis=1), bit)
            at = 0
            for h, v in zip(halves, gone):
                h.terms.append(got[:, at : at + v.shape[1]])
                at += v.shape[1]
            return [got]

        last_one = [h.terms[-1] for h in one]
        zero_first = step((0, 1), zero, last_one)
        last_one = step((1, 0), one, None)
        zero_second = step((1, 0), zero, last_one)
        last_one = joint(2, one, None)
        joint(2, zero, last_one)
        last_one = joint(3, one, None)
        joint(3, zero, last_one)
        one, zero = ([h.sum() for h in v] for v in (one, zero))
        for bit in range(4):
            sums = sums + across(sums, bit)
    else:
        one = [added([k, g])[0] for k, g in zip(keep_one, got_one)]
        zero = [added([k, other_core(s)])[0] for k, s in zip(keep_zero, send_zero)]
        sums = lax.psum(sums, ("dom", "rep"))

    d_nodes = call(
        last_kernel,
        [VMEM] * 6,
        shape((NODE_DEV, D), BF),
        VMEM,
        [],
        10**7,
        10**6,
    )(ints, d_own, *back)

    def paired(gradient, latent):
        got = other_core(jnp.where(first, latent, gradient))
        low = jnp.where(first, gradient, got)
        high = jnp.where(first, got, latent)
        return jnp.stack([low, high])[None]

    factor = float(micro * reps * NODE_DEV * doms) ** (-0.5)
    one, zero = (jnp.concatenate(v, axis=0) for v in (one, zero))
    got = other_core(jnp.where(first, one, zero))
    kept = jnp.where(first, zero, one)
    low, high = jnp.where(first, kept, got), jnp.where(first, got, kept)
    grads, at = {}, 0
    for names in GROUPS.values():
        for name in names:
            to = at + ROWS[name] // shards // 2
            grads[name] = jnp.concatenate([low[at:to], high[at:to]], axis=0)
            at = to
    if shards == 1:
        grads = {
            k: lax.psum_scatter(v, ("dom", "rep"), scatter_dimension=0, tiled=True)
            for k, v in grads.items()
        }
    width = D // (doms * reps)
    sums = lax.dynamic_slice_in_dim(sums, (part * reps + rep) * width, width, axis=1) * factor
    return (
        paired(d_nodes, node_two),
        paired(d_edges, edge_two),
        (grads["ein"] * factor)[None],
        (grads["eout"] * factor)[None],
        (grads["nin"] * factor)[None],
        (grads["nout"] * factor)[None],
        sums[:1],
        sums[1:],
    )


def solution(mesh):
    placed = (
        P("rep", "dom", None),
        P("rep", "dom", None),
        P("rep", "dom", None),
        P("dom"),
        P("dom"),
        P("dom"),
        P("dom", None, None),
        P("segment", None, None),
        P("segment", None, None),
        P("segment", None, None),
        P("segment", None, None),
        P("segment", None),
        P("segment", None),
    )
    return jax.shard_map(
        body,
        mesh=mesh,
        in_specs=placed,
        out_specs=(
            P("segment", "rep", "dom", None),
            P("segment", "rep", "dom", None),
            P("segment", ("dom", "rep"), None),
            P("segment", ("dom", "rep"), None),
            P("segment", ("dom", "rep"), None),
            P("segment", ("dom", "rep"), None),
            P("segment", ("dom", "rep")),
            P("segment", ("dom", "rep")),
        ),
        check_vma=False,
    )
```

time: 624 us -> 172 us (0.28); the launches traced: 614 us -> 171 us
  waiting for transfers between devices: 268 us -> 40.6 us
  matrix products: 68.6 us -> 0 us
  other arithmetic: 89 us -> 25.4 us
  local copies, waits for them, and re-layouts: 53.4 us -> 4.69 us
  blocking collectives: 38.8 us -> 0 us
  Pallas kernels: 0 us -> 33.7 us
  between operations: 18 us -> 1.95 us
  starting transfers between devices: 78 us -> 64.4 us
    reduce_scatter x4 -> x0, waiting for transfers between devices: 250 us -> none  [body(): lax.psum_scatter(tuple(total), ('dom', 'rep'), scatter_dimension=0, tiled...]
    dot_general x63 -> x0, matrix products: 68.6 us -> none  [the longest x12 20.9 us: layer(): jnp.dot(middle, w_eout.astype(jnp.bfloat16), preferred_element_type=jnp.f...]
    unnamed x1 -> x0, blocking collectives: 38.8 us -> none
    gather x24 -> x0, local copies, waits for them, and re-layouts: 35.9 us -> none  [the longest x6 14.9 us: layer(): receiver = jnp.take(table, dst, axis=0)]
    pallas_call x0 -> x5, Pallas kernels: none -> 33.7 us  [the longest x1 11.9 us: body(): call(second_kernel, small_specs + [ANY] * (3 + 4 + 8), [shape((NODE_DEV,...]
    scatter-add x6 -> x0, other arithmetic: 23.2 us -> none  [the longest x3 11.8 us: layer(): sender = jnp.take(table, src, axis=0)]
    ppermute x32 -> x45, waiting for transfers between devices: 18.1 us -> 40.6 us  [the longest x11 21.6 us: across(): lax.ppermute(value, 'dom', [(p, p ^ step) for p in range(lax.axis_size('d...]
    ppermute x32 -> x45, starting transfers between devices: 77.6 us -> 64.4 us  [the longest x16 38 us: exchange(): lax.ppermute(piece, 'dom', route)]
  transfers between devices with their start and end apart: 36 -> 45, of which waited for: 9 -> 18; matrix products, arithmetic and copies ran while one was open for 24% -> 13% of each run, Pallas kernels for 0% -> 2%
where the time goes in v1:
time: 172 us; the launch traced here: 171 us
  starting transfers between devices  64.4 us (37%)
  waiting for transfers between devices  40.6 us (24%)
  Pallas kernels  33.7 us (20%)
  other arithmetic  25.4 us (15%)
  local copies, waits for them, and re-layouts  4.69 us (3%)
  between operations  1.95 us (1%)
    ppermute x16, starting transfers between devices, exchange(): lax.ppermute(piece, 'dom', route)  38 us
    ppermute x11, waiting for transfers between devices, across(): lax.ppermute(value, 'dom', [(p, p ^ step) for p in range(lax.axis_size('d...  21.6 us
    ppermute x11, starting transfers between devices, across(): lax.ppermute(value, 'dom', [(p, p ^ step) for p in range(lax.axis_size('d...  17.8 us
    pallas_call x1, Pallas kernels, body(): call(second_kernel, small_specs + [ANY] * (3 + 4 + 8), [shape((NODE_DEV,...  11.9 us
    ppermute x5, waiting for transfers between devices, across(): return lax.ppermute(value, 'rep', [(0, 1), (1, 0)])  11.7 us
    convert_element_type x16, other arithmetic, gone(): value = added([t[slots:] for t in self.terms]).astype(BF)  11.5 us
    pallas_call x1, Pallas kernels, body(): call(third_kernel, small_specs + [ANY] * (6 + 8 + 8), back_shapes, [ANY]...  10.4 us
    pallas_call x1, Pallas kernels, body(): call(first_kernel, small_specs + [ANY] * (2 + 4 + 8), [shape((NODE_DEV, D...  7.21 us
  transfers between devices with their start and end apart: 45, of which 18 were waited for; matrix products, arithmetic and copies ran while one was open for 13% of the time, Pallas kernels for 2%

profile of v1, /device:TPU:0, one launch (start us, length us, event | category | flops | bytes accessed | tf_op | source)
XLA Modules:
  0.0 170.9 jit_solution(8710365932215054283)
XLA Ops:
  5.8 2.5 %shard_map.188 = (bf16[16,512]{1,0:T(8,128)(2,1)}, bf16[16,512]{1,0:T(8,128)(2,1)}, bf16[16,512]{1,0:T(8,128)(2,1)}, bf16[16,512]{1,0:T(8,128)(2,1)}) custom-call(s32[3,384]{1,0:T(4,128)} %pad_add_fusion.ints, bf16[2,128,512]{2,1,0:T(8,128)(2,1)} %nodes.5), custom_call_target="tpu_custom_call" | custom-call | flops 10000000 | bytes 1000000 | tf_op jit(solution)/shard_map/pallas_call | solution.py:526
  8.4 2.7 %collective-permute-start.1 = (bf16[16,512]{1,0:T(8,128)(2,1)}, bf16[16,512]{1,0:T(8,128)(2,1)S(1)}, u32[]{:S(2)}, u32[]{:S(2)}) collective-permute-start(bf16[16,512]{1,0:T(8,128)(2,1)} %get-tuple-element.56), channel_id=1, source_target_pairs={{0,2},{2,0},{4,6},{6,4},{8,10},{10,8},{12,14},{14,12},{1,3},{3,1},... | collective-permute-start | bytes 49160 | tf_op jit(solution)/shard_map/ppermute | solution.py:447
  11.0 1.9 %collective-permute-done.1.rest_0_ = bf16[16,512]{1,0:T(8,128)(2,1)S(1)} collective-permute-done((bf16[16,512]{1,0:T(8,128)(2,1)}, bf16[16,512]{1,0:T(8,128)(2,1)S(1)}, u32[]{:S(2)}, u32[]{:S(2)}) %collective-permute-start.1) | collective-permute-done | bytes 16416 | tf_op jit(solution)/shard_map/ppermute | solution.py:447
  13.6 8.1 %collective-permute-start.3 = (bf16[16,512]{1,0:T(8,128)(2,1)}, bf16[16,512]{1,0:T(8,128)(2,1)S(1)}, u32[]{:S(2)}, u32[]{:S(2)}) collective-permute-start(bf16[16,512]{1,0:T(8,128)(2,1)} %get-tuple-element.58), channel_id=1, source_target_pairs={{0,4},{4,0},{2,6},{6,2},{8,12},{12,8},{10,14},{14,10},{1,5},{5,1},... | collective-permute-start | bytes 49160 | tf_op jit(solution)/shard_map/ppermute | solution.py:447
  21.8 1.9 %collective-permute-done.3.rest_2_ = bf16[16,512]{1,0:T(8,128)(2,1)S(1)} collective-permute-done((bf16[16,512]{1,0:T(8,128)(2,1)}, bf16[16,512]{1,0:T(8,128)(2,1)S(1)}, u32[]{:S(2)}, u32[]{:S(2)}) %collective-permute-start.3) | collective-permute-done | bytes 16416 | tf_op jit(solution)/shard_map/ppermute | solution.py:447
  26.2 1.1 copy-done
  27.3 7.2 %shard_map.189 = (bf16[128,512]{1,0:T(8,128)(2,1)}, bf16[384,512]{1,0:T(8,128)(2,1)}, bf16[1664,512]{1,0:T(8,128)(2,1)}, f32[512,128]{1,0:T(8,128)}, bf16[16,512...) custom-call(s32[1]{0:T(128)S(6)} %copy.21.count, ...), custom_call_target="tpu_custom_call" | custom-call | flops 1100000000 | bytes 8000000 | tf_op jit(solution)/shard_map/pallas_call | solution.py:551
  35.2 7.9 %collective-permute-start.11 = (bf16[16,512]{1,0:T(8,128)(2,1)}, bf16[16,512]{1,0:T(8,128)(2,1)S(1)}, u32[]{:S(2)}, u32[]{:S(2)}) collective-permute-start(bf16[16,512]{1,0:T(8,128)(2,1)} %get-tuple-element.64), channel_id=1, source_target_pairs={{0,4},{4,0},{2,6},{6,2},{8,12},{12,8},{10,14},{14,10},{1,5},{5,1},... | collective-permute-start | bytes 49160 | tf_op jit(solution)/shard_map/ppermute | solution.py:447
  43.7 3.1 %collective-permute-start.9 = (bf16[16,512]{1,0:T(8,128)(2,1)}, bf16[16,512]{1,0:T(8,128)(2,1)S(1)}, u32[]{:S(2)}, u32[]{:S(2)}) collective-permute-start(bf16[16,512]{1,0:T(8,128)(2,1)} %get-tuple-element.62), channel_id=1, source_target_pairs={{0,2},{2,0},{4,6},{6,4},{8,10},{10,8},{12,14},{14,12},{1,3},{3,1},... | collective-permute-start | bytes 49160 | tf_op jit(solution)/shard_map/ppermute | solution.py:447
  46.8 1.9 %collective-permute-done.9.rest_0_ = bf16[16,512]{1,0:T(8,128)(2,1)S(1)} collective-permute-done((bf16[16,512]{1,0:T(8,128)(2,1)}, bf16[16,512]{1,0:T(8,128)(2,1)S(1)}, u32[]{:S(2)}, u32[]{:S(2)}) %collective-permute-start.9) | collective-permute-done | bytes 16416 | tf_op jit(solution)/shard_map/ppermute | solution.py:447
  49.3 11.9 %shard_map.190 = (bf16[128,512]{1,0:T(8,128)(2,1)}, bf16[384,512]{1,0:T(8,128)(2,1)}, f32[128,512]{1,0:T(8,128)}, bf16[384,512]{1,0:T(8,128)(2,1)}, bf16[16,512]...) custom-call(s32[1]{0:T(128)S(6)} %copy.21.count, ...), custom_call_target="tpu_custom_call" | custom-call | flops 2800000000 | bytes 14000000 | tf_op jit(solution)/shard_map/pallas_call | solution.py:588
  61.8 2.0 %collective-permute-start.13 = (bf16[16,512]{1,0:T(8,128)(2,1)}, bf16[16,512]{1,0:T(8,128)(2,1)S(1)}, u32[]{:S(2)}, u32[]{:S(2)}) collective-permute-start(bf16[16,512]{1,0:T(8,128)(2,1)} %get-tuple-element.70), channel_id=1, source_target_pairs={{0,2},{2,0},{4,6},{6,4},{8,10},{10,8},{12,14},{14,12},{1,3},{3,1},... | collective-permute-start | bytes 49160 | tf_op jit(solution)/shard_map/ppermute | solution.py:447
  64.5 4.1 %collective-permute-start.15 = (bf16[16,512]{1,0:T(8,128)(2,1)}, bf16[16,512]{1,0:T(8,128)(2,1)S(1)}, u32[]{:S(2)}, u32[]{:S(2)}) collective-permute-start(bf16[16,512]{1,0:T(8,128)(2,1)} %get-tuple-element.72), channel_id=1, source_target_pairs={{0,4},{4,0},{2,6},{6,2},{8,12},{12,8},{10,14},{14,10},{1,5},{5,1},... | collective-permute-start | bytes 49160 | tf_op jit(solution)/shard_map/ppermute | solution.py:447
  69.4 1.9 %add_convert_fusion.3 = bf16[8,48,512]{2,1,0:T(8,128)(2,1)} fusion(bf16[16,48,512]{2,1,0:T(8,128)(2,1)S(1)} %collective-permute-done.17, bf16[16,48,512]{2,1,0:T(8,128)(2,1)} %get-tuple-element.74), kind=kLoop, calls=%fused_computation.4 | loop fusion | flops 786432 | bytes 1179648 | tf_op jit(solution)/shard_map/convert_element_type | solution.py:478
  71.3 2.0 %add_convert_fusion.1 = bf16[8,64,512]{2,1,0:T(8,128)(2,1)} fusion(bf16[16,64,512]{2,1,0:T(8,128)(2,1)S(1)} %collective-permute-done.18, bf16[16,64,512]{2,1,0:T(8,128)(2,1)} %get-tuple-element.76), kind=kLoop, calls=%fused_computation.1 | loop fusion | flops 1048576 | bytes 1572864 | tf_op jit(solution)/shard_map/convert_element_type | solution.py:478
  73.9 10.4 %shard_map.191 = (f32[128,512]{1,0:T(8,128)}, bf16[384,512]{1,0:T(8,128)(2,1)}, bf16[16,512]{1,0:T(8,128)(2,1)}, bf16[16,512]{1,0:T(8,128)(2,1)}, bf16[16,512]{1...) custom-call(s32[1]{0:T(128)S(6)} %copy.21.count, ...), custom_call_target="tpu_custom_call" | custom-call | flops 1800000000 | bytes 14000000 | tf_op jit(solution)/shard_map/pallas_call | solution.py:608
  85.2 1.2 collective-permute-done.40
  87.0 1.5 collective-permute-start.41
  88.5 2.1 %collective-permute-done.41 = f32[2,512]{1,0:T(2,128)S(1)} collective-permute-done((f32[2,512]{1,0:T(2,128)S(1)}, f32[2,512]{1,0:T(2,128)S(1)}, u32[]{:S(2)}, u32[]{:S(2)}) %collective-permute-start.41) | collective-permute-done | bytes 4128 | tf_op jit(solution)/shard_map/ppermute | solution.py:456
  90.7 2.4 %collective-permute-start.42 = (f32[2,512]{1,0:T(2,128)S(1)}, f32[2,512]{1,0:T(2,128)S(1)}, u32[]{:S(2)}, u32[]{:S(2)}) collective-permute-start(f32[2,512]{1,0:T(2,128)S(1)} %add.274), channel_id=1, source_target_pairs={{0,2},{2,0},{4,6},{6,4},{8,10},{10,8},{12,14},{14,12},{1,3},{3,1},... | collective-permute-start | bytes 12296 | tf_op jit(solution)/shard_map/ppermute | solution.py:458
  93.1 1.6 collective-permute-done.42
  94.6 4.4 %collective-permute-start.43 = (f32[2,512]{1,0:T(2,128)S(1)}, f32[2,512]{1,0:T(2,128)S(1)}, u32[]{:S(2)}, u32[]{:S(2)}) collective-permute-start(f32[2,512]{1,0:T(2,128)S(1)} %add.275), channel_id=1, source_target_pairs={{0,4},{2,6},{4,0},{6,2},{8,12},{10,14},{12,8},{14,10},{1,5},{3,7},... | collective-permute-start | bytes 12296 | tf_op jit(solution)/shard_map/ppermute | solution.py:458
  99.0 1.5 collective-permute-start.27
  101.2 4.8 %collective-permute-start.21 = (bf16[16,512]{1,0:T(8,128)(2,1)}, bf16[16,512]{1,0:T(8,128)(2,1)S(1)}, u32[]{:S(2)}, u32[]{:S(2)}) collective-permute-start(bf16[16,512]{1,0:T(8,128)(2,1)} %get-tuple-element.85), channel_id=1, source_target_pairs={{0,4},{4,0},{2,6},{6,2},{8,12},{12,8},{10,14},{14,10},{1,5},{5,1},... | collective-permute-start | bytes 49160 | tf_op jit(solution)/shard_map/ppermute | solution.py:447
  108.7 3.3 %collective-permute-start.44 = (f32[2,512]{1,0:T(2,128)}, f32[2,512]{1,0:T(2,128)}, u32[]{:S(2)}, u32[]{:S(2)}) collective-permute-start(f32[2,512]{1,0:T(2,128)} %add.276), channel_id=1, source_target_pairs={{0,8},{2,10},{4,12},{6,14},{8,0},{10,2},{12,4},{14,6},{1,9},{3,11}... | collective-permute-start | bytes 12296 | tf_op jit(solution)/shard_map/ppermute | solution.py:458
  112.0 1.8 %shard_map.192 = bf16[128,512]{1,0:T(8,128)(2,1)} custom-call(s32[3,384]{1,0:T(4,128)} %pad_add_fusion.ints, f32[128,512]{1,0:T(8,128)} %get-tuple-element.82.d_own, bf16[16,512]{1,0:T(8,128)(2,1)} %copy-done.21, bf16[16,512]{1,0:T(8,128)(2,1)} %copy-done.22, bf16[16,512]{1,0:T(8,128)(2,1)} %copy-done.23, bf16[16,512]{1,0:T(8,128)(2,1)} %copy-done.24), custom_call_target="tpu_custom_call" | custom-call | flops 10000000 | bytes 1000000 | tf_op jit(solution)/shard_map/pallas_call | solution.py:666
  115.6 1.3 add_convert_fusion.6
  116.8 1.5 collective-permute-start.31
  118.3 1.3 collective-permute-done.28
  120.8 3.4 %collective-permute-done.31 = bf16[4,48,512]{2,1,0:T(8,128)(2,1)S(1)} collective-permute-done((bf16[4,48,512]{2,1,0:T(8,128)(2,1)S(1)}, bf16[4,48,512]{2,1,0:T(8,128)(2,1)S(1)}, u32[]{:S(2)}, u32[]{:S(2)}) %collective-permute-start.31) | collective-permute-done | bytes 196640 | tf_op jit(solution)/shard_map/ppermute | solution.py:458
  124.2 1.0 add_convert_fusion.10
  125.2 1.7 collective-permute-done.32
  127.0 1.3 collective-permute-start.35
  128.4 1.1 add_convert_fusion.2
  130.3 1.5 collective-permute-start.30
  132.5 1.2 collective-permute-done.35
  133.7 6.3 %collective-permute-done.29 = bf16[8,48,512]{2,1,0:T(8,128)(2,1)S(1)} collective-permute-done((bf16[8,48,512]{2,1,0:T(8,128)(2,1)S(1)}, bf16[8,48,512]{2,1,0:T(8,128)(2,1)S(1)}, u32[]{:S(2)}, u32[]{:S(2)}) %collective-permute-start.29) | collective-permute-done | bytes 393248 | tf_op jit(solution)/shard_map/ppermute | solution.py:456
  140.0 1.0 add_convert_fusion.7
  141.0 2.2 %collective-permute-done.30 = bf16[8,64,512]{2,1,0:T(8,128)(2,1)S(1)} collective-permute-done((bf16[8,64,512]{2,1,0:T(8,128)(2,1)S(1)}, bf16[8,64,512]{2,1,0:T(8,128)(2,1)S(1)}, u32[]{:S(2)}, u32[]{:S(2)}) %collective-permute-start.30) | collective-permute-done | bytes 524320 | tf_op jit(solution)/shard_map/ppermute | solution.py:458
  143.2 1.0 collective-permute-start.33
  145.1 1.6 collective-permute-start.34
  147.6 1.4 collective-permute-done.33
  149.0 0.9 add_convert_fusion.11
  149.9 1.6 collective-permute-done.34
  152.3 1.4 collective-permute-done.37
  153.8 4.0 %collective-permute-done.36 = bf16[2,112,512]{2,1,0:T(8,128)(2,1)S(1)} collective-permute-done((bf16[2,112,512]{2,1,0:T(8,128)(2,1)S(1)}, bf16[2,112,512]{2,1,0:T(8,128)(2,1)S(1)}, u32[]{:S(2)}, u32[]{:S(2)}) %collective-permute-start.36) | collective-permute-done | bytes 229408 | tf_op jit(solution)/shard_map/ppermute | solution.py:458
  160.5 5.2 %collective-permute-done.38 = bf16[1,112,512]{2,1,0:T(8,128)(2,1)S(1)} collective-permute-done((bf16[1,112,512]{2,1,0:T(8,128)(2,1)S(1)}, bf16[1,112,512]{2,1,0:T(8,128)(2,1)S(1)}, u32[]{:S(2)}, u32[]{:S(2)}) %collective-permute-start.38) | collective-permute-done | bytes 114720 | tf_op jit(solution)/shard_map/ppermute | solution.py:458
  166.7 0.9 maximum_bitcast_fusion
  (162 shorter events, 31.2 us)
Async XLA Ops:
  0.6 24.4 %collective-permute-start.5 = (bf16[1,1536,512]{2,1,0:T(8,128)(2,1)}, bf16[1,1536,512]{2,1,0:T(8,128)(2,1)S(1)}, u32[]{:S(2)}, u32[]{:S(2)}) collective-permute-start(bf16[1,1536,512]{2,1,0:T(8,128)(2,1)} %rest_8_.1), channel_id=1, source_target_pairs={{0,16},{16,0},{1,17},{17,1},{2,18},{18,2},{3,19},{19,3},{4,20},{20... | collective-permute-start | bytes 4718600 | tf_op jit(solution)/shard_map/ppermute | solution.py:451
  1.2 23.9 %collective-permute-start.7 = (bf16[1,1024,512]{2,1,0:T(8,128)(2,1)}, bf16[1,1024,512]{2,1,0:T(8,128)(2,1)S(1)}, u32[]{:S(2)}, u32[]{:S(2)}) collective-permute-start(bf16[1,1024,512]{2,1,0:T(8,128)(2,1)} %rest_10_.1), channel_id=1, source_target_pairs={{0,16},{16,0},{1,17},{17,1},{2,18},{18,2},{3,19},{19,3},{4,20},{20... | collective-permute-start | bytes 3145736 | tf_op jit(solution)/shard_map/ppermute | solution.py:451
  1.9 23.1 %copy-start.15 = (f32[2,512]{1,0:T(2,128)}, f32[2,512]{1,0:T(2,128)S(1)}, u32[]{:S(2)}) copy-start(f32[2,512]{1,0:T(2,128)S(1)} %pad_maximum_fusion.6.g_mine) | copy-start | bytes 12292
  1.9 6.4 %collective-permute-start = (f32[2,512]{1,0:T(2,128)S(1)}, f32[2,512]{1,0:T(2,128)S(1)}, u32[]{:S(2)}, u32[]{:S(2)}) collective-permute-start(f32[2,512]{1,0:T(2,128)S(1)} %pad_maximum_fusion.6.g_mine), channel_id=1, source_target_pairs={{0,16},{16,0},{1,17},{17,1},{2,18},{18,2},{3,19},{19,3},{4,20},{20... | collective-permute-start | bytes 12296 | tf_op jit(solution)/shard_map/ppermute | solution.py:451
  2.4 22.6 %collective-permute-start.6 = (bf16[1,512,512]{2,1,0:T(8,128)(2,1)}, bf16[1,512,512]{2,1,0:T(8,128)(2,1)S(1)}, u32[]{:S(2)}, u32[]{:S(2)}) collective-permute-start(bf16[1,512,512]{2,1,0:T(8,128)(2,1)} %rest_9_.1), channel_id=1, source_target_pairs={{0,16},{16,0},{1,17},{17,1},{2,18},{18,2},{3,19},{19,3},{4,20},{20... | collective-permute-start | bytes 1572872 | tf_op jit(solution)/shard_map/ppermute | solution.py:451
  2.5 22.5 %collective-permute-start.8 = (bf16[1,512,512]{2,1,0:T(8,128)(2,1)}, bf16[1,512,512]{2,1,0:T(8,128)(2,1)}, u32[]{:S(2)}, u32[]{:S(2)}) collective-permute-start(bf16[1,512,512]{2,1,0:T(8,128)(2,1)} %rest_11_.1), channel_id=1, source_target_pairs={{0,16},{16,0},{1,17},{17,1},{2,18},{18,2},{3,19},{19,3},{4,20},{20... | collective-permute-start | bytes 1572872 | tf_op jit(solution)/shard_map/ppermute | solution.py:451
  8.4 4.6 %collective-permute-start.1 = (bf16[16,512]{1,0:T(8,128)(2,1)}, bf16[16,512]{1,0:T(8,128)(2,1)S(1)}, u32[]{:S(2)}, u32[]{:S(2)}) collective-permute-start(bf16[16,512]{1,0:T(8,128)(2,1)} %get-tuple-element.56), channel_id=1, source_target_pairs={{0,2},{2,0},{4,6},{6,4},{8,10},{10,8},{12,14},{14,12},{1,3},{3,1},... | collective-permute-start | bytes 49160 | tf_op jit(solution)/shard_map/ppermute | solution.py:447
  12.9 0.7 collective-permute-start.2
  13.6 10.0 %collective-permute-start.3 = (bf16[16,512]{1,0:T(8,128)(2,1)}, bf16[16,512]{1,0:T(8,128)(2,1)S(1)}, u32[]{:S(2)}, u32[]{:S(2)}) collective-permute-start(bf16[16,512]{1,0:T(8,128)(2,1)} %get-tuple-element.58), channel_id=1, source_target_pairs={{0,4},{4,0},{2,6},{6,2},{8,12},{12,8},{10,14},{14,10},{1,5},{5,1},... | collective-permute-start | bytes 49160 | tf_op jit(solution)/shard_map/ppermute | solution.py:447
  23.7 1.3 collective-permute-start.4
  34.5 12.3 %collective-permute-start.10 = (bf16[16,512]{1,0:T(8,128)(2,1)}, bf16[16,512]{1,0:T(8,128)(2,1)S(1)}, u32[]{:S(2)}, u32[]{:S(2)}) collective-permute-start(bf16[16,512]{1,0:T(8,128)(2,1)} %get-tuple-element.63), channel_id=1, source_target_pairs={{2,4},{4,2},{6,8},{8,6},{10,12},{12,10},{3,5},{5,3},{7,9},{9,7},{1... | collective-permute-start | bytes 49160 | tf_op jit(solution)/shard_map/ppermute | solution.py:447
  35.2 11.6 %collective-permute-start.11 = (bf16[16,512]{1,0:T(8,128)(2,1)}, bf16[16,512]{1,0:T(8,128)(2,1)S(1)}, u32[]{:S(2)}, u32[]{:S(2)}) collective-permute-start(bf16[16,512]{1,0:T(8,128)(2,1)} %get-tuple-element.64), channel_id=1, source_target_pairs={{0,4},{4,0},{2,6},{6,2},{8,12},{12,8},{10,14},{14,10},{1,5},{5,1},... | collective-permute-start | bytes 49160 | tf_op jit(solution)/shard_map/ppermute | solution.py:447
  43.0 3.8 %collective-permute-start.12 = (bf16[16,512]{1,0:T(8,128)(2,1)}, bf16[16,512]{1,0:T(8,128)(2,1)S(1)}, u32[]{:S(2)}, u32[]{:S(2)}) collective-permute-start(bf16[16,512]{1,0:T(8,128)(2,1)} %get-tuple-element.65), channel_id=1, source_target_pairs={{4,8},{8,4},{6,10},{10,6},{5,9},{9,5},{7,11},{11,7},{20,24},{24,20... | collective-permute-start | bytes 49160 | tf_op jit(solution)/shard_map/ppermute | solution.py:447
  43.7 5.0 %collective-permute-start.9 = (bf16[16,512]{1,0:T(8,128)(2,1)}, bf16[16,512]{1,0:T(8,128)(2,1)S(1)}, u32[]{:S(2)}, u32[]{:S(2)}) collective-permute-start(bf16[16,512]{1,0:T(8,128)(2,1)} %get-tuple-element.62), channel_id=1, source_target_pairs={{0,2},{2,0},{4,6},{6,4},{8,10},{10,8},{12,14},{14,12},{1,3},{3,1},... | collective-permute-start | bytes 49160 | tf_op jit(solution)/shard_map/ppermute | solution.py:447
  61.2 10.1 %collective-permute-start.18 = (bf16[16,64,512]{2,1,0:T(8,128)(2,1)}, bf16[16,64,512]{2,1,0:T(8,128)(2,1)S(1)}, u32[]{:S(2)}, u32[]{:S(2)}) collective-permute-start(bf16[16,64,512]{2,1,0:T(8,128)(2,1)} %get-tuple-element.77), channel_id=1, source_target_pairs={{0,16},{16,0},{1,17},{17,1},{2,18},{18,2},{3,19},{19,3},{4,20},{20... | collective-permute-start | bytes 3145736 | tf_op jit(solution)/shard_map/ppermute | solution.py:451
  61.3 7.3 %collective-permute-start.17 = (bf16[16,48,512]{2,1,0:T(8,128)(2,1)}, bf16[16,48,512]{2,1,0:T(8,128)(2,1)S(1)}, u32[]{:S(2)}, u32[]{:S(2)}) collective-permute-start(bf16[16,48,512]{2,1,0:T(8,128)(2,1)} %get-tuple-element.75), channel_id=1, source_target_pairs={{0,16},{16,0},{1,17},{17,1},{2,18},{18,2},{3,19},{19,3},{4,20},{20... | collective-permute-start | bytes 2359304 | tf_op jit(solution)/shard_map/ppermute | solution.py:451
  61.8 11.5 %collective-permute-start.13 = (bf16[16,512]{1,0:T(8,128)(2,1)}, bf16[16,512]{1,0:T(8,128)(2,1)S(1)}, u32[]{:S(2)}, u32[]{:S(2)}) collective-permute-start(bf16[16,512]{1,0:T(8,128)(2,1)} %get-tuple-element.70), channel_id=1, source_target_pairs={{0,2},{2,0},{4,6},{6,4},{8,10},{10,8},{12,14},{14,12},{1,3},{3,1},... | collective-permute-start | bytes 49160 | tf_op jit(solution)/shard_map/ppermute | solution.py:447
  63.8 9.5 %collective-permute-start.14 = (bf16[16,512]{1,0:T(8,128)(2,1)}, bf16[16,512]{1,0:T(8,128)(2,1)S(1)}, u32[]{:S(2)}, u32[]{:S(2)}) collective-permute-start(bf16[16,512]{1,0:T(8,128)(2,1)} %get-tuple-element.71), channel_id=1, source_target_pairs={{2,4},{4,2},{6,8},{8,6},{10,12},{12,10},{3,5},{5,3},{7,9},{9,7},{1... | collective-permute-start | bytes 49160 | tf_op jit(solution)/shard_map/ppermute | solution.py:447
  64.5 8.8 %collective-permute-start.15 = (bf16[16,512]{1,0:T(8,128)(2,1)}, bf16[16,512]{1,0:T(8,128)(2,1)S(1)}, u32[]{:S(2)}, u32[]{:S(2)}) collective-permute-start(bf16[16,512]{1,0:T(8,128)(2,1)} %get-tuple-element.72), channel_id=1, source_target_pairs={{0,4},{4,0},{2,6},{6,2},{8,12},{12,8},{10,14},{14,10},{1,5},{5,1},... | collective-permute-start | bytes 49160 | tf_op jit(solution)/shard_map/ppermute | solution.py:447
  68.6 4.8 %collective-permute-start.16 = (bf16[16,512]{1,0:T(8,128)(2,1)}, bf16[16,512]{1,0:T(8,128)(2,1)S(1)}, u32[]{:S(2)}, u32[]{:S(2)}) collective-permute-start(bf16[16,512]{1,0:T(8,128)(2,1)} %get-tuple-element.73), channel_id=1, source_target_pairs={{4,8},{8,4},{6,10},{10,6},{5,9},{9,5},{7,11},{11,7},{20,24},{24,20... | collective-permute-start | bytes 49160 | tf_op jit(solution)/shard_map/ppermute | solution.py:447
  73.9 32.7 %copy-start.3 = (bf16[384,512]{1,0:T(8,128)(2,1)S(1)}, bf16[384,512]{1,0:T(8,128)(2,1)}, u32[]{:S(2)}) copy-start(bf16[384,512]{1,0:T(8,128)(2,1)} %get-tuple-element.89) | copy-start | bytes 1179652
  84.3 35.3 %copy-start.6 = (bf16[16,64,512]{2,1,0:T(8,128)(2,1)S(1)}, bf16[16,64,512]{2,1,0:T(8,128)(2,1)}, u32[]{:S(2)}) copy-start(bf16[16,64,512]{2,1,0:T(8,128)(2,1)} %get-tuple-element.76) | copy-start | bytes 3145732
  85.1 1.2 collective-permute-start.40
  87.0 3.6 %collective-permute-start.41 = (f32[2,512]{1,0:T(2,128)S(1)}, f32[2,512]{1,0:T(2,128)S(1)}, u32[]{:S(2)}, u32[]{:S(2)}) collective-permute-start(f32[2,512]{1,0:T(2,128)S(1)} %select_add_fusion), channel_id=1, source_target_pairs={{0,1},{1,0},{2,3},{3,2},{4,5},{5,4},{6,7},{7,6},{8,9},{9,8},{10,11... | collective-permute-start | bytes 12296 | tf_op jit(solution)/shard_map/ppermute | solution.py:456
  90.7 4.0 %collective-permute-start.42 = (f32[2,512]{1,0:T(2,128)S(1)}, f32[2,512]{1,0:T(2,128)S(1)}, u32[]{:S(2)}, u32[]{:S(2)}) collective-permute-start(f32[2,512]{1,0:T(2,128)S(1)} %add.274), channel_id=1, source_target_pairs={{0,2},{2,0},{4,6},{6,4},{8,10},{10,8},{12,14},{14,12},{1,3},{3,1},... | collective-permute-start | bytes 12296 | tf_op jit(solution)/shard_map/ppermute | solution.py:458
  94.6 11.3 %collective-permute-start.43 = (f32[2,512]{1,0:T(2,128)S(1)}, f32[2,512]{1,0:T(2,128)S(1)}, u32[]{:S(2)}, u32[]{:S(2)}) collective-permute-start(f32[2,512]{1,0:T(2,128)S(1)} %add.275), channel_id=1, source_target_pairs={{0,4},{2,6},{4,0},{6,2},{8,12},{10,14},{12,8},{14,10},{1,5},{3,7},... | collective-permute-start | bytes 12296 | tf_op jit(solution)/shard_map/ppermute | solution.py:458
  99.0 16.5 %collective-permute-start.27 = (bf16[8,48,512]{2,1,0:T(8,128)(2,1)}, bf16[8,48,512]{2,1,0:T(8,128)(2,1)}, u32[]{:S(2)}, u32[]{:S(2)}) collective-permute-start(bf16[8,48,512]{2,1,0:T(8,128)(2,1)} %add_convert_fusion.3), channel_id=1, source_target_pairs={{0,1},{1,0},{2,3},{3,2},{4,5},{5,4},{6,7},{7,6},{8,9},{9,8},{10,11... | collective-permute-start | bytes 1179656 | tf_op jit(solution)/shard_map/ppermute | solution.py:456
  100.5 7.6 %collective-permute-start.19 = (bf16[16,512]{1,0:T(8,128)(2,1)}, bf16[16,512]{1,0:T(8,128)(2,1)S(1)}, u32[]{:S(2)}, u32[]{:S(2)}) collective-permute-start(bf16[16,512]{1,0:T(8,128)(2,1)} %get-tuple-element.83), channel_id=1, source_target_pairs={{0,2},{2,0},{4,6},{6,4},{8,10},{10,8},{12,14},{14,12},{1,3},{3,1},... | collective-permute-start | bytes 49160 | tf_op jit(solution)/shard_map/ppermute | solution.py:447
  100.5 7.6 %collective-permute-start.20 = (bf16[16,512]{1,0:T(8,128)(2,1)}, bf16[16,512]{1,0:T(8,128)(2,1)S(1)}, u32[]{:S(2)}, u32[]{:S(2)}) collective-permute-start(bf16[16,512]{1,0:T(8,128)(2,1)} %get-tuple-element.84), channel_id=1, source_target_pairs={{2,4},{4,2},{6,8},{8,6},{10,12},{12,10},{3,5},{5,3},{7,9},{9,7},{1... | collective-permute-start | bytes 49160 | tf_op jit(solution)/shard_map/ppermute | solution.py:447
  101.2 7.0 %collective-permute-start.21 = (bf16[16,512]{1,0:T(8,128)(2,1)}, bf16[16,512]{1,0:T(8,128)(2,1)S(1)}, u32[]{:S(2)}, u32[]{:S(2)}) collective-permute-start(bf16[16,512]{1,0:T(8,128)(2,1)} %get-tuple-element.85), channel_id=1, source_target_pairs={{0,4},{4,0},{2,6},{6,2},{8,12},{12,8},{10,14},{14,10},{1,5},{5,1},... | collective-permute-start | bytes 49160 | tf_op jit(solution)/shard_map/ppermute | solution.py:447
  106.0 2.7 %collective-permute-start.22 = (bf16[16,512]{1,0:T(8,128)(2,1)}, bf16[16,512]{1,0:T(8,128)(2,1)S(1)}, u32[]{:S(2)}, u32[]{:S(2)}) collective-permute-start(bf16[16,512]{1,0:T(8,128)(2,1)} %get-tuple-element.86), channel_id=1, source_target_pairs={{4,8},{8,4},{6,10},{10,6},{5,9},{9,5},{7,11},{11,7},{20,24},{24,20... | collective-permute-start | bytes 49160 | tf_op jit(solution)/shard_map/ppermute | solution.py:447
  108.1 11.5 %collective-permute-start.28 = (bf16[8,64,512]{2,1,0:T(8,128)(2,1)}, bf16[8,64,512]{2,1,0:T(8,128)(2,1)S(1)}, u32[]{:S(2)}, u32[]{:S(2)}) collective-permute-start(bf16[8,64,512]{2,1,0:T(8,128)(2,1)} %add_convert_fusion.1), channel_id=1, source_target_pairs={{0,2},{2,0},{4,6},{6,4},{8,10},{10,8},{12,14},{14,12},{1,3},{3,1},... | collective-permute-start | bytes 1572872 | tf_op jit(solution)/shard_map/ppermute | solution.py:458
  108.1 21.3 %collective-permute-start.26 = (bf16[16,64,512]{2,1,0:T(8,128)(2,1)}, bf16[16,64,512]{2,1,0:T(8,128)(2,1)S(1)}, u32[]{:S(2)}, u32[]{:S(2)}) collective-permute-start(bf16[16,64,512]{2,1,0:T(8,128)(2,1)} %get-tuple-element.93), channel_id=1, source_target_pairs={{0,16},{16,0},{1,17},{17,1},{2,18},{18,2},{3,19},{19,3},{4,20},{20... | collective-permute-start | bytes 3145736 | tf_op jit(solution)/shard_map/ppermute | solution.py:451
  108.2 20.1 %collective-permute-start.25 = (bf16[16,48,512]{2,1,0:T(8,128)(2,1)}, bf16[16,48,512]{2,1,0:T(8,128)(2,1)}, u32[]{:S(2)}, u32[]{:S(2)}) collective-permute-start(bf16[16,48,512]{2,1,0:T(8,128)(2,1)} %get-tuple-element.91), channel_id=1, source_target_pairs={{0,16},{16,0},{1,17},{17,1},{2,18},{18,2},{3,19},{19,3},{4,20},{20... | collective-permute-start | bytes 2359304 | tf_op jit(solution)/shard_map/ppermute | solution.py:451
  108.7 6.0 %collective-permute-start.44 = (f32[2,512]{1,0:T(2,128)}, f32[2,512]{1,0:T(2,128)}, u32[]{:S(2)}, u32[]{:S(2)}) collective-permute-start(f32[2,512]{1,0:T(2,128)} %add.276), channel_id=1, source_target_pairs={{0,8},{2,10},{4,12},{6,14},{8,0},{10,2},{12,4},{14,6},{1,9},{3,11}... | collective-permute-start | bytes 12296 | tf_op jit(solution)/shard_map/ppermute | solution.py:458
  114.7 51.9 %collective-permute-start.24 = (bf16[384,512]{1,0:T(8,128)(2,1)}, bf16[384,512]{1,0:T(8,128)(2,1)S(1)}, u32[]{:S(2)}, u32[]{:S(2)}) collective-permute-start(bf16[384,512]{1,0:T(8,128)(2,1)} %broadcast_select_fusion), channel_id=1, source_target_pairs={{0,16},{16,0},{1,17},{17,1},{2,18},{18,2},{3,19},{19,3},{4,20},{20... | collective-permute-start | bytes 1179656 | tf_op jit(solution)/shard_map/ppermute | solution.py:451
  116.8 7.4 %collective-permute-start.31 = (bf16[4,48,512]{2,1,0:T(8,128)(2,1)S(1)}, bf16[4,48,512]{2,1,0:T(8,128)(2,1)S(1)}, u32[]{:S(2)}, u32[]{:S(2)}) collective-permute-start(bf16[4,48,512]{2,1,0:T(8,128)(2,1)S(1)} %add_convert_fusion.6), channel_id=1, source_target_pairs={{0,2},{2,0},{4,6},{6,4},{8,10},{10,8},{12,14},{14,12},{1,3},{3,1},... | collective-permute-start | bytes 589832 | tf_op jit(solution)/shard_map/ppermute | solution.py:458
  119.7 7.2 %collective-permute-start.32 = (bf16[4,64,512]{2,1,0:T(8,128)(2,1)S(1)}, bf16[4,64,512]{2,1,0:T(8,128)(2,1)S(1)}, u32[]{:S(2)}, u32[]{:S(2)}) collective-permute-start(bf16[4,64,512]{2,1,0:T(8,128)(2,1)S(1)} %add_convert_fusion.4), channel_id=1, source_target_pairs={{0,1},{1,0},{2,3},{3,2},{4,5},{5,4},{6,7},{7,6},{8,9},{9,8},{10,11... | collective-permute-start | bytes 786440 | tf_op jit(solution)/shard_map/ppermute | solution.py:456
  124.2 6.0 %collective-permute-start.23 = (bf16[128,512]{1,0:T(8,128)(2,1)S(1)}, bf16[128,512]{1,0:T(8,128)(2,1)S(1)}, u32[]{:S(2)}, u32[]{:S(2)}) collective-permute-start(bf16[128,512]{1,0:T(8,128)(2,1)S(1)} %broadcast_select_fusion.1), channel_id=1, source_target_pairs={{0,16},{16,0},{1,17},{17,1},{2,18},{18,2},{3,19},{19,3},{4,20},{20... | collective-permute-start | bytes 393224 | tf_op jit(solution)/shard_map/ppermute | solution.py:451
  127.0 6.6 %collective-permute-start.35 = (bf16[2,112,512]{2,1,0:T(8,128)(2,1)S(1)}, bf16[2,112,512]{2,1,0:T(8,128)(2,1)S(1)}, u32[]{:S(2)}, u32[]{:S(2)}) collective-permute-start(bf16[2,112,512]{2,1,0:T(8,128)(2,1)S(1)} %pad_maximum_fusion), channel_id=1, source_target_pairs={{0,4},{2,6},{4,0},{6,2},{8,12},{10,14},{12,8},{14,10},{1,5},{3,7},... | collective-permute-start | bytes 688136 | tf_op jit(solution)/shard_map/ppermute | solution.py:458
  129.6 10.3 %collective-permute-start.29 = (bf16[8,48,512]{2,1,0:T(8,128)(2,1)S(1)}, bf16[8,48,512]{2,1,0:T(8,128)(2,1)S(1)}, u32[]{:S(2)}, u32[]{:S(2)}) collective-permute-start(bf16[8,48,512]{2,1,0:T(8,128)(2,1)S(1)} %add_convert_fusion.2), channel_id=1, source_target_pairs={{0,1},{1,0},{2,3},{3,2},{4,5},{5,4},{6,7},{7,6},{8,9},{9,8},{10,11... | collective-permute-start | bytes 1179656 | tf_op jit(solution)/shard_map/ppermute | solution.py:456
  130.3 12.9 %collective-permute-start.30 = (bf16[8,64,512]{2,1,0:T(8,128)(2,1)S(1)}, bf16[8,64,512]{2,1,0:T(8,128)(2,1)S(1)}, u32[]{:S(2)}, u32[]{:S(2)}) collective-permute-start(bf16[8,64,512]{2,1,0:T(8,128)(2,1)S(1)} %add_convert_fusion), channel_id=1, source_target_pairs={{0,2},{2,0},{4,6},{6,4},{8,10},{10,8},{12,14},{14,12},{1,3},{3,1},... | collective-permute-start | bytes 1572872 | tf_op jit(solution)/shard_map/ppermute | solution.py:458
  143.2 5.7 %collective-permute-start.33 = (bf16[4,48,512]{2,1,0:T(8,128)(2,1)S(1)}, bf16[4,48,512]{2,1,0:T(8,128)(2,1)S(1)}, u32[]{:S(2)}, u32[]{:S(2)}) collective-permute-start(bf16[4,48,512]{2,1,0:T(8,128)(2,1)S(1)} %add_convert_fusion.7), channel_id=1, source_target_pairs={{0,2},{2,0},{4,6},{6,4},{8,10},{10,8},{12,14},{14,12},{1,3},{3,1},... | collective-permute-start | bytes 589832 | tf_op jit(solution)/shard_map/ppermute | solution.py:458
  145.1 6.4 %collective-permute-start.34 = (bf16[4,64,512]{2,1,0:T(8,128)(2,1)S(1)}, bf16[4,64,512]{2,1,0:T(8,128)(2,1)S(1)}, u32[]{:S(2)}, u32[]{:S(2)}) collective-permute-start(bf16[4,64,512]{2,1,0:T(8,128)(2,1)S(1)} %add_convert_fusion.5), channel_id=1, source_target_pairs={{0,1},{1,0},{2,3},{3,2},{4,5},{5,4},{6,7},{7,6},{8,9},{9,8},{10,11... | collective-permute-start | bytes 786440 | tf_op jit(solution)/shard_map/ppermute | solution.py:456
  146.7 7.0 %collective-permute-start.37 = (bf16[1,112,512]{2,1,0:T(8,128)(2,1)S(1)}, bf16[1,112,512]{2,1,0:T(8,128)(2,1)S(1)}, u32[]{:S(2)}, u32[]{:S(2)}) collective-permute-start(bf16[1,112,512]{2,1,0:T(8,128)(2,1)S(1)} %pad_maximum_fusion.4), channel_id=1, source_target_pairs={{0,8},{2,10},{4,12},{6,14},{8,0},{10,2},{12,4},{14,6},{1,9},{3,11}... | collective-permute-start | bytes 344072 | tf_op jit(solution)/shard_map/ppermute | solution.py:458
  151.7 6.1 %collective-permute-start.36 = (bf16[2,112,512]{2,1,0:T(8,128)(2,1)S(1)}, bf16[2,112,512]{2,1,0:T(8,128)(2,1)S(1)}, u32[]{:S(2)}, u32[]{:S(2)}) collective-permute-start(bf16[2,112,512]{2,1,0:T(8,128)(2,1)S(1)} %pad_maximum_fusion.1), channel_id=1, source_target_pairs={{0,4},{2,6},{4,0},{6,2},{8,12},{10,14},{12,8},{14,10},{1,5},{3,7},... | collective-permute-start | bytes 688136 | tf_op jit(solution)/shard_map/ppermute | solution.py:458
  158.7 7.0 %collective-permute-start.38 = (bf16[1,112,512]{2,1,0:T(8,128)(2,1)S(1)}, bf16[1,112,512]{2,1,0:T(8,128)(2,1)S(1)}, u32[]{:S(2)}, u32[]{:S(2)}) collective-permute-start(bf16[1,112,512]{2,1,0:T(8,128)(2,1)S(1)} %pad_maximum_fusion.5), channel_id=1, source_target_pairs={{0,8},{2,10},{4,12},{6,14},{8,0},{10,2},{12,4},{14,6},{1,9},{3,11}... | collective-permute-start | bytes 344072 | tf_op jit(solution)/shard_map/ppermute | solution.py:458
  166.6 1.6 collective-permute-start.39
  (27 other events, 126.3 us)

commit v2 on v1

v2 whole, which is shorter than its diff:
```python
import functools

import jax
import jax.numpy as jnp
from jax import lax
from jax.experimental import pallas as pl
from jax.experimental.pallas import tpu as pltpu
from jax.sharding import PartitionSpec as P

NODE_DEV = 128
HALO = 16
OFFSETS = (1, -1, 2, -2)
ROUNDS = len(OFFSETS)
D = 512
EPS = 1e-05
CHUNK = 384
BF = jnp.bfloat16
F32 = jnp.float32
GAINS = 16
VMEM_LIMIT = 63 * 1024 * 1024

ROWS = {"ein": 3 * D, "eout": D, "nin": 2 * D, "nout": D}
GROUPS = {"node": ("nin", "nout"), "edge": ("ein", "eout")}
SEQUENCE = (
    {"node": (0, 1, 3, 2), "edge": (1, 0, 3, 2)},
    {"node": (0, 2, 3, 1), "edge": (1, 2, 3, 0)},
)


def mm(a, b):
    return lax.dot_general(a, b, (((1,), (0,)), ((), ())), preferred_element_type=F32)


def mm_t(a, b):
    return lax.dot_general(a, b, (((1,), (1,)), ((), ())), preferred_element_type=F32)


def t_mm(a, b):
    return lax.dot_general(a, b, (((0,), (0,)), ((), ())), preferred_element_type=F32)


def one_hot(rows, index):
    where = lax.broadcasted_iota(jnp.int32, (rows, index.shape[1]), 0) == index
    return jnp.where(where, 1.0, 0.0).astype(BF)


def incidence(dst, count):
    edges = dst.shape[1]
    hit = lax.broadcasted_iota(jnp.int32, (NODE_DEV, edges), 0) == dst
    live = lax.broadcasted_iota(jnp.int32, (NODE_DEV, edges), 1) < count
    return jnp.where(hit & live, 1.0, 0.0).astype(BF)


def normed(values):
    center = values - jnp.mean(values, axis=-1, keepdims=True)
    spread = jnp.mean(center * center, axis=-1, keepdims=True)
    return center, lax.rsqrt(spread + EPS)


def silu_pair(pre):
    gate = lax.logistic(pre)
    return pre * gate, gate * (1.0 + pre * (1.0 - gate))


def norm_back(cot, hat, rate, gain):
    scaled = cot * gain
    first = jnp.mean(scaled, axis=-1, keepdims=True)
    second = jnp.mean(scaled * hat, axis=-1, keepdims=True)
    return rate * (scaled - first - hat * second)


def forward(own, edges, table, src, dst, count, weights, waits, gains, res):
    w_ein, w_eout, w_nin, w_nout = weights
    g_edge, g_node = gains
    rows = edges.shape[0]
    hot_src = one_hot(table.shape[0], src)
    hot_dst = one_hot(NODE_DEV, dst)
    waits[0]()
    waits[1]()
    for at in range(0, rows, CHUNK):
        part = slice(at, at + CHUNK)
        edge = edges[part]
        sender = t_mm(hot_src[:, part], table[...]).astype(BF)
        receiver = t_mm(hot_dst[:, part], own[...]).astype(BF)
        pre = mm(edge, w_ein[:D]) + mm(sender, w_ein[D : 2 * D]) + mm(receiver, w_ein[2 * D :])
        middle, slope = silu_pair(pre)
        middle = middle.astype(BF)
        center, rate = normed(mm(middle, w_eout[...]))
        live = lax.broadcasted_iota(jnp.int32, (CHUNK, 1), 0) + at < count
        rate = jnp.where(live, rate, 0.0)
        hat = center * rate
        res["edge_new"][part] = (edge.astype(F32) + hat * g_edge).astype(BF)
        res["edge_mid"][part] = middle
        res["edge_slope"][part] = slope.astype(BF)
        res["edge_hat"][part] = hat.astype(BF)
        res["edge_rate"][part] = jnp.broadcast_to(rate, (CHUNK, 128))
    agg = mm(incidence(dst, count), res["edge_new"][...]).astype(BF)
    waits[2]()
    waits[3]()
    pre = mm(own[...], w_nin[:D]) + mm(agg, w_nin[D:])
    middle, slope = silu_pair(pre)
    middle = middle.astype(BF)
    center, rate = normed(mm(middle, w_nout[...]))
    hat = center * rate
    res["node_new"][...] = (own[...].astype(F32) + hat * g_node).astype(BF)
    res["agg"][...] = agg
    res["node_mid"][...] = middle
    res["node_slope"][...] = slope.astype(BF)
    res["node_hat"][...] = hat.astype(BF)
    res["node_rate"][...] = jnp.broadcast_to(rate, (NODE_DEV, 128))


def slot_of(shard, me, shards, sequence):
    if shards == 1:
        return 0
    apart = jnp.bitwise_xor(jnp.int32(shard), me)
    slot = jnp.int32(0)
    for bit in sequence:
        slot = slot * 2 + jnp.bitwise_and(lax.shift_right_logical(apart, jnp.int32(bit)), 1)
    return slot


class Layout:
    def __init__(self, shards):
        self.shards = shards
        self.half = {name: rows // shards // 2 for name, rows in ROWS.items()}
        self.size = {g: sum(self.half[n] for n in names) for g, names in GROUPS.items()}
        self.gains = shards * self.size["node"]
        self.base = {"node": 0, "edge": self.gains + GAINS}
        self.rows = self.base["edge"] + shards * self.size["edge"]
        self.inner = {}
        for names in GROUPS.values():
            at = 0
            for name in names:
                self.inner[name] = at
                at += self.half[name]

    def span(self, group):
        return slice(self.base[group], self.base[group] + self.shards * self.size[group])


def emit(value, name, first_row, layout, group, store, core, slots):
    half = layout.half[name]
    value = value.astype(BF)
    last_row = first_row + value.shape[0]
    for piece in range(2 * layout.shards):
        low, high = max(piece * half, first_row), min((piece + 1) * half, last_row)
        if low < high:
            keep = jnp.bitwise_xor(core, piece % 2)
            to = layout.base[group] + layout.inner[name] + low - piece * half
            if layout.shards > 1:
                to = pl.multiple_of(slots[piece // 2] * layout.size[group] + to, 16)
            store[keep, pl.ds(to, high - low), :] = value[low - first_row : high - first_row]


def backward(
    cot_node, cot_edge, own, edges, table, src, dst, count, weights, gains, res, core, me, layout, sequence,
    store, outs, work, ready,
):
    w_ein, w_eout, w_nin, w_nout = weights
    g_edge, g_node = gains
    d_own_out, d_edges_out, room, put_gains = outs
    d_outer, d_pre = work
    rows = edges.shape[0]
    shards = layout.shards
    slots = {
        g: [slot_of(i, me, shards, sequence[g]) for i in range(shards)] for g in GROUPS
    }

    def put(value, name, first_row):
        group = "node" if name in GROUPS["node"] else "edge"
        emit(value, name, first_row, layout, group, store, core, slots[group])

    hat = res["node_hat"][...].astype(F32)
    gain_node = jnp.sum(cot_node * hat, axis=0, keepdims=True)
    d_out = norm_back(cot_node, hat, res["node_rate"][:, :1], g_node).astype(BF)
    put(t_mm(res["node_mid"][...], d_out), "nout", 0)
    d_pre_node = (mm_t(d_out, w_nout[...]) * res["node_slope"][...].astype(F32)).astype(BF)
    put(t_mm(own[...], d_pre_node), "nin", 0)
    put(t_mm(res["agg"][...], d_pre_node), "nin", D)
    ready("node")
    d_own = cot_node + mm_t(d_pre_node, w_nin[:D])
    d_agg = mm_t(d_pre_node, w_nin[D:]).astype(BF)

    joins = incidence(dst, count)
    gain_edge = jnp.zeros((1, D), F32)
    for at in range(0, rows, CHUNK):
        part = slice(at, at + CHUNK)
        cot = t_mm(joins[:, part], d_agg)
        if cot_edge is not None:
            cot = cot + cot_edge[part].astype(F32)
        hat = res["edge_hat"][part].astype(F32)
        gain_edge = gain_edge + jnp.sum(cot * hat, axis=0, keepdims=True)
        outer = norm_back(cot, hat, res["edge_rate"][part, :1], g_edge).astype(BF)
        d_outer[part] = outer
        pre = (mm_t(outer, w_eout[...]) * res["edge_slope"][part].astype(F32)).astype(BF)
        d_pre[part] = pre
        d_edges_out[part] = (cot + mm_t(pre, w_ein[:D])).astype(BF)
    put(t_mm(res["edge_mid"][...], d_outer[...]), "eout", 0)
    put(t_mm(edges[...], d_pre[...]), "ein", 0)
    to_src = mm(one_hot(table.shape[0], src), d_pre[...]).astype(BF)
    to_dst = mm(one_hot(NODE_DEV, dst), d_pre[...]).astype(BF)
    put(t_mm(table[...], to_src), "ein", D)
    put(t_mm(own[...], to_dst), "ein", 2 * D)
    put_gains(jnp.concatenate([gain_edge, gain_node, jnp.zeros((GAINS - 2, D), F32)], axis=0))
    ready("edge")
    d_table = mm_t(to_src, w_ein[D : 2 * D])
    d_own = d_own + d_table[:NODE_DEV] + mm_t(to_dst, w_ein[2 * D :])
    d_own_out[...] = d_own
    d_halo = d_table[NODE_DEV:].astype(BF)
    place(-1, [d_halo[j * HALO : (j + 1) * HALO] for j in range(ROUNDS)], room)


SAVED = (
    ("edge_mid", None),
    ("edge_slope", None),
    ("edge_hat", None),
    ("agg", NODE_DEV),
    ("node_mid", NODE_DEV),
    ("node_slope", NODE_DEV),
    ("node_hat", NODE_DEV),
)


def saved_rows(rows):
    return sum(h or rows for _, h in SAVED)


def views(rows, held, rates):
    out, at = {}, 0
    for name, height in SAVED:
        out[name] = held.at[at : at + (height or rows)]
        at += height or rows
    out["edge_rate"] = rates.at[:rows]
    out["node_rate"] = rates.at[rows : rows + NODE_DEV]
    return out


class Copies:
    def __init__(self, sems):
        self.sems, self.used, self.out = sems, 0, []

    def start(self, source, target):
        copy = pltpu.make_async_copy(source, target, self.sems.at[self.used])
        self.used += 1
        copy.start()
        return copy

    def send(self, source, target):
        self.out.append(self.start(source, target))

    def either(self, choice, yes, no, targets):
        sems = [self.sems.at[self.used + i] for i in range(len(targets))]
        self.used += len(targets)

        def start(refs):
            for ref, to, sem in zip(refs, targets, sems):
                pltpu.make_async_copy(ref, to, sem).start()

        pl.when(choice)(lambda: start(yes))
        pl.when(jnp.logical_not(choice))(lambda: start(no))
        return [
            pltpu.make_async_copy(ref, to, sem).wait for ref, to, sem in zip(yes, targets, sems)
        ]

    def finish(self):
        for copy in self.out:
            copy.wait()


def shard_number(shards):
    if shards == 1:
        return jnp.int32(0)
    return lax.axis_index("dom") * lax.axis_size("rep") + lax.axis_index("rep")


def first_rows(refs):
    return [ref.at[0] for ref in refs]


def one_hots(lists):
    return [one_hot(NODE_DEV, lists[0, j : j + 1]) for j in range(ROUNDS)]


def place(sign, pieces, room):
    part, parts = lax.axis_index("dom"), lax.axis_size("dom")
    room[...] = jnp.zeros_like(room)
    for piece, offset in zip(pieces, OFFSETS):
        to = part + sign * offset

        def put(piece=piece, to=to):
            room[pl.ds(pl.multiple_of(to * HALO, HALO), HALO), :] = piece

        pl.when((to >= 0) & (to < parts))(put)


def placed(sign, room):
    part, parts = lax.axis_index("dom"), lax.axis_size("dom")
    out = []
    for offset in OFFSETS:
        source = part + sign * offset
        there = jnp.clip(source, 0, parts - 1)
        rows = room[pl.ds(pl.multiple_of(there * HALO, HALO), HALO), :]
        out.append(jnp.where((source >= 0) & (source < parts), rows, jnp.zeros_like(rows)))
    return out


def pick(hot, values):
    return [t_mm(one, values).astype(BF) for one in hot]


def fill_halo(table, room):
    for j, rows in enumerate(placed(-1, room)):
        table[NODE_DEV + j * HALO : NODE_DEV + (j + 1) * HALO] = rows


def spread(hot, pieces):
    total = mm(hot[0], pieces[0])
    for j in range(1, ROUNDS):
        total = total + mm(hot[j], pieces[j])
    return total


def pick_kernel(lists, nodes, sent, own, room, sems):
    copies = Copies(sems)
    copy = copies.start(nodes.at[lax.axis_index("segment")], own)
    hot = one_hots(lists)
    copy.wait()
    place(1, pick(hot, own[...]), room)
    copies.send(room, sent)
    copies.finish()


def first_kernel(count, src, dst, lists, g_mine, g_other, nodes, latents, *rest):
    halo, mine, other, rest = rest[0], rest[1:5], rest[5:9], rest[9:]
    (node_out, edge_out, saved_out, rate_out, sent), rest = rest[:5], rest[5:]
    held, rest = rest[:4], rest[4:]
    table, edges, saved, rates, room, node_new, edge_new, sems = rest
    core = lax.axis_index("segment")
    own = table.at[:NODE_DEV]
    copies = Copies(sems)
    coming = [copies.start(nodes.at[core], own), copies.start(latents.at[core], edges)]
    coming += [copies.start(halo, room)]
    waits = copies.either(core == 0, first_rows(mine), first_rows(other), held)
    src, dst = src[...], dst[...]
    gains = jnp.where(core == 0, g_mine[...], g_other[...])
    res = views(edges.shape[0], saved, rates)
    res.update(node_new=node_new, edge_new=edge_new)
    for copy in coming:
        copy.wait()
    fill_halo(table, room)
    forward(
        own, edges, table, src, dst, count[0], held, waits, (gains[:1], gains[1:2]), res
    )
    place(1, pick(one_hots(lists), node_new[...]), room)
    for source, target in zip(
        (room, node_new, edge_new, saved, rates),
        (sent, node_out, edge_out, saved_out, rate_out),
    ):
        copies.send(source, target)
    copies.finish()


def back_outs(copies, layout, store, outs, work):
    d_own, d_edges, sent, keep, send = outs
    d_own_s, d_edges_s, room = work

    def ready(group):
        first = layout.base[group] if group == "node" else layout.gains
        rows = pl.ds(first, layout.span(group).stop - first)
        copies.send(store.at[1, rows], send.at[rows])
        copies.send(store.at[0, rows], keep.at[rows])

    def finish():
        copies.send(room, sent)
        copies.send(d_own_s, d_own)
        copies.send(d_edges_s, d_edges)
        copies.finish()

    return ready, finish


def second_kernel(shards, count, src, dst, lists, g_mine, g_other, nodes, latents, cots, *rest):
    halo, mine, other, rest = rest[0], rest[1:5], rest[5:9], rest[9:]
    (node_out, edge_out, gain_out), rest = rest[:3], rest[3:]
    outs, rest = rest[:5], rest[5:]
    held, rest = rest[:4], rest[4:]
    table, edges, saved, rates, room, node_new, edge_new, cot, rest = *rest[:8], rest[8:]
    d_outer, d_pre, store, *work, sems = rest
    layout = Layout(shards)
    core, me = lax.axis_index("segment"), shard_number(shards)
    own = table.at[:NODE_DEV]
    copies = Copies(sems)
    coming = [copies.start(nodes, own), copies.start(latents, edges)]
    coming += [copies.start(halo, room)]
    waits = copies.either(core == 1, first_rows(mine), first_rows(other), held)
    cot_copy = copies.start(cots.at[core], cot)
    src, dst = src[...], dst[...]
    gains = jnp.where(core == 1, g_mine[...], g_other[...])
    gains = (gains[:1], gains[1:2])
    res = views(edges.shape[0], saved, rates)
    res.update(node_new=node_new, edge_new=edge_new)
    for copy in coming:
        copy.wait()
    fill_halo(table, room)
    forward(own, edges, table, src, dst, count[0], held, waits, gains, res)
    copies.send(node_new, node_out)
    copies.send(edge_new, edge_out)
    cot_copy.wait()
    ready, finish = back_outs(copies, layout, store, outs, (*work, room))

    def put_gains(value):
        gain_out[...] = value
        for side in range(2):
            store[side, layout.gains : layout.gains + GAINS] = jnp.zeros((GAINS, D), BF)

    backward(
        cot[...].astype(F32), None, own, edges, table, src, dst, count[0], held, gains, res,
        core, me, layout, SEQUENCE[1], store, (*work[:2], room, put_gains), (d_outer, d_pre), ready,
    )
    finish()


def third_kernel(
    shards, count, src, dst, lists, g_mine, g_other, gain_one, nodes, latents, d_own_in,
    d_edges_in, saved_in, rate_in, *rest
):
    halo, back, mine, other, rest = rest[0], rest[1], rest[2:6], rest[6:10], rest[10:]
    outs, rest = rest[:5], rest[5:]
    held, rest = rest[:4], rest[4:]
    table, edges, saved, rates, room, cot_own, cot_edge, got, rest = *rest[:8], rest[8:]
    d_outer, d_pre, store, *work, sems = rest
    layout = Layout(shards)
    core, me = lax.axis_index("segment"), shard_number(shards)
    own = table.at[:NODE_DEV]
    copies = Copies(sems)
    coming = [copies.start(back, got)]
    coming += [copies.start(d_own_in, cot_own), copies.start(rate_in, rates)]
    coming += [copies.start(saved_in, saved), copies.start(nodes.at[core], own)]
    coming += [copies.start(halo, room)]
    waits = copies.either(core == 0, first_rows(mine), first_rows(other), held)
    coming += [copies.start(d_edges_in, cot_edge), copies.start(latents.at[core], edges)]
    src, dst = src[...], dst[...]
    gains = jnp.where(core == 0, g_mine[...], g_other[...])
    gains = (gains[:1], gains[1:2])
    res = views(edges.shape[0], saved, rates)
    hot = one_hots(lists)
    for copy in coming:
        copy.wait()
    fill_halo(table, room)
    cot = (cot_own[...] + spread(hot, placed(1, got))).astype(BF).astype(F32)
    for wait in waits:
        wait()
    ready, finish = back_outs(copies, layout, store, outs, (*work, room))

    def put_gains(value):
        both = (value.astype(BF), gain_one[...].astype(BF))
        rows = slice(layout.gains, layout.gains + GAINS)
        store[0, rows] = jnp.where(core == 0, both[0], both[1])
        store[1, rows] = jnp.where(core == 0, both[1], both[0])

    backward(
        cot, cot_edge, own, edges, table, src, dst, count[0], held, gains, res,
        core, me, layout, SEQUENCE[0], store, (*work[:2], room, put_gains), (d_outer, d_pre), ready,
    )
    finish()


def last_kernel(lists, d_own, back, out):
    out[...] = (d_own[...] + spread(one_hots(lists), placed(1, back))).astype(BF)


def weight_scratch():
    return [pltpu.VMEM((r, D), BF) for r in ROWS.values()]


SMEM = pl.BlockSpec(memory_space=pltpu.SMEM)
VMEM = pl.BlockSpec(memory_space=pltpu.VMEM)
ANY = pl.BlockSpec(memory_space=pl.ANY)


def shape(dims, dtype):
    return jax.ShapeDtypeStruct(tuple(dims), dtype)


def call(kernel, in_specs, outs, out_specs, scratch, flops, traffic):
    return pl.pallas_call(
        kernel,
        in_specs=in_specs,
        out_shape=outs,
        out_specs=out_specs,
        scratch_shapes=scratch,
        compiler_params=pltpu.CompilerParams(vmem_limit_bytes=VMEM_LIMIT),
        cost_estimate=pl.CostEstimate(flops=flops, bytes_accessed=traffic, transcendentals=0),
    )


def exchange(rows):
    return lax.all_to_all(rows, "dom", 0, 0, tiled=True)


def other_core(value):
    return lax.ppermute(value, "segment", [(0, 1), (1, 0)])


def across(value, apart):
    if apart == 1:
        return lax.ppermute(value, "rep", [(0, 1), (1, 0)])
    step = apart // 2
    return lax.ppermute(value, "dom", [(p, p ^ step) for p in range(lax.axis_size("dom"))])


def added(pieces):
    total = pieces[0].astype(F32)
    for piece in pieces[1:]:
        total = total + piece.astype(F32)
    return total


def tied(values, others):
    return lax.optimization_barrier((list(values), list(others)))[0]


class Rows:
    def __init__(self, first, rows, arrays):
        self.rows, self.terms = rows, [(a, first) for a in arrays]

    def upper(self):
        self.rows //= 2
        return self.rows, [(a, first + self.rows) for a, first in self.terms]

    def whole(self):
        return self.rows, list(self.terms)

    def quarter(self, i):
        rows = self.rows // 4
        return rows, [(a, first + i * rows) for a, first in self.terms]

    def add(self, array, first):
        self.terms.append((array, first))


def combine(outputs):
    arrays = []
    for _, segments in outputs:
        for _, terms in segments:
            arrays += [a for a, _ in terms if all(a is not b for b in arrays)]
    total = sum(rows * len(terms) for _, segments in outputs for rows, terms in segments)
    copies = sum(len(terms) for _, segments in outputs for _, terms in segments)
    heights = [sum(rows for rows, _ in segments) for _, segments in outputs]

    def kernel(*refs):
        sources, refs = refs[: len(arrays)], refs[len(arrays) :]
        outs, refs = refs[: len(outputs)], refs[len(outputs) :]
        held, sums, sems, out_sems = refs[0], refs[1:-2], refs[-2], refs[-1]
        plan, at, used = [], 0, 0
        for _, segments in outputs:
            for rows, terms in segments:
                places = []
                for array, first in terms:
                    which = [array is a for a in arrays].index(True)
                    copy = pltpu.make_async_copy(
                        sources[which].at[first : first + rows],
                        held.at[at : at + rows],
                        sems.at[used],
                    )
                    copy.start()
                    places.append((at, copy))
                    at, used = at + rows, used + 1
                plan.append(places)
        plan, gone = iter(plan), []
        for i, (dtype, segments) in enumerate(outputs):
            to = 0
            for rows, _ in segments:
                places = next(plan)
                for _, copy in places:
                    copy.wait()
                for low in range(0, rows, 64):
                    high = min(low + 64, rows)
                    value = added([held[p + low : p + high] for p, _ in places])
                    sums[i][to + low : to + high] = value.astype(dtype)
                to += rows
            gone.append(pltpu.make_async_copy(sums[i], outs[i], out_sems.at[i]))
            gone[-1].start()
        for copy in gone:
            copy.wait()

    shapes = [((height, D), dtype) for height, (dtype, _) in zip(heights, outputs)]
    return call(
        kernel,
        [ANY] * len(arrays),
        [shape(*s) for s in shapes],
        [ANY] * len(outputs),
        [
            pltpu.VMEM((total, D), BF),
            *[pltpu.VMEM(*s) for s in shapes],
            pltpu.SemaphoreType.DMA((copies,)),
            pltpu.SemaphoreType.DMA((len(outputs),)),
        ],
        10**6,
        8 * 10**6,
    )(*arrays)


def summed(rows, terms):
    return added([a[first : first + rows] for a, first in terms]).astype(BF)


def sent_parts(parts):
    return (BF, [p.upper() for p in parts])


def receive(parts, got):
    at = 0
    for part in parts:
        part.add(got, at)
        at += part.rows
    return got


def body(
    node_latent,
    edge_latent,
    node_cot,
    edge_src,
    edge_dst,
    edge_count,
    send_index,
    w_edge_in,
    w_edge_out,
    w_node_in,
    w_node_out,
    gain_edge,
    gain_node,
):
    micro, _, _ = node_latent.shape
    rows = edge_latent.shape[1]
    assert micro == lax.axis_size("segment") == 2
    doms, reps = lax.axis_size("dom"), lax.axis_size("rep")
    core, part, rep = (lax.axis_index(a) for a in ("segment", "dom", "rep"))
    shards = doms * reps if doms * reps == 16 else 1
    first = core == 0

    src, dst = edge_src[None], edge_dst[None]

    dma = pltpu.SemaphoreType.DMA
    halo_shape = shape((doms * HALO, D), BF)
    node_s, edge_s = pltpu.VMEM((NODE_DEV, D), BF), pltpu.VMEM((rows, D), BF)
    room_s = pltpu.VMEM((doms * HALO, D), BF)
    sent = call(
        pick_kernel,
        [VMEM, ANY],
        halo_shape,
        ANY,
        [node_s, room_s, dma((2,))],
        10**7,
        7 * 10**6,
    )(send_index, node_latent)
    halo_zero = exchange(sent)
    mine = (w_edge_in, w_edge_out, w_node_in, w_node_out)
    other = tuple(other_core(w) for w in mine)
    g_mine = jnp.concatenate([gain_edge, gain_node], axis=0)
    small = (edge_count, src, dst, send_index, g_mine, other_core(g_mine))
    small_specs = [SMEM] + [VMEM] * 5

    table_s = pltpu.VMEM((NODE_DEV + ROUNDS * HALO, D), BF)
    saved_dims, rate_dims = (saved_rows(rows), D), (rows + NODE_DEV, 128)
    layer_s = [
        *weight_scratch(),
        table_s,
        edge_s,
        pltpu.VMEM(saved_dims, BF),
        pltpu.VMEM(rate_dims, F32),
        room_s,
    ]
    node_one, edge_one, saved, rates, sent = call(
        first_kernel,
        small_specs + [ANY] * (2 + 1 + 8),
        [
            shape((NODE_DEV, D), BF),
            shape((rows, D), BF),
            shape(saved_dims, BF),
            shape(rate_dims, F32),
            halo_shape,
        ],
        [ANY] * 5,
        [*layer_s, node_s, edge_s, dma((20,))],
        11 * 10**8,
        26 * 10**6,
    )(*small, node_latent, edge_latent, halo_zero, *mine, *other)
    halo_one = exchange(sent)

    layout = Layout(shards)

    def group_rows(values):
        return [
            Rows(layout.base[g], shards * layout.size[g], values) for g in GROUPS
        ]

    share = shape((layout.rows, D), BF)
    back_shapes = [
        shape((NODE_DEV, D), F32),
        shape((rows, D), BF),
        halo_shape,
        share,
        share,
    ]
    back_s = [
        edge_s,
        edge_s,
        pltpu.VMEM((2, layout.rows, D), BF),
        pltpu.VMEM((NODE_DEV, D), F32),
        edge_s,
        dma((40,)),
    ]
    node_two, edge_two, gain_one, *done = call(
        functools.partial(second_kernel, shards),
        small_specs + [ANY] * (3 + 1 + 8),
        [shape((NODE_DEV, D), BF), shape((rows, D), BF), shape((GAINS, D), F32)] + back_shapes,
        [ANY, ANY, VMEM] + [ANY] * len(back_shapes),
        [*layer_s, node_s, edge_s, node_s, *back_s],
        28 * 10**8,
        44 * 10**6,
    )(*small, node_one, edge_one, node_cot, halo_one, *mine, *other)
    d_own, d_edges, sent, keep_one, send_one = done
    back = exchange(sent)
    one = keep_one, other_core(send_one)
    if shards > 1:
        one = group_rows(one)
        gone = [summed(*p.upper()) for p in one]
        (back,) = tied([back], gone)
        got = [receive([p], across(v, a)) for p, v, a in zip(one, gone, (1, 2))]

    d_own, d_edges, sent, keep_zero, send_zero = call(
        functools.partial(third_kernel, shards),
        small_specs + [VMEM] + [ANY] * (6 + 2 + 8),
        back_shapes,
        [ANY] * len(back_shapes),
        [*layer_s, pltpu.VMEM((NODE_DEV, D), F32), edge_s, room_s, *back_s],
        18 * 10**8,
        37 * 10**6,
    )(
        *small, gain_one, node_latent, edge_latent, d_own, d_edges, saved, rates, halo_zero,
        back, *mine, *other,
    )

    if shards > 1:
        (send_zero,) = tied([send_zero], got)
        zero = keep_zero, other_core(send_zero)
        sums = Rows(layout.gains, GAINS, zero)
        nodes, edges = group_rows(zero)
        gone = combine(
            [sent_parts(one), (BF, [edges.upper()]), (BF, [nodes.upper(), sums.whole()])]
        )
        receive(one, across(gone[0], 4))
        receive([edges], across(gone[1], 2))
        receive([nodes, sums], across(gone[2], 1))
        gone = combine(
            [(BF, [edges.upper()]), (BF, [nodes.upper(), sums.whole()]), sent_parts(one)]
        )
        (sent,) = tied([sent], gone)
        back = exchange(sent)
        receive([edges], across(gone[0], 1))
        receive([nodes, sums], across(gone[1], 2))
        receive(one, across(gone[2], 8))
        zero = [sums, nodes, edges]
        far = [
            [p.quarter(i) if p.rows > GAINS else p.whole() for p in zero] for i in range(4)
        ]
        near = [p.upper() for p in one]
        far[0] += [p.whole() for p in one]
        *far, near_n, near_e, stay = combine(
            [*[(BF, v) for v in far[1:]], *[(BF, [v]) for v in near], (F32, far[0])]
        )
        got = [across(v, 4 * i) for i, v in enumerate(far, 1)]
        near = [across(near_n, 2), across(near_e, 1)]
        rows = got[0].shape[0]
        zero = added([stay[:rows], *got])
        one = added([stay[rows:], jnp.concatenate(near, axis=0)])
        sums, zero = zero[:GAINS], zero[GAINS:]
        (back,) = tied([back], far)
    else:
        back = exchange(sent)
        zero = keep_zero, other_core(send_zero)
        rows = slice(layout.gains, layout.gains + GAINS)
        sums = lax.psum(added([v[rows] for v in zero]), ("dom", "rep"))
        one, zero = (
            jnp.concatenate([added([v[layout.span(g)] for v in x]) for g in GROUPS], axis=0)
            for x in (one, zero)
        )

    d_nodes = call(
        last_kernel,
        [VMEM] * 3,
        shape((NODE_DEV, D), BF),
        VMEM,
        [],
        10**7,
        7 * 10**6,
    )(send_index, d_own, back)

    def paired(gradient, latent):
        got = other_core(jnp.where(first, latent, gradient))
        low = jnp.where(first, gradient, got)
        high = jnp.where(first, got, latent)
        return jnp.stack([low, high])[None]

    factor = float(micro * reps * NODE_DEV * doms) ** (-0.5)
    got = other_core(jnp.where(first, one, zero))
    at, places = 0, {}
    for names in GROUPS.values():
        for name in names:
            places[name] = (at, ROWS[name] // shards // 2)
            at += places[name][1]
    scale = factor if shards > 1 else 1.0

    def grads_kernel(got, one, zero, *outs):
        mine = lax.axis_index("segment") == 0
        for out, name in zip(outs, ROWS):
            at, size = places[name]
            rows = slice(at, at + size)
            kept = jnp.where(mine, zero[rows], one[rows])
            out[:size] = jnp.where(mine, kept, got[rows]) * scale
            out[size:] = jnp.where(mine, got[rows], kept) * scale

    grads = call(
        grads_kernel,
        [VMEM] * 3,
        [shape((rows // shards, D), F32) for rows in ROWS.values()],
        [VMEM] * 4,
        [],
        10**6,
        7 * 10**6,
    )(got, one, zero)
    grads = dict(zip(ROWS, grads))
    if shards == 1:
        grads = {
            k: lax.psum_scatter(v, ("dom", "rep"), scatter_dimension=0, tiled=True) * factor
            for k, v in grads.items()
        }
    width = D // (doms * reps)
    sums = lax.dynamic_slice_in_dim(sums[:2], (part * reps + rep) * width, width, axis=1) * factor
    return (
        paired(d_nodes, node_two),
        paired(d_edges, edge_two),
        grads["ein"][None],
        grads["eout"][None],
        grads["nin"][None],
        grads["nout"][None],
        sums[:1],
        sums[1:2],
    )


def solution(mesh):
    placed = (
        P("rep", "dom", None),
        P("rep", "dom", None),
        P("rep", "dom", None),
        P("dom"),
        P("dom"),
        P("dom"),
        P("dom", None, None),
        P("segment", None, None),
        P("segment", None, None),
        P("segment", None, None),
        P("segment", None, None),
        P("segment", None),
        P("segment", None),
    )
    return jax.shard_map(
        body,
        mesh=mesh,
        in_specs=placed,
        out_specs=(
            P("segment", "rep", "dom", None),
            P("segment", "rep", "dom", None),
            P("segment", ("dom", "rep"), None),
            P("segment", ("dom", "rep"), None),
            P("segment", ("dom", "rep"), None),
            P("segment", ("dom", "rep"), None),
            P("segment", ("dom", "rep")),
            P("segment", ("dom", "rep")),
        ),
        check_vma=False,
    )
```

time: 172 us -> 137 us (0.80)
  starting transfers between devices: 64.4 us -> 34.1 us
  waiting for transfers between devices: 40.6 us -> 25.2 us
  other arithmetic: 25.4 us -> 12.5 us
  blocking collectives: 0 us -> 11.3 us
  Pallas kernels: 33.7 us -> 42.5 us
  local copies, waits for them, and re-layouts: 4.69 us -> 9.05 us
    ppermute x16 -> x0, starting transfers between devices: 38 us -> none  [exchange(): lax.ppermute(piece, 'dom', route)]
    all_to_all x0 -> x3, starting transfers between devices: none -> 14.6 us  [exchange(): return lax.all_to_all(rows, 'dom', 0, 0, tiled=True)]
    ppermute x11 -> x9, waiting for transfers between devices: 21.6 us -> 9.34 us  [across(): lax.ppermute(value, 'dom', [(p, p ^ step) for p in range(lax.axis_size('d...]
    all_to_all x0 -> x1, blocking collectives: none -> 11.3 us  [exchange(): return lax.all_to_all(rows, 'dom', 0, 0, tiled=True)]
    pallas_call x5 -> x9, Pallas kernels: 33.7 us -> 42.5 us  [the longest x1 10.8 us: body(): call(functools.partial(second_kernel, shards), small_specs + [ANY] * (3 +...]
    convert_element_type x16 -> x2, other arithmetic: 11.5 us -> 4.21 us  [summed(): return added([a[first:first + rows] for a, first in terms]).astype(BF)]
    ppermute x16 -> x0, waiting for transfers between devices: 5.78 us -> none  [exchange(): lax.ppermute(piece, 'dom', route)]
    ppermute x11 -> x9, starting transfers between devices: 17.8 us -> 13 us  [across(): lax.ppermute(value, 'dom', [(p, p ^ step) for p in range(lax.axis_size('d...]
  transfers between devices with their start and end apart: 45 -> 26, of which waited for: 18 -> 7; matrix products, arithmetic and copies ran while one was open for 13% -> 11% of each run, Pallas kernels for 2% -> 15%
where the time goes in v2:
time: 137 us; the launch traced here: 136 us
  Pallas kernels  42.5 us (31%)
  starting transfers between devices  34.1 us (25%)
  waiting for transfers between devices  25.2 us (18%)
  other arithmetic  12.5 us (9%)
  blocking collectives  11.3 us (8%)
  local copies, waits for them, and re-layouts  9.05 us (7%)
  between operations  1.61 us (1%)
    all_to_all x3, starting transfers between devices, exchange(): return lax.all_to_all(rows, 'dom', 0, 0, tiled=True)  14.6 us
    ppermute x9, starting transfers between devices, across(): lax.ppermute(value, 'dom', [(p, p ^ step) for p in range(lax.axis_size('d...  13 us
    all_to_all x1, blocking collectives, exchange(): return lax.all_to_all(rows, 'dom', 0, 0, tiled=True)  11.3 us
    pallas_call x1, Pallas kernels, body(): call(functools.partial(second_kernel, shards), small_specs + [ANY] * (3 +...  10.8 us
    pallas_call x1, Pallas kernels, body(): call(functools.partial(third_kernel, shards), small_specs + [VMEM] + [ANY...  9.35 us
    ppermute x9, waiting for transfers between devices, across(): lax.ppermute(value, 'dom', [(p, p ^ step) for p in range(lax.axis_size('d...  9.34 us
    pallas_call x3, Pallas kernels, combine(): call(kernel, [ANY] * len(arrays), [shape(*s) for s in shapes], [ANY] * le...  9.13 us
    ppermute x4, waiting for transfers between devices, across(): return lax.ppermute(value, 'rep', [(0, 1), (1, 0)])  7.87 us
  transfers between devices with their start and end apart: 26, of which 7 were waited for; matrix products, arithmetic and copies ran while one was open for 11% of the time, Pallas kernels for 15%

profile of v2, /device:TPU:0, one launch (start us, length us, event | category | flops | bytes accessed | tf_op | source)
XLA Modules:
  0.0 136.4 jit_solution(10056270847295330887)
XLA Ops:
  1.7 2.5 %shard_map.188 = bf16[128,512]{1,0:T(8,128)(2,1)} custom-call(s32[1,4,16]{2,1,0:T(4,128)} %lists.9, bf16[2,128,512]{2,1,0:T(8,128)(2,1)} %nodes.5), custom_call_target="tpu_custom_call" | custom-call | flops 10000000 | bytes 7000000 | tf_op jit(solution)/shard_map/pallas_call | solution.py:650
  4.2 7.3 %all-to-all-start = ((bf16[8,16,512]{2,1,0:T(8,128)(2,1)}), bf16[8,16,512]{2,1,0:T(8,128)(2,1)S(1)}, u32[]{:S(2)}, u32[]{:S(2)}) async-start(bf16[8,16,512]{2,1,0:T(8,128)(2,1)} %bitcast.26), calls=%async_computation | async-start | bytes 262144 | tf_op jit(solution)/shard_map/all_to_all | solution.py:499
  11.5 0.7 pad_maximum_fusion.g_mine
  12.3 1.3 broadcast_in_dim.24.src
  13.6 1.3 broadcast_in_dim.25.dst
  15.5 3.3 %all-to-all-done = bf16[8,16,512]{2,1,0:T(8,128)(2,1)S(1)} async-done(((bf16[8,16,512]{2,1,0:T(8,128)(2,1)}), bf16[8,16,512]{2,1,0:T(8,128)(2,1)S(1)}, u32[]{:S(2)}, u32[]{:S(2)}) %all-to-all-start) | async-done | bytes 131104 | tf_op jit(solution)/shard_map/all_to_all | solution.py:499
  18.9 0.6 copy-done.7
  19.7 6.8 %shard_map.189 = (bf16[128,512]{1,0:T(8,128)(2,1)}, bf16[384,512]{1,0:T(8,128)(2,1)}, bf16[1664,512]{1,0:T(8,128)(2,1)}, f32[512,128]{1,0:T(8,128)}, bf16[128,512]{1,0:T(8,128)(2,1)}) custom-call(s32[1]{0:T(128)S(6)} %copy.21.count, s32[1,384]{1,0:T(1,128)} %broadcast_in_dim.24.src, s32[1,384]{1,0:T(1,128)} %broadcast_in_dim.25.dst, s32[1,4,16]{2,1,0:T(4,128)} %lists.9, ...), custom_call_target="tpu_custom_call" | custom-call | flops 1100000000 | bytes 26000000 | tf_op jit(solution)/shard_map/pallas_call | solution.py:676
  26.5 11.3 %all_to_all.46 = bf16[8,16,512]{2,1,0:T(8,128)(2,1)} all-to-all(bf16[8,16,512]{2,1,0:T(8,128)(2,1)} %bitcast.31), channel_id=1, replica_groups=mesh['segment'=2,'dom'=8,'rep'=2] {'dom'}, dimensions={0} | all-to-all | bytes 262144 | tf_op jit(solution)/shard_map/all_to_all | solution.py:499
  37.9 10.8 %shard_map.190 = (bf16[128,512]{1,0:T(8,128)(2,1)}, bf16[384,512]{1,0:T(8,128)(2,1)}, f32[16,512]{1,0:T(8,128)}, f32[128,512]{1,0:T(8,128)}, bf16[384,512]{1,0:T...) custom-call(s32[1]{0:T(128)S(6)} %copy.21.count, ...), custom_call_target="tpu_custom_call" | custom-call | flops 2800000000 | bytes 44000000 | tf_op jit(solution)/shard_map/pallas_call | solution.py:716
  48.8 4.0 %all-to-all-start.2 = ((bf16[8,16,512]{2,1,0:T(8,128)(2,1)}), bf16[8,16,512]{2,1,0:T(8,128)(2,1)}, u32[]{:S(2)}, u32[]{:S(2)}) async-start(bf16[8,16,512]{2,1,0:T(8,128)(2,1)} %bitcast.29), calls=%async_computation.2 | async-start | bytes 262144 | tf_op jit(solution)/shard_map/all_to_all | solution.py:499
  52.8 2.4 %add_convert_fusion = bf16[512,512]{1,0:T(8,128)(2,1)} fusion(bf16[1808,512]{1,0:T(8,128)(2,1)S(1)} %collective-permute-done.5.refs_1_.refs_5_.refs_7_, bf16[1808,512]{1,0:T(8,128)(2,1)} %get-tuple-element.55.refs_0_.refs_4_.refs_6_), kind=kLoop, calls=%fused_computation | loop fusion | flops 1048576 | bytes 1572864 | tf_op jit(solution)/shard_map/convert_element_type | solution.py:606
  55.2 1.9 %collective-permute-start.7 = (bf16[512,512]{1,0:T(8,128)(2,1)}, bf16[512,512]{1,0:T(8,128)(2,1)S(1)}, u32[]{:S(2)}, u32[]{:S(2)}) collective-permute-start(bf16[512,512]{1,0:T(8,128)(2,1)} %add_convert_fusion), channel_id=1, source_target_pairs={{0,2},{2,0},{4,6},{6,4},{8,10},{10,8},{12,14},{14,12},{1,3},{3,1},... | collective-permute-start | bytes 1572872 | tf_op jit(solution)/shard_map/ppermute | solution.py:510
  57.1 1.8 %add_convert_fusion.1 = bf16[384,512]{1,0:T(8,128)(2,1)} fusion(bf16[1808,512]{1,0:T(8,128)(2,1)S(1)} %collective-permute-done.5.refs_1_.refs_5_.refs_7_, bf16[1808,512]{1,0:T(8,128)(2,1)} %get-tuple-element.55.refs_0_.refs_4_.refs_6_), kind=kLoop, calls=%fused_computation.2 | loop fusion | flops 786432 | bytes 1179648 | tf_op jit(solution)/shard_map/convert_element_type | solution.py:606
  58.9 1.5 %collective-permute-start.6 = (bf16[384,512]{1,0:T(8,128)(2,1)}, bf16[384,512]{1,0:T(8,128)(2,1)S(1)}, u32[]{:S(2)}, u32[]{:S(2)}) collective-permute-start(bf16[384,512]{1,0:T(8,128)(2,1)} %add_convert_fusion.1), channel_id=1, source_target_pairs={{0,1},{1,0},{2,3},{3,2},{4,5},{5,4},{6,7},{7,6},{8,9},{9,8},{10,11... | collective-permute-start | bytes 1179656 | tf_op jit(solution)/shard_map/ppermute | solution.py:508
  60.8 9.4 %shard_map.191 = (f32[128,512]{1,0:T(8,128)}, bf16[384,512]{1,0:T(8,128)(2,1)}, bf16[128,512]{1,0:T(8,128)(2,1)}, bf16[1808,512]{1,0:T(8,128)(2,1)}, bf16[1808,512]{1,0:T(8,128)(2,1)}) custom-call(s32[1]{0:T(128)S(6)} %copy.21.count, s32[1,384]{1,0:T(1,128)} %broadcast_in_dim.24.src, s32[1,384]{1,0:T(1,128)} %broadcast_in_dim.25.dst, s32[1,4,16]{2,1,0:T(4,128)} %lists.9, ...), custom_call_target="tpu_custom_call" | custom-call | flops 1800000000 | bytes 37000000 | tf_op jit(solution)/shard_map/pallas_call | solution.py:734
  70.3 4.1 %collective-permute-done.8.refs_5_.refs_1_ = bf16[1808,512]{1,0:T(8,128)(2,1)} collective-permute-done((bf16[1808,512]{1,0:T(8,128)(2,1)}, bf16[1808,512]{1,0:T(8,128)(2,1)}, u32[]{:S(2)}, u32[]{:S(2)}) %collective-permute-start.8) | collective-permute-done | bytes 1851424 | tf_op jit(solution)/shard_map/ppermute | solution.py:503
  74.5 3.0 %shard_map.192 = (bf16[448,512]{1,0:T(8,128)(2,1)}, bf16[512,512]{1,0:T(8,128)(2,1)}, bf16[400,512]{1,0:T(8,128)(2,1)}) custom-call(bf16[1808,512]{1,0:T(8,128)(2,1)} %get-tuple-element.55.refs_0_.refs_4_.refs_6_, bf16[1808,512]{1,0:T(8,128)(2,1)} %copy-done, bf16[384,512]{1,0:T(8,128)(2,1)} %copy-done.2, bf16[512,512]{1,0:T(8,128)(2,1)} %copy-done.1, ...), custom_call_target="tpu_custom_call" | custom-call | flops 1000000 | bytes 8000000 | tf_op jit(solution)/shard_map/pallas_call | solution.py:589
  77.5 1.2 collective-permute-start.9
  78.7 1.5 %collective-permute-start.11 = (bf16[448,512]{1,0:T(8,128)(2,1)}, bf16[448,512]{1,0:T(8,128)(2,1)S(1)}, u32[]{:S(2)}, u32[]{:S(2)}) collective-permute-start(bf16[448,512]{1,0:T(8,128)(2,1)} %get-tuple-element.65), channel_id=1, source_target_pairs={{0,4},{2,6},{4,0},{6,2},{8,12},{10,14},{12,8},{14,10},{1,5},{3,7},... | collective-permute-start | bytes 1376264 | tf_op jit(solution)/shard_map/ppermute | solution.py:510
  80.2 1.5 %collective-permute-start.10 = (bf16[400,512]{1,0:T(8,128)(2,1)}, bf16[400,512]{1,0:T(8,128)(2,1)S(1)}, u32[]{:S(2)}, u32[]{:S(2)}) collective-permute-start(bf16[400,512]{1,0:T(8,128)(2,1)} %get-tuple-element.64), channel_id=1, source_target_pairs={{0,1},{1,0},{2,3},{3,2},{4,5},{5,4},{6,7},{7,6},{8,9},{9,8},{10,11... | collective-permute-start | bytes 1228808 | tf_op jit(solution)/shard_map/ppermute | solution.py:508
  81.7 1.8 %broadcast_select_fusion = bf16[384,512]{1,0:T(8,128)(2,1)} fusion(bf16[384,512]{1,0:T(8,128)(2,1)} %get-tuple-element.76, bf16[384,512]{1,0:T(8,128)(2,1)} %get-tuple-element.75, pred[]{:T(512)S(6)} %eq.3), kind=kLoop, calls=%fused_computation.5 | loop fusion | flops 196608 | bytes 1179649 | tf_op jit(solution)/shard_map/jit(_where)/select_n | solution.py:803
  83.5 7.9 %collective-permute-done.10.refs_3_.refs_2_ = bf16[400,512]{1,0:T(8,128)(2,1)S(1)} collective-permute-done((bf16[400,512]{1,0:T(8,128)(2,1)}, bf16[400,512]{1,0:T(8,128)(2,1)S(1)}, u32[]{:S(2)}, u32[]{:S(2)}) %collective-permute-start.10) | collective-permute-done | bytes 409632 | tf_op jit(solution)/shard_map/ppermute | solution.py:508
  91.4 0.8 copy-done.6
  92.1 0.8 copy-done.5
  92.9 0.9 copy-done.3
  93.8 2.5 %shard_map.193 = (bf16[256,512]{1,0:T(8,128)(2,1)}, bf16[208,512]{1,0:T(8,128)(2,1)}, bf16[224,512]{1,0:T(8,128)(2,1)}) custom-call(bf16[1808,512]{1,0:T(8,128)(2,1)} %get-tuple-element.60.refs_4_.refs_0_, bf16[1808,512]{1,0:T(8,128)(2,1)} %collective-permute-done.8.refs_5_.refs_1_, bf16[512,512]{1,0:T(8,128)(2,1)} %copy-done.3, bf16[400,512]{1,0:T(8,128)(2,1)} %copy-done.6, ...), custom_call_target="tpu_custom_call" | custom-call | flops 1000000 | bytes 8000000 | tf_op jit(solution)/shard_map/pallas_call | solution.py:589
  96.3 1.6 %collective-permute-start.13 = (bf16[256,512]{1,0:T(8,128)(2,1)}, bf16[256,512]{1,0:T(8,128)(2,1)S(1)}, u32[]{:S(2)}, u32[]{:S(2)}) collective-permute-start(bf16[256,512]{1,0:T(8,128)(2,1)} %get-tuple-element.66), channel_id=1, source_target_pairs={{0,1},{1,0},{2,3},{3,2},{4,5},{5,4},{6,7},{7,6},{8,9},{9,8},{10,11... | collective-permute-start | bytes 786440 | tf_op jit(solution)/shard_map/ppermute | solution.py:508
  97.9 2.2 %collective-permute-start.14 = (bf16[224,512]{1,0:T(8,128)(2,1)}, bf16[224,512]{1,0:T(8,128)(2,1)S(1)}, u32[]{:S(2)}, u32[]{:S(2)}) collective-permute-start(bf16[224,512]{1,0:T(8,128)(2,1)} %get-tuple-element.68), channel_id=1, source_target_pairs={{0,8},{2,10},{4,12},{6,14},{8,0},{10,2},{12,4},{14,6},{1,9},{3,11}... | collective-permute-start | bytes 688136 | tf_op jit(solution)/shard_map/ppermute | solution.py:510
  100.1 0.8 collective-permute-start.12
  100.9 3.4 %all-to-all-start.3 = ((bf16[8,16,512]{2,1,0:T(8,128)(2,1)}), bf16[8,16,512]{2,1,0:T(8,128)(2,1)S(1)}, u32[]{:S(2)}, u32[]{:S(2)}) async-start(bf16[8,16,512]{2,1,0:T(8,128)(2,1)} %bitcast.28), calls=%async_computation.3 | async-start | bytes 262144 | tf_op jit(solution)/shard_map/all_to_all | solution.py:499
  104.3 1.2 select_bitcast_fusion.1
  105.5 0.9 maximum_bitcast_fusion
  106.5 5.2 %collective-permute-done.14.refs_10_ = bf16[224,512]{1,0:T(8,128)(2,1)S(1)} collective-permute-done((bf16[224,512]{1,0:T(8,128)(2,1)}, bf16[224,512]{1,0:T(8,128)(2,1)S(1)}, u32[]{:S(2)}, u32[]{:S(2)}) %collective-permute-start.14) | collective-permute-done | bytes 229408 | tf_op jit(solution)/shard_map/ppermute | solution.py:510
  111.7 0.7 copy-done.12
  112.4 0.7 copy-done.11
  113.1 3.6 %shard_map.194 = (bf16[128,512]{1,0:T(8,128)(2,1)}, bf16[128,512]{1,0:T(8,128)(2,1)}, bf16[128,512]{1,0:T(8,128)(2,1)}, bf16[48,512]{1,0:T(8,128)(2,1)}, bf16[64,512]{1,0:T(8,128)(2,1)}, /*index=5*/f32[240,512]{1,0:T(8,128)}) custom-call(bf16[1808,512]{1,0:T(8,128)(2,1)} %get-tuple-element.60.refs_4_.refs_0_, ...), custom_call_target="tpu_custom_call" | custom-call | flops 1000000 | bytes 8000000 | tf_op jit(solution)/shard_map/pallas_call | solution.py:589
  116.8 3.3 %collective-permute-start.20 = (bf16[128,512]{1,0:T(8,128)(2,1)}, bf16[128,512]{1,0:T(8,128)(2,1)S(1)}, u32[]{:S(2)}, u32[]{:S(2)}) collective-permute-start(bf16[128,512]{1,0:T(8,128)(2,1)} %get-tuple-element.71), channel_id=1, source_target_pairs={{0,8},{2,10},{4,12},{6,14},{8,0},{10,2},{12,4},{14,6},{1,9},{3,11}... | collective-permute-start | bytes 393224 | tf_op jit(solution)/shard_map/ppermute | solution.py:510
  120.1 1.1 collective-permute-start.21
  121.7 0.9 collective-permute-start.17
  122.6 0.7 copy-done.10
  123.3 1.9 %shard_map.195 = bf16[128,512]{1,0:T(8,128)(2,1)} custom-call(s32[1,4,16]{2,1,0:T(4,128)} %lists.9, f32[128,512]{1,0:T(8,128)} %get-tuple-element.58.d_own, bf16[128,512]{1,0:T(8,128)(2,1)} %bitcast.27), custom_call_target="tpu_custom_call" | custom-call | flops 10000000 | bytes 7000000 | tf_op jit(solution)/shard_map/pallas_call | solution.py:792
  125.3 4.1 %collective-permute-done.20 = bf16[128,512]{1,0:T(8,128)(2,1)S(1)} collective-permute-done((bf16[128,512]{1,0:T(8,128)(2,1)}, bf16[128,512]{1,0:T(8,128)(2,1)S(1)}, u32[]{:S(2)}, u32[]{:S(2)}) %collective-permute-start.20) | collective-permute-done | bytes 131104 | tf_op jit(solution)/shard_map/ppermute | solution.py:510
  129.4 1.0 convert_add_fusion
  130.5 1.8 %broadcast_select_fusion.2 = (f32[112,512]{1,0:T(8,128)S(1)}, f32[112,512]{1,0:T(8,128)}, f32[112,512]{1,0:T(8,128)}) fusion(pred[]{:T(512)S(6)} %eq.3, f32[128,512]{1,0:T(8,128)S(1)} %convert_add_fusion, bf16[64,512]{1,0:T(8,128)(2,1)S(1)} %collective-permute-done.18, bf16[48,512]{1,0:T(8,128)(2,1)S(1)} %collective-permute-done.17, ...), kind=kLoop, calls=%fused_computation.12 | loop fusion | flops 344064 | bytes 1261569 | tf_op jit(solution)/shard_map/jit(_where)/select_n | solution.py:809
  132.3 0.7 maximum_bitcast_fusion.1
  133.7 0.7 copy-done.13
  134.4 1.9 %shard_map.196 = (f32[96,512]{1,0:T(8,128)}, f32[32,512]{1,0:T(8,128)}, f32[64,512]{1,0:T(8,128)}, f32[32,512]{1,0:T(8,128)}) custom-call(f32[112,512]{1,0:T(8,128)} %copy-done.13, f32[112,512]{1,0:T(8,128)} %get-tuple-element.85.one, f32[112,512]{1,0:T(8,128)} %get-tuple-element.88.zero), custom_call_target="tpu_custom_call" | custom-call | flops 1000000 | bytes 7000000 | tf_op jit(solution)/shard_map/pallas_call | solution.py:826
  (64 shorter events, 3.5 us)
Async XLA Ops:
  0.6 18.2 %collective-permute-start.1 = (bf16[1,1536,512]{2,1,0:T(8,128)(2,1)}, bf16[1,1536,512]{2,1,0:T(8,128)(2,1)}, u32[]{:S(2)}, u32[]{:S(2)}) collective-permute-start(bf16[1,1536,512]{2,1,0:T(8,128)(2,1)} %rest_2_.5), channel_id=1, source_target_pairs={{0,16},{16,0},{1,17},{17,1},{2,18},{18,2},{3,19},{19,3},{4,20},{20... | collective-permute-start | bytes 4718600 | tf_op jit(solution)/shard_map/ppermute | solution.py:503
  1.1 17.7 %collective-permute-start.3 = (bf16[1,1024,512]{2,1,0:T(8,128)(2,1)}, bf16[1,1024,512]{2,1,0:T(8,128)(2,1)}, u32[]{:S(2)}, u32[]{:S(2)}) collective-permute-start(bf16[1,1024,512]{2,1,0:T(8,128)(2,1)} %rest_4_.5), channel_id=1, source_target_pairs={{0,16},{16,0},{1,17},{17,1},{2,18},{18,2},{3,19},{19,3},{4,20},{20... | collective-permute-start | bytes 3145736 | tf_op jit(solution)/shard_map/ppermute | solution.py:503
  1.2 17.6 %collective-permute-start.2 = (bf16[1,512,512]{2,1,0:T(8,128)(2,1)}, bf16[1,512,512]{2,1,0:T(8,128)(2,1)S(1)}, u32[]{:S(2)}, u32[]{:S(2)}) collective-permute-start(bf16[1,512,512]{2,1,0:T(8,128)(2,1)} %rest_3_.5), channel_id=1, source_target_pairs={{0,16},{16,0},{1,17},{17,1},{2,18},{18,2},{3,19},{19,3},{4,20},{20... | collective-permute-start | bytes 1572872 | tf_op jit(solution)/shard_map/ppermute | solution.py:503
  1.7 17.2 %collective-permute-start.4 = (bf16[1,512,512]{2,1,0:T(8,128)(2,1)}, bf16[1,512,512]{2,1,0:T(8,128)(2,1)}, u32[]{:S(2)}, u32[]{:S(2)}) collective-permute-start(bf16[1,512,512]{2,1,0:T(8,128)(2,1)} %rest_5_.1), channel_id=1, source_target_pairs={{0,16},{16,0},{1,17},{17,1},{2,18},{18,2},{3,19},{19,3},{4,20},{20... | collective-permute-start | bytes 1572872 | tf_op jit(solution)/shard_map/ppermute | solution.py:503
  4.2 14.6 %all-to-all-start = ((bf16[8,16,512]{2,1,0:T(8,128)(2,1)}), bf16[8,16,512]{2,1,0:T(8,128)(2,1)S(1)}, u32[]{:S(2)}, u32[]{:S(2)}) async-start(bf16[8,16,512]{2,1,0:T(8,128)(2,1)} %bitcast.26), calls=%async_computation | async-start | bytes 262144 | tf_op jit(solution)/shard_map/all_to_all | solution.py:499
  12.2 6.7 %copy-start.15 = (f32[2,512]{1,0:T(2,128)}, f32[2,512]{1,0:T(2,128)S(1)}, u32[]{:S(2)}) copy-start(f32[2,512]{1,0:T(2,128)S(1)} %pad_maximum_fusion.g_mine) | copy-start | bytes 12292
  12.2 3.3 %collective-permute-start = (f32[2,512]{1,0:T(2,128)S(1)}, f32[2,512]{1,0:T(2,128)S(1)}, u32[]{:S(2)}, u32[]{:S(2)}) collective-permute-start(f32[2,512]{1,0:T(2,128)S(1)} %pad_maximum_fusion.g_mine), channel_id=1, source_target_pairs={{0,16},{16,0},{1,17},{17,1},{2,18},{18,2},{3,19},{19,3},{4,20},{20... | collective-permute-start | bytes 12296 | tf_op jit(solution)/shard_map/ppermute | solution.py:503
  15.5 3.4 %copy-start.16 = (f32[2,512]{1,0:T(2,128)}, f32[2,512]{1,0:T(2,128)S(1)}, u32[]{:S(2)}) copy-start(f32[2,512]{1,0:T(2,128)S(1)} %collective-permute-done.g_other) | copy-start | bytes 12292
  18.9 0.7 copy-start.7
  18.9 0.8 copy-start.4
  48.7 4.1 %collective-permute-start.5 = (bf16[1808,512]{1,0:T(8,128)(2,1)}, bf16[1808,512]{1,0:T(8,128)(2,1)S(1)}, u32[]{:S(2)}, u32[]{:S(2)}) collective-permute-start(bf16[1808,512]{1,0:T(8,128)(2,1)} %get-tuple-element.56), channel_id=1, source_target_pairs={{0,16},{16,0},{1,17},{17,1},{2,18},{18,2},{3,19},{19,3},{4,20},{20... | collective-permute-start | bytes 5554184 | tf_op jit(solution)/shard_map/ppermute | solution.py:503
  48.8 12.1 %all-to-all-start.2 = ((bf16[8,16,512]{2,1,0:T(8,128)(2,1)}), bf16[8,16,512]{2,1,0:T(8,128)(2,1)}, u32[]{:S(2)}, u32[]{:S(2)}) async-start(bf16[8,16,512]{2,1,0:T(8,128)(2,1)} %bitcast.29), calls=%async_computation.2 | async-start | bytes 262144 | tf_op jit(solution)/shard_map/all_to_all | solution.py:499
  52.8 4.3 %copy-start = (bf16[1808,512]{1,0:T(8,128)(2,1)}, bf16[1808,512]{1,0:T(8,128)(2,1)S(1)}, u32[]{:S(2)}) copy-start(bf16[1808,512]{1,0:T(8,128)(2,1)S(1)} %collective-permute-done.5.refs_1_.refs_5_.refs_7_) | copy-start | bytes 5554180
  55.2 15.0 %collective-permute-start.7 = (bf16[512,512]{1,0:T(8,128)(2,1)}, bf16[512,512]{1,0:T(8,128)(2,1)S(1)}, u32[]{:S(2)}, u32[]{:S(2)}) collective-permute-start(bf16[512,512]{1,0:T(8,128)(2,1)} %add_convert_fusion), channel_id=1, source_target_pairs={{0,2},{2,0},{4,6},{6,4},{8,10},{10,8},{12,14},{14,12},{1,3},{3,1},... | collective-permute-start | bytes 1572872 | tf_op jit(solution)/shard_map/ppermute | solution.py:510
  58.9 11.3 %collective-permute-start.6 = (bf16[384,512]{1,0:T(8,128)(2,1)}, bf16[384,512]{1,0:T(8,128)(2,1)S(1)}, u32[]{:S(2)}, u32[]{:S(2)}) collective-permute-start(bf16[384,512]{1,0:T(8,128)(2,1)} %add_convert_fusion.1), channel_id=1, source_target_pairs={{0,1},{1,0},{2,3},{3,2},{4,5},{5,4},{6,7},{7,6},{8,9},{9,8},{10,11... | collective-permute-start | bytes 1179656 | tf_op jit(solution)/shard_map/ppermute | solution.py:508
  70.2 4.2 %copy-start.2 = (bf16[384,512]{1,0:T(8,128)(2,1)}, bf16[384,512]{1,0:T(8,128)(2,1)S(1)}, u32[]{:S(2)}) copy-start(bf16[384,512]{1,0:T(8,128)(2,1)S(1)} %collective-permute-done.6.refs_2_.refs_6_.refs_8_) | copy-start | bytes 1179652
  70.2 4.2 %copy-start.1 = (bf16[512,512]{1,0:T(8,128)(2,1)}, bf16[512,512]{1,0:T(8,128)(2,1)S(1)}, u32[]{:S(2)}) copy-start(bf16[512,512]{1,0:T(8,128)(2,1)S(1)} %collective-permute-done.7.refs_3_.refs_8_.refs_11_) | copy-start | bytes 1572868
  70.2 4.2 %collective-permute-start.8 = (bf16[1808,512]{1,0:T(8,128)(2,1)}, bf16[1808,512]{1,0:T(8,128)(2,1)}, u32[]{:S(2)}, u32[]{:S(2)}) collective-permute-start(bf16[1808,512]{1,0:T(8,128)(2,1)} %get-tuple-element.62), channel_id=1, source_target_pairs={{0,16},{16,0},{1,17},{17,1},{2,18},{18,2},{3,19},{19,3},{4,20},{20... | collective-permute-start | bytes 5554184 | tf_op jit(solution)/shard_map/ppermute | solution.py:503
  77.5 14.7 %collective-permute-start.9 = (bf16[512,512]{1,0:T(8,128)(2,1)}, bf16[512,512]{1,0:T(8,128)(2,1)S(1)}, u32[]{:S(2)}, u32[]{:S(2)}) collective-permute-start(bf16[512,512]{1,0:T(8,128)(2,1)} %get-tuple-element.63), channel_id=1, source_target_pairs={{0,2},{2,0},{4,6},{6,4},{8,10},{10,8},{12,14},{14,12},{1,3},{3,1},... | collective-permute-start | bytes 1572872 | tf_op jit(solution)/shard_map/ppermute | solution.py:510
  78.7 12.7 %collective-permute-start.11 = (bf16[448,512]{1,0:T(8,128)(2,1)}, bf16[448,512]{1,0:T(8,128)(2,1)S(1)}, u32[]{:S(2)}, u32[]{:S(2)}) collective-permute-start(bf16[448,512]{1,0:T(8,128)(2,1)} %get-tuple-element.65), channel_id=1, source_target_pairs={{0,4},{2,6},{4,0},{6,2},{8,12},{10,14},{12,8},{14,10},{1,5},{3,7},... | collective-permute-start | bytes 1376264 | tf_op jit(solution)/shard_map/ppermute | solution.py:510
  80.2 11.2 %collective-permute-start.10 = (bf16[400,512]{1,0:T(8,128)(2,1)}, bf16[400,512]{1,0:T(8,128)(2,1)S(1)}, u32[]{:S(2)}, u32[]{:S(2)}) collective-permute-start(bf16[400,512]{1,0:T(8,128)(2,1)} %get-tuple-element.64), channel_id=1, source_target_pairs={{0,1},{1,0},{2,3},{3,2},{4,5},{5,4},{6,7},{7,6},{8,9},{9,8},{10,11... | collective-permute-start | bytes 1228808 | tf_op jit(solution)/shard_map/ppermute | solution.py:508
  83.5 20.8 %collective-permute-start.16 = (bf16[384,512]{1,0:T(8,128)(2,1)}, bf16[384,512]{1,0:T(8,128)(2,1)}, u32[]{:S(2)}, u32[]{:S(2)}) collective-permute-start(bf16[384,512]{1,0:T(8,128)(2,1)} %broadcast_select_fusion), channel_id=1, source_target_pairs={{0,16},{16,0},{1,17},{17,1},{2,18},{18,2},{3,19},{19,3},{4,20},{20... | collective-permute-start | bytes 1179656 | tf_op jit(solution)/shard_map/ppermute | solution.py:503
  91.4 0.8 copy-start.6
  92.1 0.8 copy-start.5
  92.9 0.9 copy-start.3
  96.3 15.4 %collective-permute-start.13 = (bf16[256,512]{1,0:T(8,128)(2,1)}, bf16[256,512]{1,0:T(8,128)(2,1)S(1)}, u32[]{:S(2)}, u32[]{:S(2)}) collective-permute-start(bf16[256,512]{1,0:T(8,128)(2,1)} %get-tuple-element.66), channel_id=1, source_target_pairs={{0,1},{1,0},{2,3},{3,2},{4,5},{5,4},{6,7},{7,6},{8,9},{9,8},{10,11... | collective-permute-start | bytes 786440 | tf_op jit(solution)/shard_map/ppermute | solution.py:508
  97.9 13.8 %collective-permute-start.14 = (bf16[224,512]{1,0:T(8,128)(2,1)}, bf16[224,512]{1,0:T(8,128)(2,1)S(1)}, u32[]{:S(2)}, u32[]{:S(2)}) collective-permute-start(bf16[224,512]{1,0:T(8,128)(2,1)} %get-tuple-element.68), channel_id=1, source_target_pairs={{0,8},{2,10},{4,12},{6,14},{8,0},{10,2},{12,4},{14,6},{1,9},{3,11}... | collective-permute-start | bytes 688136 | tf_op jit(solution)/shard_map/ppermute | solution.py:510
  100.1 6.4 %collective-permute-start.12 = (bf16[208,512]{1,0:T(8,128)(2,1)}, bf16[208,512]{1,0:T(8,128)(2,1)S(1)}, u32[]{:S(2)}, u32[]{:S(2)}) collective-permute-start(bf16[208,512]{1,0:T(8,128)(2,1)} %get-tuple-element.67), channel_id=1, source_target_pairs={{0,2},{2,0},{4,6},{6,4},{8,10},{10,8},{12,14},{14,12},{1,3},{3,1},... | collective-permute-start | bytes 638984 | tf_op jit(solution)/shard_map/ppermute | solution.py:510
  100.9 21.7 %all-to-all-start.3 = ((bf16[8,16,512]{2,1,0:T(8,128)(2,1)}), bf16[8,16,512]{2,1,0:T(8,128)(2,1)S(1)}, u32[]{:S(2)}, u32[]{:S(2)}) async-start(bf16[8,16,512]{2,1,0:T(8,128)(2,1)} %bitcast.28), calls=%async_computation.3 | async-start | bytes 262144 | tf_op jit(solution)/shard_map/all_to_all | solution.py:499
  106.5 18.8 %copy-start.9 = (bf16[128,512]{1,0:T(8,128)(2,1)S(1)}, bf16[128,512]{1,0:T(8,128)(2,1)}, u32[]{:S(2)}) copy-start(bf16[128,512]{1,0:T(8,128)(2,1)} %get-tuple-element.74) | copy-start | bytes 393220
  106.5 5.2 %copy-start.14 = (bf16[208,512]{1,0:T(8,128)(2,1)}, bf16[208,512]{1,0:T(8,128)(2,1)S(1)}, u32[]{:S(2)}) copy-start(bf16[208,512]{1,0:T(8,128)(2,1)S(1)} %collective-permute-done.12.refs_3_) | copy-start | bytes 638980
  111.7 0.7 copy-start.12
  112.4 0.7 copy-start.11
  116.7 8.5 %collective-permute-start.19 = (bf16[128,512]{1,0:T(8,128)(2,1)}, bf16[128,512]{1,0:T(8,128)(2,1)S(1)}, u32[]{:S(2)}, u32[]{:S(2)}) collective-permute-start(bf16[128,512]{1,0:T(8,128)(2,1)} %get-tuple-element.70), channel_id=1, source_target_pairs={{0,4},{2,6},{4,0},{6,2},{8,12},{10,14},{12,8},{14,10},{1,5},{3,7},... | collective-permute-start | bytes 393224 | tf_op jit(solution)/shard_map/ppermute | solution.py:510
  116.8 12.6 %collective-permute-start.20 = (bf16[128,512]{1,0:T(8,128)(2,1)}, bf16[128,512]{1,0:T(8,128)(2,1)S(1)}, u32[]{:S(2)}, u32[]{:S(2)}) collective-permute-start(bf16[128,512]{1,0:T(8,128)(2,1)} %get-tuple-element.71), channel_id=1, source_target_pairs={{0,8},{2,10},{4,12},{6,14},{8,0},{10,2},{12,4},{14,6},{1,9},{3,11}... | collective-permute-start | bytes 393224 | tf_op jit(solution)/shard_map/ppermute | solution.py:510
  120.1 9.3 %collective-permute-start.21 = (bf16[128,512]{1,0:T(8,128)(2,1)}, bf16[128,512]{1,0:T(8,128)(2,1)S(1)}, u32[]{:S(2)}, u32[]{:S(2)}) collective-permute-start(bf16[128,512]{1,0:T(8,128)(2,1)} %get-tuple-element.72), channel_id=1, source_target_pairs={{0,12},{2,14},{4,8},{6,10},{8,4},{10,6},{12,0},{14,2},{1,13},{3,15... | collective-permute-start | bytes 393224 | tf_op jit(solution)/shard_map/ppermute | solution.py:510
  121.2 9.3 %collective-permute-start.18 = (bf16[64,512]{1,0:T(8,128)(2,1)}, bf16[64,512]{1,0:T(8,128)(2,1)S(1)}, u32[]{:S(2)}, u32[]{:S(2)}) collective-permute-start(bf16[64,512]{1,0:T(8,128)(2,1)} %get-tuple-element.79), channel_id=1, source_target_pairs={{0,1},{1,0},{2,3},{3,2},{4,5},{5,4},{6,7},{7,6},{8,9},{9,8},{10,11... | collective-permute-start | bytes 196616 | tf_op jit(solution)/shard_map/ppermute | solution.py:508
  121.7 8.7 %collective-permute-start.17 = (bf16[48,512]{1,0:T(8,128)(2,1)}, bf16[48,512]{1,0:T(8,128)(2,1)S(1)}, u32[]{:S(2)}, u32[]{:S(2)}) collective-permute-start(bf16[48,512]{1,0:T(8,128)(2,1)} %get-tuple-element.78), channel_id=1, source_target_pairs={{0,2},{2,0},{4,6},{6,4},{8,10},{10,8},{12,14},{14,12},{1,3},{3,1},... | collective-permute-start | bytes 147464 | tf_op jit(solution)/shard_map/ppermute | solution.py:510
  122.6 0.7 copy-start.10
  125.2 7.1 %copy-start.8 = (bf16[128,512]{1,0:T(8,128)(2,1)S(1)}, bf16[128,512]{1,0:T(8,128)(2,1)}, u32[]{:S(2)}) copy-start(bf16[128,512]{1,0:T(8,128)(2,1)} %shard_map.195) | copy-start | bytes 393220
  125.2 7.0 %collective-permute-start.15 = (bf16[128,512]{1,0:T(8,128)(2,1)S(1)}, bf16[128,512]{1,0:T(8,128)(2,1)S(1)}, u32[]{:S(2)}, u32[]{:S(2)}) collective-permute-start(bf16[128,512]{1,0:T(8,128)(2,1)S(1)} %broadcast_select_fusion.1), channel_id=1, source_target_pairs={{0,16},{16,0},{1,17},{17,1},{2,18},{18,2},{3,19},{19,3},{4,20},{20... | collective-permute-start | bytes 393224 | tf_op jit(solution)/shard_map/ppermute | solution.py:503
  132.2 1.5 %collective-permute-start.22 = (f32[112,512]{1,0:T(8,128)S(1)}, f32[112,512]{1,0:T(8,128)S(1)}, u32[]{:S(2)}, u32[]{:S(2)}) collective-permute-start(f32[112,512]{1,0:T(8,128)S(1)} %get-tuple-element.84), channel_id=1, source_target_pairs={{0,16},{16,0},{1,17},{17,1},{2,18},{18,2},{3,19},{19,3},{4,20},{20... | collective-permute-start | bytes 688136 | tf_op jit(solution)/shard_map/ppermute | solution.py:503
  133.7 0.7 copy-start.13

commit v3 on v2

--- a/solution.py
+++ b/solution.py
@@ -18,6 +18,7 @@
 F32 = jnp.float32
 GAINS = 16
 VMEM_LIMIT = 63 * 1024 * 1024
+SMALL_LIMIT = 62 * 1024 * 1024
 
 ROWS = {"ein": 3 * D, "eout": D, "nin": 2 * D, "nout": D}
 GROUPS = {"node": ("nin", "nout"), "edge": ("ein", "eout")}
@@ -69,7 +70,7 @@
     return rate * (scaled - first - hat * second)
 
 
-def forward(own, edges, table, src, dst, count, weights, waits, gains, res):
+def forward(own, edges, table, src, dst, count, weights, waits, gains, res, edges_done):
     w_ein, w_eout, w_nin, w_nout = weights
     g_edge, g_node = gains
     rows = edges.shape[0]
@@ -95,6 +96,7 @@
         res["edge_hat"][part] = hat.astype(BF)
         res["edge_rate"][part] = jnp.broadcast_to(rate, (CHUNK, 128))
     agg = mm(incidence(dst, count), res["edge_new"][...]).astype(BF)
+    edges_done()
     waits[2]()
     waits[3]()
     pre = mm(own[...], w_nin[:D]) + mm(agg, w_nin[D:])
@@ -155,7 +157,7 @@
 
 def backward(
     cot_node, cot_edge, own, edges, table, src, dst, count, weights, gains, res, core, me, layout, sequence,
-    store, outs, work, ready,
+    store, outs, work, ready, arrive,
 ):
     w_ein, w_eout, w_nin, w_nout = weights
     g_edge, g_node = gains
@@ -182,6 +184,7 @@
     d_own = cot_node + mm_t(d_pre_node, w_nin[:D])
     d_agg = mm_t(d_pre_node, w_nin[D:]).astype(BF)
 
+    arrive()
     joins = incidence(dst, count)
     gain_edge = jnp.zeros((1, D), F32)
     for at in range(0, rows, CHUNK):
@@ -349,13 +352,22 @@
     for copy in coming:
         copy.wait()
     fill_halo(table, room)
+    tall = 3 * edges.shape[0]
+
+    def edges_done():
+        copies.send(edge_new, edge_out)
+        copies.send(saved.at[:tall], saved_out.at[:tall])
+
     forward(
-        own, edges, table, src, dst, count[0], held, waits, (gains[:1], gains[1:2]), res
+        own, edges, table, src, dst, count[0], held, waits, (gains[:1], gains[1:2]), res,
+        edges_done,
     )
     place(1, pick(one_hots(lists), node_new[...]), room)
-    for source, target in zip(
-        (room, node_new, edge_new, saved, rates),
-        (sent, node_out, edge_out, saved_out, rate_out),
+    for source, target in (
+        (room, sent),
+        (node_new, node_out),
+        (saved.at[tall:], saved_out.at[tall:]),
+        (rates, rate_out),
     ):
         copies.send(source, target)
     copies.finish()
@@ -403,9 +415,11 @@
     for copy in coming:
         copy.wait()
     fill_halo(table, room)
-    forward(own, edges, table, src, dst, count[0], held, waits, gains, res)
+    forward(
+        own, edges, table, src, dst, count[0], held, waits, gains, res,
+        lambda: copies.send(edge_new, edge_out),
+    )
     copies.send(node_new, node_out)
-    copies.send(edge_new, edge_out)
     cot_copy.wait()
     ready, finish = back_outs(copies, layout, store, outs, (*work, room))
 
@@ -416,7 +430,7 @@
 
     backward(
         cot[...].astype(F32), None, own, edges, table, src, dst, count[0], held, gains, res,
-        core, me, layout, SEQUENCE[1], store, (*work[:2], room, put_gains), (d_outer, d_pre), ready,
+        core, me, layout, SEQUENCE[1], store, (*work[:2], room, put_gains), (d_outer, d_pre), ready, lambda: None,
     )
     finish()
 
@@ -434,12 +448,17 @@
     core, me = lax.axis_index("segment"), shard_number(shards)
     own = table.at[:NODE_DEV]
     copies = Copies(sems)
-    coming = [copies.start(back, got)]
-    coming += [copies.start(d_own_in, cot_own), copies.start(rate_in, rates)]
-    coming += [copies.start(saved_in, saved), copies.start(nodes.at[core], own)]
-    coming += [copies.start(halo, room)]
-    waits = copies.either(core == 0, first_rows(mine), first_rows(other), held)
-    coming += [copies.start(d_edges_in, cot_edge), copies.start(latents.at[core], edges)]
+    tall = 3 * edges.shape[0]
+    coming = [copies.start(back, got), copies.start(d_own_in, cot_own)]
+    coming += [copies.start(rate_in, rates), copies.start(nodes.at[core], own)]
+    coming += [copies.start(saved_in.at[tall:], saved.at[tall:]), copies.start(halo, room)]
+    order = (3, 2, 1, 0)
+    waits = copies.either(
+        core == 0, *[[v[i] for i in order] for v in (first_rows(mine), first_rows(other), held)]
+    )
+    waits = [waits[i] for i in order]
+    late = [copies.start(d_edges_in, cot_edge), copies.start(saved_in.at[:tall], saved.at[:tall])]
+    late += [copies.start(latents.at[core], edges)]
     src, dst = src[...], dst[...]
     gains = jnp.where(core == 0, g_mine[...], g_other[...])
     gains = (gains[:1], gains[1:2])
@@ -449,8 +468,15 @@
         copy.wait()
     fill_halo(table, room)
     cot = (cot_own[...] + spread(hot, placed(1, got))).astype(BF).astype(F32)
-    for wait in waits:
-        wait()
+    waits[3]()
+    waits[2]()
+
+    def arrive():
+        for copy in late:
+            copy.wait()
+        waits[1]()
+        waits[0]()
+
     ready, finish = back_outs(copies, layout, store, outs, (*work, room))
 
     def put_gains(value):
@@ -461,7 +487,7 @@
 
     backward(
         cot, cot_edge, own, edges, table, src, dst, count[0], held, gains, res,
-        core, me, layout, SEQUENCE[0], store, (*work[:2], room, put_gains), (d_outer, d_pre), ready,
+        core, me, layout, SEQUENCE[0], store, (*work[:2], room, put_gains), (d_outer, d_pre), ready, arrive,
     )
     finish()
 
@@ -483,14 +509,14 @@
     return jax.ShapeDtypeStruct(tuple(dims), dtype)
 
 
-def call(kernel, in_specs, outs, out_specs, scratch, flops, traffic):
+def call(kernel, in_specs, outs, out_specs, scratch, flops, traffic, limit=SMALL_LIMIT):
     return pl.pallas_call(
         kernel,
         in_specs=in_specs,
         out_shape=outs,
         out_specs=out_specs,
         scratch_shapes=scratch,
-        compiler_params=pltpu.CompilerParams(vmem_limit_bytes=VMEM_LIMIT),
+        compiler_params=pltpu.CompilerParams(vmem_limit_bytes=limit),
         cost_estimate=pl.CostEstimate(flops=flops, bytes_accessed=traffic, transcendentals=0),
     )
 
@@ -687,6 +713,7 @@
         [*layer_s, node_s, edge_s, dma((20,))],
         11 * 10**8,
         26 * 10**6,
+        VMEM_LIMIT,
     )(*small, node_latent, edge_latent, halo_zero, *mine, *other)
     halo_one = exchange(sent)
 
@@ -721,6 +748,7 @@
         [*layer_s, node_s, edge_s, node_s, *back_s],
         28 * 10**8,
         44 * 10**6,
+        VMEM_LIMIT,
     )(*small, node_one, edge_one, node_cot, halo_one, *mine, *other)
     d_own, d_edges, sent, keep_one, send_one = done
     back = exchange(sent)
@@ -739,6 +767,7 @@
         [*layer_s, pltpu.VMEM((NODE_DEV, D), F32), edge_s, room_s, *back_s],
         18 * 10**8,
         37 * 10**6,
+        VMEM_LIMIT,
     )(
         *small, gain_one, node_latent, edge_latent, d_own, d_edges, saved, rates, halo_zero,
         back, *mine, *other,
@@ -767,16 +796,18 @@
         far = [
             [p.quarter(i) if p.rows > GAINS else p.whole() for p in zero] for i in range(4)
         ]
+        *far, stay = combine([*[(BF, v) for v in far[1:]], (F32, far[0])])
+        got = [across(v, 4 * i) for i, v in enumerate(far, 1)]
+        got_one = tied([one[1].terms.pop()[0]], far)[0]
+        one[0].terms.pop()
+        receive(one, got_one)
         near = [p.upper() for p in one]
-        far[0] += [p.whole() for p in one]
-        *far, near_n, near_e, stay = combine(
-            [*[(BF, v) for v in far[1:]], *[(BF, [v]) for v in near], (F32, far[0])]
+        near_n, near_e, stay_one = combine(
+            [*[(BF, [v]) for v in near], (F32, [p.whole() for p in one])]
         )
-        got = [across(v, 4 * i) for i, v in enumerate(far, 1)]
         near = [across(near_n, 2), across(near_e, 1)]
-        rows = got[0].shape[0]
-        zero = added([stay[:rows], *got])
-        one = added([stay[rows:], jnp.concatenate(near, axis=0)])
+        zero = added([stay, *got])
+        one = added([stay_one, jnp.concatenate(near, axis=0)])
         sums, zero = zero[:GAINS], zero[GAINS:]
         (back,) = tied([back], far)
     else:
@@ -831,6 +862,7 @@
         [],
         10**6,
         7 * 10**6,
+        16 * 1024 * 1024,
     )(got, one, zero)
     grads = dict(zip(ROWS, grads))
     if shards == 1:

time: 137 us -> 129 us (0.942)
  waiting for transfers between devices: 25.2 us -> 18.5 us
  other arithmetic: 12.5 us -> 9.83 us
  Pallas kernels: 42.5 us -> 40.9 us
  starting transfers between devices: 34.1 us -> 35.7 us
    ppermute x9, waiting for transfers between devices: 9.34 us -> 1.06 us  [across(): lax.ppermute(value, 'dom', [(p, p ^ step) for p in range(lax.axis_size('d...]
    select_n x1, other arithmetic: 1.79 us -> 0.07 us  [body(): got = other_core(jnp.where(first, one, zero))]
    pallas_call x3 -> x4, Pallas kernels: 9.13 us -> 10.5 us  [combine(): call(kernel, [ANY] * len(arrays), [shape(*s) for s in shapes], [ANY] * le...]
    unnamed x34 -> x40, local copies, waits for them, and re-layouts: 5.98 us -> 7.28 us
  transfers between devices with their start and end apart: 26 -> 26, of which waited for: 7 -> 8; matrix products, arithmetic and copies ran while one was open for 11% -> 10% of each run, Pallas kernels for 15% -> 16%
where the time goes in v3:
time: 129 us; the launch traced here: 128 us
  Pallas kernels  40.9 us (32%)
  starting transfers between devices  35.7 us (28%)
  waiting for transfers between devices  18.5 us (14%)
  blocking collectives  11.3 us (9%)
  local copies, waits for them, and re-layouts  10.3 us (8%)
  other arithmetic  9.83 us (8%)
  between operations  1.59 us (1%)
    all_to_all x3, starting transfers between devices, exchange(): return lax.all_to_all(rows, 'dom', 0, 0, tiled=True)  14.7 us
    ppermute x9, starting transfers between devices, across(): lax.ppermute(value, 'dom', [(p, p ^ step) for p in range(lax.axis_size('d...  14.2 us
    all_to_all x1, blocking collectives, exchange(): return lax.all_to_all(rows, 'dom', 0, 0, tiled=True)  11.3 us
    pallas_call x1, Pallas kernels, body(): call(functools.partial(second_kernel, shards), small_specs + [ANY] * (3 +...  10.8 us
    pallas_call x4, Pallas kernels, combine(): call(kernel, [ANY] * len(arrays), [shape(*s) for s in shapes], [ANY] * le...  10.5 us
    ppermute x4, waiting for transfers between devices, across(): return lax.ppermute(value, 'rep', [(0, 1), (1, 0)])  9.02 us
    pallas_call x1, Pallas kernels, body(): call(functools.partial(third_kernel, shards), small_specs + [VMEM] + [ANY...  8.05 us
    unnamed x40, local copies, waits for them, and re-layouts  7.28 us
  transfers between devices with their start and end apart: 26, of which 8 were waited for; matrix products, arithmetic and copies ran while one was open for 10% of the time, Pallas kernels for 16%

profile of v3, /device:TPU:0, one launch (start us, length us, event | category | flops | bytes accessed | tf_op | source)
XLA Modules:
  0.0 128.2 jit_solution(6572525150136225704)
XLA Ops:
  1.7 2.5 %shard_map.188 = bf16[128,512]{1,0:T(8,128)(2,1)} custom-call(s32[1,4,16]{2,1,0:T(4,128)} %lists.9, bf16[2,128,512]{2,1,0:T(8,128)(2,1)} %nodes.5), custom_call_target="tpu_custom_call" | custom-call | flops 10000000 | bytes 7000000 | tf_op jit(solution)/shard_map/pallas_call | solution.py:676
  4.2 7.3 %all-to-all-start = ((bf16[8,16,512]{2,1,0:T(8,128)(2,1)}), bf16[8,16,512]{2,1,0:T(8,128)(2,1)S(1)}, u32[]{:S(2)}, u32[]{:S(2)}) async-start(bf16[8,16,512]{2,1,0:T(8,128)(2,1)} %bitcast.26), calls=%async_computation | async-start | bytes 262144 | tf_op jit(solution)/shard_map/all_to_all | solution.py:525
  11.5 0.7 pad_maximum_fusion.g_mine
  12.3 1.3 broadcast_in_dim.24.src
  13.6 1.2 broadcast_in_dim.25.dst
  15.4 3.4 %all-to-all-done = bf16[8,16,512]{2,1,0:T(8,128)(2,1)S(1)} async-done(((bf16[8,16,512]{2,1,0:T(8,128)(2,1)}), bf16[8,16,512]{2,1,0:T(8,128)(2,1)S(1)}, u32[]{:S(2)}, u32[]{:S(2)}) %all-to-all-start) | async-done | bytes 131104 | tf_op jit(solution)/shard_map/all_to_all | solution.py:525
  18.9 0.6 copy-done.9
  19.7 6.3 %shard_map.189 = (bf16[128,512]{1,0:T(8,128)(2,1)}, bf16[384,512]{1,0:T(8,128)(2,1)}, bf16[1664,512]{1,0:T(8,128)(2,1)}, f32[512,128]{1,0:T(8,128)}, bf16[128,512]{1,0:T(8,128)(2,1)}) custom-call(s32[1]{0:T(128)S(6)} %copy.21.count, s32[1,384]{1,0:T(1,128)} %broadcast_in_dim.24.src, s32[1,384]{1,0:T(1,128)} %broadcast_in_dim.25.dst, s32[1,4,16]{2,1,0:T(4,128)} %lists.9, ...), custom_call_target="tpu_custom_call" | custom-call | flops 1100000000 | bytes 26000000 | tf_op jit(solution)/shard_map/pallas_call | solution.py:702
  26.0 11.3 %all_to_all.46 = bf16[8,16,512]{2,1,0:T(8,128)(2,1)} all-to-all(bf16[8,16,512]{2,1,0:T(8,128)(2,1)} %bitcast.30), channel_id=1, replica_groups=mesh['segment'=2,'dom'=8,'rep'=2] {'dom'}, dimensions={0} | all-to-all | bytes 262144 | tf_op jit(solution)/shard_map/all_to_all | solution.py:525
  37.3 10.8 %shard_map.190 = (bf16[128,512]{1,0:T(8,128)(2,1)}, bf16[384,512]{1,0:T(8,128)(2,1)}, f32[16,512]{1,0:T(8,128)}, f32[128,512]{1,0:T(8,128)}, bf16[384,512]{1,0:T...) custom-call(s32[1]{0:T(128)S(6)} %copy.21.count, ...), custom_call_target="tpu_custom_call" | custom-call | flops 2800000000 | bytes 44000000 | tf_op jit(solution)/shard_map/pallas_call | solution.py:743
  48.3 4.0 %all-to-all-start.2 = ((bf16[8,16,512]{2,1,0:T(8,128)(2,1)}), bf16[8,16,512]{2,1,0:T(8,128)(2,1)}, u32[]{:S(2)}, u32[]{:S(2)}) async-start(bf16[8,16,512]{2,1,0:T(8,128)(2,1)} %bitcast.28), calls=%async_computation.2 | async-start | bytes 262144 | tf_op jit(solution)/shard_map/all_to_all | solution.py:525
  52.3 2.4 %add_convert_fusion = bf16[512,512]{1,0:T(8,128)(2,1)} fusion(bf16[1808,512]{1,0:T(8,128)(2,1)S(1)} %collective-permute-done.5.refs_1_.refs_5_, bf16[1808,512]{1,0:T(8,128)(2,1)} %get-tuple-element.57.refs_0_.refs_4_), kind=kLoop, calls=%fused_computation | loop fusion | flops 1048576 | bytes 1572864 | tf_op jit(solution)/shard_map/convert_element_type | solution.py:632
  54.7 1.9 %collective-permute-start.7 = (bf16[512,512]{1,0:T(8,128)(2,1)}, bf16[512,512]{1,0:T(8,128)(2,1)S(1)}, u32[]{:S(2)}, u32[]{:S(2)}) collective-permute-start(bf16[512,512]{1,0:T(8,128)(2,1)} %add_convert_fusion), channel_id=1, source_target_pairs={{0,2},{2,0},{4,6},{6,4},{8,10},{10,8},{12,14},{14,12},{1,3},{3,1},... | collective-permute-start | bytes 1572872 | tf_op jit(solution)/shard_map/ppermute | solution.py:536
  56.5 1.8 %add_convert_fusion.1 = bf16[384,512]{1,0:T(8,128)(2,1)} fusion(bf16[1808,512]{1,0:T(8,128)(2,1)S(1)} %collective-permute-done.5.refs_1_.refs_5_, bf16[1808,512]{1,0:T(8,128)(2,1)} %get-tuple-element.57.refs_0_.refs_4_), kind=kLoop, calls=%fused_computation.2 | loop fusion | flops 786432 | bytes 1179648 | tf_op jit(solution)/shard_map/convert_element_type | solution.py:632
  58.4 1.5 %collective-permute-start.6 = (bf16[384,512]{1,0:T(8,128)(2,1)}, bf16[384,512]{1,0:T(8,128)(2,1)S(1)}, u32[]{:S(2)}, u32[]{:S(2)}) collective-permute-start(bf16[384,512]{1,0:T(8,128)(2,1)} %add_convert_fusion.1), channel_id=1, source_target_pairs={{0,1},{1,0},{2,3},{3,2},{4,5},{5,4},{6,7},{7,6},{8,9},{9,8},{10,11... | collective-permute-start | bytes 1179656 | tf_op jit(solution)/shard_map/ppermute | solution.py:534
  60.3 8.0 %shard_map.191 = (f32[128,512]{1,0:T(8,128)}, bf16[384,512]{1,0:T(8,128)(2,1)}, bf16[128,512]{1,0:T(8,128)(2,1)}, bf16[1808,512]{1,0:T(8,128)(2,1)}, bf16[1808,512]{1,0:T(8,128)(2,1)}) custom-call(s32[1]{0:T(128)S(6)} %copy.21.count, s32[1,384]{1,0:T(1,128)} %broadcast_in_dim.24.src, s32[1,384]{1,0:T(1,128)} %broadcast_in_dim.25.dst, s32[1,4,16]{2,1,0:T(4,128)} %lists.9, ...), custom_call_target="tpu_custom_call" | custom-call | flops 1800000000 | bytes 37000000 | tf_op jit(solution)/shard_map/pallas_call | solution.py:762
  68.4 1.2 collective-permute-done.6.refs_2_.refs_6_
  69.6 0.7 copy-done.3
  70.3 0.8 copy-done.2
  71.1 4.0 %collective-permute-done.8.refs_5_.refs_1_ = bf16[1808,512]{1,0:T(8,128)(2,1)S(1)} collective-permute-done((bf16[1808,512]{1,0:T(8,128)(2,1)}, bf16[1808,512]{1,0:T(8,128)(2,1)S(1)}, u32[]{:S(2)}, u32[]{:S(2)}) %collective-permute-start.8) | collective-permute-done | bytes 1851424 | tf_op jit(solution)/shard_map/ppermute | solution.py:529
  75.2 1.3 copy-done.1
  76.4 2.9 %shard_map.192 = (bf16[448,512]{1,0:T(8,128)(2,1)}, bf16[512,512]{1,0:T(8,128)(2,1)}, bf16[400,512]{1,0:T(8,128)(2,1)}) custom-call(bf16[1808,512]{1,0:T(8,128)(2,1)} %get-tuple-element.57.refs_0_.refs_4_, bf16[1808,512]{1,0:T(8,128)(2,1)} %copy-done, bf16[384,512]{1,0:T(8,128)(2,1)} %copy-done.3, bf16[512,512]{1,0:T(8,128)(2,1)} %copy-done.2, ...), custom_call_target="tpu_custom_call" | custom-call | flops 1000000 | bytes 8000000 | tf_op jit(solution)/shard_map/pallas_call | solution.py:615
  79.4 0.7 collective-permute-start.9
  80.1 1.5 %collective-permute-start.11 = (bf16[448,512]{1,0:T(8,128)(2,1)}, bf16[448,512]{1,0:T(8,128)(2,1)S(1)}, u32[]{:S(2)}, u32[]{:S(2)}) collective-permute-start(bf16[448,512]{1,0:T(8,128)(2,1)} %get-tuple-element.67), channel_id=1, source_target_pairs={{0,4},{2,6},{4,0},{6,2},{8,12},{10,14},{12,8},{14,10},{1,5},{3,7},... | collective-permute-start | bytes 1376264 | tf_op jit(solution)/shard_map/ppermute | solution.py:536
  81.6 1.5 %collective-permute-start.10 = (bf16[400,512]{1,0:T(8,128)(2,1)}, bf16[400,512]{1,0:T(8,128)(2,1)S(1)}, u32[]{:S(2)}, u32[]{:S(2)}) collective-permute-start(bf16[400,512]{1,0:T(8,128)(2,1)} %get-tuple-element.66), channel_id=1, source_target_pairs={{0,1},{1,0},{2,3},{3,2},{4,5},{5,4},{6,7},{7,6},{8,9},{9,8},{10,11... | collective-permute-start | bytes 1228808 | tf_op jit(solution)/shard_map/ppermute | solution.py:534
  83.1 1.8 %broadcast_select_fusion = bf16[384,512]{1,0:T(8,128)(2,1)} fusion(bf16[384,512]{1,0:T(8,128)(2,1)} %get-tuple-element.78, bf16[384,512]{1,0:T(8,128)(2,1)} %get-tuple-element.77, pred[]{:T(512)S(6)} %eq.3), kind=kLoop, calls=%fused_computation.5 | loop fusion | flops 196608 | bytes 1179649 | tf_op jit(solution)/shard_map/jit(_where)/select_n | solution.py:834
  84.9 7.8 %collective-permute-done.10.refs_3_.refs_2_ = bf16[400,512]{1,0:T(8,128)(2,1)S(1)} collective-permute-done((bf16[400,512]{1,0:T(8,128)(2,1)}, bf16[400,512]{1,0:T(8,128)(2,1)S(1)}, u32[]{:S(2)}, u32[]{:S(2)}) %collective-permute-start.10) | collective-permute-done | bytes 409632 | tf_op jit(solution)/shard_map/ppermute | solution.py:534
  92.8 0.9 collective-permute-done.9.refs_2_.refs_4_
  93.7 0.9 copy-done.4
  94.5 2.5 %shard_map.193 = (bf16[256,512]{1,0:T(8,128)(2,1)}, bf16[208,512]{1,0:T(8,128)(2,1)}, bf16[224,512]{1,0:T(8,128)(2,1)}) custom-call(bf16[1808,512]{1,0:T(8,128)(2,1)} %get-tuple-element.62.refs_4_.refs_0_, bf16[1808,512]{1,0:T(8,128)(2,1)} %copy-done.1, bf16[512,512]{1,0:T(8,128)(2,1)} %copy-done.4, bf16[400,512]{1,0:T(8,128)(2,1)} %copy-done.7, ...), custom_call_target="tpu_custom_call" | custom-call | flops 1000000 | bytes 8000000 | tf_op jit(solution)/shard_map/pallas_call | solution.py:615
  97.0 1.6 %collective-permute-start.13 = (bf16[256,512]{1,0:T(8,128)(2,1)}, bf16[256,512]{1,0:T(8,128)(2,1)S(1)}, u32[]{:S(2)}, u32[]{:S(2)}) collective-permute-start(bf16[256,512]{1,0:T(8,128)(2,1)} %get-tuple-element.68), channel_id=1, source_target_pairs={{0,1},{1,0},{2,3},{3,2},{4,5},{5,4},{6,7},{7,6},{8,9},{9,8},{10,11... | collective-permute-start | bytes 786440 | tf_op jit(solution)/shard_map/ppermute | solution.py:534
  98.6 1.4 %collective-permute-start.12 = (bf16[208,512]{1,0:T(8,128)(2,1)}, bf16[208,512]{1,0:T(8,128)(2,1)S(1)}, u32[]{:S(2)}, u32[]{:S(2)}) collective-permute-start(bf16[208,512]{1,0:T(8,128)(2,1)} %get-tuple-element.69), channel_id=1, source_target_pairs={{0,2},{2,0},{4,6},{6,4},{8,10},{10,8},{12,14},{14,12},{1,3},{3,1},... | collective-permute-start | bytes 638984 | tf_op jit(solution)/shard_map/ppermute | solution.py:536
  99.9 2.4 %collective-permute-start.16 = (bf16[224,512]{1,0:T(8,128)(2,1)}, bf16[224,512]{1,0:T(8,128)(2,1)S(1)}, u32[]{:S(2)}, u32[]{:S(2)}) collective-permute-start(bf16[224,512]{1,0:T(8,128)(2,1)} %get-tuple-element.70), channel_id=1, source_target_pairs={{0,8},{2,10},{4,12},{6,14},{8,0},{10,2},{12,4},{14,6},{1,9},{3,11}... | collective-permute-start | bytes 688136 | tf_op jit(solution)/shard_map/ppermute | solution.py:536
  102.3 3.4 %all-to-all-start.3 = ((bf16[8,16,512]{2,1,0:T(8,128)(2,1)}), bf16[8,16,512]{2,1,0:T(8,128)(2,1)S(1)}, u32[]{:S(2)}, u32[]{:S(2)}) async-start(bf16[8,16,512]{2,1,0:T(8,128)(2,1)} %bitcast.6), calls=%async_computation.3 | async-start | bytes 262144 | tf_op jit(solution)/shard_map/all_to_all | solution.py:525
  105.7 1.2 select_bitcast_fusion.1
  106.9 0.9 maximum_bitcast_fusion
  107.9 0.7 copy-done.17
  108.6 0.7 copy-done.14
  109.3 2.8 %shard_map.194 = (bf16[128,512]{1,0:T(8,128)(2,1)}, bf16[128,512]{1,0:T(8,128)(2,1)}, bf16[128,512]{1,0:T(8,128)(2,1)}, f32[128,512]{1,0:T(8,128)}) custom-call(bf16[1808,512]{1,0:T(8,128)(2,1)} %get-tuple-element.62.refs_4_.refs_0_, bf16[1808,512]{1,0:T(8,128)(2,1)} %copy-done.1, bf16[400,512]{1,0:T(8,128)(2,1)} %copy-done.7, bf16[208,512]{1,0:T(8,128)(2,1)} %copy-done.17, ...), custom_call_target="tpu_custom_call" | custom-call | flops 1000000 | bytes 8000000 | tf_op jit(solution)/shard_map/pallas_call | solution.py:615
  112.1 2.0 %collective-permute-start.19 = (bf16[128,512]{1,0:T(8,128)(2,1)}, bf16[128,512]{1,0:T(8,128)(2,1)S(1)}, u32[]{:S(2)}, u32[]{:S(2)}) collective-permute-start(bf16[128,512]{1,0:T(8,128)(2,1)} %get-tuple-element.72), channel_id=1, source_target_pairs={{0,4},{2,6},{4,0},{6,2},{8,12},{10,14},{12,8},{14,10},{1,5},{3,7},... | collective-permute-start | bytes 393224 | tf_op jit(solution)/shard_map/ppermute | solution.py:536
  114.1 2.4 %collective-permute-start.20 = (bf16[128,512]{1,0:T(8,128)(2,1)}, bf16[128,512]{1,0:T(8,128)(2,1)S(1)}, u32[]{:S(2)}, u32[]{:S(2)}) collective-permute-start(bf16[128,512]{1,0:T(8,128)(2,1)} %get-tuple-element.73), channel_id=1, source_target_pairs={{0,8},{2,10},{4,12},{6,14},{8,0},{10,2},{12,4},{14,6},{1,9},{3,11}... | collective-permute-start | bytes 393224 | tf_op jit(solution)/shard_map/ppermute | solution.py:536
  116.6 0.7 copy-done.16
  117.3 2.2 %shard_map.196 = (bf16[48,512]{1,0:T(8,128)(2,1)}, bf16[64,512]{1,0:T(8,128)(2,1)}, f32[112,512]{1,0:T(8,128)}) custom-call(bf16[1808,512]{1,0:T(8,128)(2,1)} %get-tuple-element.57.refs_0_.refs_4_, bf16[1808,512]{1,0:T(8,128)(2,1)} %copy-done, bf16[384,512]{1,0:T(8,128)(2,1)} %copy-done.3, bf16[448,512]{1,0:T(8,128)(2,1)} %copy-done.6, ...), custom_call_target="tpu_custom_call" | custom-call | flops 1000000 | bytes 8000000 | tf_op jit(solution)/shard_map/pallas_call | solution.py:615
  120.1 1.9 %collective-permute-start.17 = (bf16[48,512]{1,0:T(8,128)(2,1)}, bf16[48,512]{1,0:T(8,128)(2,1)S(1)}, u32[]{:S(2)}, u32[]{:S(2)}) collective-permute-start(bf16[48,512]{1,0:T(8,128)(2,1)} %get-tuple-element.81), channel_id=1, source_target_pairs={{0,2},{2,0},{4,6},{6,4},{8,10},{10,8},{12,14},{14,12},{1,3},{3,1},... | collective-permute-start | bytes 147464 | tf_op jit(solution)/shard_map/ppermute | solution.py:536
  122.0 0.7 copy-done.12
  122.7 1.9 %shard_map.195 = bf16[128,512]{1,0:T(8,128)(2,1)} custom-call(s32[1,4,16]{2,1,0:T(4,128)} %lists.9, f32[128,512]{1,0:T(8,128)} %get-tuple-element.60.d_own, bf16[128,512]{1,0:T(8,128)(2,1)} %bitcast.27), custom_call_target="tpu_custom_call" | custom-call | flops 10000000 | bytes 7000000 | tf_op jit(solution)/shard_map/pallas_call | solution.py:823
  126.1 0.7 maximum_bitcast_fusion.1
  127.4 0.8 shard_map.197
  (71 shorter events, 4.7 us)
Async XLA Ops:
  0.6 18.2 %collective-permute-start.1 = (bf16[1,1536,512]{2,1,0:T(8,128)(2,1)}, bf16[1,1536,512]{2,1,0:T(8,128)(2,1)}, u32[]{:S(2)}, u32[]{:S(2)}) collective-permute-start(bf16[1,1536,512]{2,1,0:T(8,128)(2,1)} %rest_2_.5), channel_id=1, source_target_pairs={{0,16},{16,0},{1,17},{17,1},{2,18},{18,2},{3,19},{19,3},{4,20},{20... | collective-permute-start | bytes 4718600 | tf_op jit(solution)/shard_map/ppermute | solution.py:529
  1.1 17.7 %collective-permute-start.3 = (bf16[1,1024,512]{2,1,0:T(8,128)(2,1)}, bf16[1,1024,512]{2,1,0:T(8,128)(2,1)}, u32[]{:S(2)}, u32[]{:S(2)}) collective-permute-start(bf16[1,1024,512]{2,1,0:T(8,128)(2,1)} %rest_4_.5), channel_id=1, source_target_pairs={{0,16},{16,0},{1,17},{17,1},{2,18},{18,2},{3,19},{19,3},{4,20},{20... | collective-permute-start | bytes 3145736 | tf_op jit(solution)/shard_map/ppermute | solution.py:529
  1.2 17.6 %collective-permute-start.2 = (bf16[1,512,512]{2,1,0:T(8,128)(2,1)}, bf16[1,512,512]{2,1,0:T(8,128)(2,1)S(1)}, u32[]{:S(2)}, u32[]{:S(2)}) collective-permute-start(bf16[1,512,512]{2,1,0:T(8,128)(2,1)} %rest_3_.5), channel_id=1, source_target_pairs={{0,16},{16,0},{1,17},{17,1},{2,18},{18,2},{3,19},{19,3},{4,20},{20... | collective-permute-start | bytes 1572872 | tf_op jit(solution)/shard_map/ppermute | solution.py:529
  1.7 17.2 %collective-permute-start.4 = (bf16[1,512,512]{2,1,0:T(8,128)(2,1)}, bf16[1,512,512]{2,1,0:T(8,128)(2,1)}, u32[]{:S(2)}, u32[]{:S(2)}) collective-permute-start(bf16[1,512,512]{2,1,0:T(8,128)(2,1)} %rest_5_.1), channel_id=1, source_target_pairs={{0,16},{16,0},{1,17},{17,1},{2,18},{18,2},{3,19},{19,3},{4,20},{20... | collective-permute-start | bytes 1572872 | tf_op jit(solution)/shard_map/ppermute | solution.py:529
  4.2 14.6 %all-to-all-start = ((bf16[8,16,512]{2,1,0:T(8,128)(2,1)}), bf16[8,16,512]{2,1,0:T(8,128)(2,1)S(1)}, u32[]{:S(2)}, u32[]{:S(2)}) async-start(bf16[8,16,512]{2,1,0:T(8,128)(2,1)} %bitcast.26), calls=%async_computation | async-start | bytes 262144 | tf_op jit(solution)/shard_map/all_to_all | solution.py:525
  12.2 6.7 %copy-start.18 = (f32[2,512]{1,0:T(2,128)}, f32[2,512]{1,0:T(2,128)S(1)}, u32[]{:S(2)}) copy-start(f32[2,512]{1,0:T(2,128)S(1)} %pad_maximum_fusion.g_mine) | copy-start | bytes 12292
  12.2 3.2 %collective-permute-start = (f32[2,512]{1,0:T(2,128)S(1)}, f32[2,512]{1,0:T(2,128)S(1)}, u32[]{:S(2)}, u32[]{:S(2)}) collective-permute-start(f32[2,512]{1,0:T(2,128)S(1)} %pad_maximum_fusion.g_mine), channel_id=1, source_target_pairs={{0,16},{16,0},{1,17},{17,1},{2,18},{18,2},{3,19},{19,3},{4,20},{20... | collective-permute-start | bytes 12296 | tf_op jit(solution)/shard_map/ppermute | solution.py:529
  15.4 3.5 %copy-start.19 = (f32[2,512]{1,0:T(2,128)}, f32[2,512]{1,0:T(2,128)S(1)}, u32[]{:S(2)}) copy-start(f32[2,512]{1,0:T(2,128)S(1)} %collective-permute-done.g_other) | copy-start | bytes 12292
  18.9 0.7 copy-start.9
  18.9 0.8 copy-start.5
  48.2 4.1 %collective-permute-start.5 = (bf16[1808,512]{1,0:T(8,128)(2,1)}, bf16[1808,512]{1,0:T(8,128)(2,1)S(1)}, u32[]{:S(2)}, u32[]{:S(2)}) collective-permute-start(bf16[1808,512]{1,0:T(8,128)(2,1)} %get-tuple-element.58), channel_id=1, source_target_pairs={{0,16},{16,0},{1,17},{17,1},{2,18},{18,2},{3,19},{19,3},{4,20},{20... | collective-permute-start | bytes 5554184 | tf_op jit(solution)/shard_map/ppermute | solution.py:529
  48.3 12.1 %all-to-all-start.2 = ((bf16[8,16,512]{2,1,0:T(8,128)(2,1)}), bf16[8,16,512]{2,1,0:T(8,128)(2,1)}, u32[]{:S(2)}, u32[]{:S(2)}) async-start(bf16[8,16,512]{2,1,0:T(8,128)(2,1)} %bitcast.28), calls=%async_computation.2 | async-start | bytes 262144 | tf_op jit(solution)/shard_map/all_to_all | solution.py:525
  52.3 4.3 %copy-start = (bf16[1808,512]{1,0:T(8,128)(2,1)}, bf16[1808,512]{1,0:T(8,128)(2,1)S(1)}, u32[]{:S(2)}) copy-start(bf16[1808,512]{1,0:T(8,128)(2,1)S(1)} %collective-permute-done.5.refs_1_.refs_5_) | copy-start | bytes 5554180
  54.7 14.9 %collective-permute-start.7 = (bf16[512,512]{1,0:T(8,128)(2,1)}, bf16[512,512]{1,0:T(8,128)(2,1)S(1)}, u32[]{:S(2)}, u32[]{:S(2)}) collective-permute-start(bf16[512,512]{1,0:T(8,128)(2,1)} %add_convert_fusion), channel_id=1, source_target_pairs={{0,2},{2,0},{4,6},{6,4},{8,10},{10,8},{12,14},{14,12},{1,3},{3,1},... | collective-permute-start | bytes 1572872 | tf_op jit(solution)/shard_map/ppermute | solution.py:536
  58.4 11.2 %collective-permute-start.6 = (bf16[384,512]{1,0:T(8,128)(2,1)}, bf16[384,512]{1,0:T(8,128)(2,1)S(1)}, u32[]{:S(2)}, u32[]{:S(2)}) collective-permute-start(bf16[384,512]{1,0:T(8,128)(2,1)} %add_convert_fusion.1), channel_id=1, source_target_pairs={{0,1},{1,0},{2,3},{3,2},{4,5},{5,4},{6,7},{7,6},{8,9},{9,8},{10,11... | collective-permute-start | bytes 1179656 | tf_op jit(solution)/shard_map/ppermute | solution.py:534
  69.5 0.8 copy-start.3
  70.3 0.8 copy-start.2
  71.1 4.0 %collective-permute-start.8 = (bf16[1808,512]{1,0:T(8,128)(2,1)}, bf16[1808,512]{1,0:T(8,128)(2,1)S(1)}, u32[]{:S(2)}, u32[]{:S(2)}) collective-permute-start(bf16[1808,512]{1,0:T(8,128)(2,1)} %get-tuple-element.64), channel_id=1, source_target_pairs={{0,16},{16,0},{1,17},{17,1},{2,18},{18,2},{3,19},{19,3},{4,20},{20... | collective-permute-start | bytes 5554184 | tf_op jit(solution)/shard_map/ppermute | solution.py:529
  75.2 1.3 copy-start.1
  79.4 14.2 %collective-permute-start.9 = (bf16[512,512]{1,0:T(8,128)(2,1)}, bf16[512,512]{1,0:T(8,128)(2,1)S(1)}, u32[]{:S(2)}, u32[]{:S(2)}) collective-permute-start(bf16[512,512]{1,0:T(8,128)(2,1)} %get-tuple-element.65), channel_id=1, source_target_pairs={{0,2},{2,0},{4,6},{6,4},{8,10},{10,8},{12,14},{14,12},{1,3},{3,1},... | collective-permute-start | bytes 1572872 | tf_op jit(solution)/shard_map/ppermute | solution.py:536
  80.1 12.7 %collective-permute-start.11 = (bf16[448,512]{1,0:T(8,128)(2,1)}, bf16[448,512]{1,0:T(8,128)(2,1)S(1)}, u32[]{:S(2)}, u32[]{:S(2)}) collective-permute-start(bf16[448,512]{1,0:T(8,128)(2,1)} %get-tuple-element.67), channel_id=1, source_target_pairs={{0,4},{2,6},{4,0},{6,2},{8,12},{10,14},{12,8},{14,10},{1,5},{3,7},... | collective-permute-start | bytes 1376264 | tf_op jit(solution)/shard_map/ppermute | solution.py:536
  81.6 11.2 %collective-permute-start.10 = (bf16[400,512]{1,0:T(8,128)(2,1)}, bf16[400,512]{1,0:T(8,128)(2,1)S(1)}, u32[]{:S(2)}, u32[]{:S(2)}) collective-permute-start(bf16[400,512]{1,0:T(8,128)(2,1)} %get-tuple-element.66), channel_id=1, source_target_pairs={{0,1},{1,0},{2,3},{3,2},{4,5},{5,4},{6,7},{7,6},{8,9},{9,8},{10,11... | collective-permute-start | bytes 1228808 | tf_op jit(solution)/shard_map/ppermute | solution.py:534
  84.9 20.8 %collective-permute-start.15 = (bf16[384,512]{1,0:T(8,128)(2,1)}, bf16[384,512]{1,0:T(8,128)(2,1)}, u32[]{:S(2)}, u32[]{:S(2)}) collective-permute-start(bf16[384,512]{1,0:T(8,128)(2,1)} %broadcast_select_fusion), channel_id=1, source_target_pairs={{0,16},{16,0},{1,17},{17,1},{2,18},{18,2},{3,19},{19,3},{4,20},{20... | collective-permute-start | bytes 1179656 | tf_op jit(solution)/shard_map/ppermute | solution.py:529
  84.9 20.8 %copy-start.8 = (bf16[384,512]{1,0:T(8,128)(2,1)S(1)}, bf16[384,512]{1,0:T(8,128)(2,1)}, u32[]{:S(2)}) copy-start(bf16[384,512]{1,0:T(8,128)(2,1)} %get-tuple-element.78) | copy-start | bytes 1179652
  92.7 0.9 copy-start.7
  92.8 0.9 copy-start.6
  93.6 0.9 copy-start.4
  97.0 10.9 %collective-permute-start.13 = (bf16[256,512]{1,0:T(8,128)(2,1)}, bf16[256,512]{1,0:T(8,128)(2,1)S(1)}, u32[]{:S(2)}, u32[]{:S(2)}) collective-permute-start(bf16[256,512]{1,0:T(8,128)(2,1)} %get-tuple-element.68), channel_id=1, source_target_pairs={{0,1},{1,0},{2,3},{3,2},{4,5},{5,4},{6,7},{7,6},{8,9},{9,8},{10,11... | collective-permute-start | bytes 786440 | tf_op jit(solution)/shard_map/ppermute | solution.py:534
  98.6 9.3 %collective-permute-start.12 = (bf16[208,512]{1,0:T(8,128)(2,1)}, bf16[208,512]{1,0:T(8,128)(2,1)S(1)}, u32[]{:S(2)}, u32[]{:S(2)}) collective-permute-start(bf16[208,512]{1,0:T(8,128)(2,1)} %get-tuple-element.69), channel_id=1, source_target_pairs={{0,2},{2,0},{4,6},{6,4},{8,10},{10,8},{12,14},{14,12},{1,3},{3,1},... | collective-permute-start | bytes 638984 | tf_op jit(solution)/shard_map/ppermute | solution.py:536
  99.9 16.6 %collective-permute-start.16 = (bf16[224,512]{1,0:T(8,128)(2,1)}, bf16[224,512]{1,0:T(8,128)(2,1)S(1)}, u32[]{:S(2)}, u32[]{:S(2)}) collective-permute-start(bf16[224,512]{1,0:T(8,128)(2,1)} %get-tuple-element.70), channel_id=1, source_target_pairs={{0,8},{2,10},{4,12},{6,14},{8,0},{10,2},{12,4},{14,6},{1,9},{3,11}... | collective-permute-start | bytes 688136 | tf_op jit(solution)/shard_map/ppermute | solution.py:536
  102.3 19.7 %all-to-all-start.3 = ((bf16[8,16,512]{2,1,0:T(8,128)(2,1)}), bf16[8,16,512]{2,1,0:T(8,128)(2,1)S(1)}, u32[]{:S(2)}, u32[]{:S(2)}) async-start(bf16[8,16,512]{2,1,0:T(8,128)(2,1)} %bitcast.6), calls=%async_computation.3 | async-start | bytes 262144 | tf_op jit(solution)/shard_map/all_to_all | solution.py:525
  107.9 0.7 copy-start.17
  108.6 0.7 copy-start.14
  112.1 12.5 %collective-permute-start.19 = (bf16[128,512]{1,0:T(8,128)(2,1)}, bf16[128,512]{1,0:T(8,128)(2,1)S(1)}, u32[]{:S(2)}, u32[]{:S(2)}) collective-permute-start(bf16[128,512]{1,0:T(8,128)(2,1)} %get-tuple-element.72), channel_id=1, source_target_pairs={{0,4},{2,6},{4,0},{6,2},{8,12},{10,14},{12,8},{14,10},{1,5},{3,7},... | collective-permute-start | bytes 393224 | tf_op jit(solution)/shard_map/ppermute | solution.py:536
  114.1 10.8 %collective-permute-start.20 = (bf16[128,512]{1,0:T(8,128)(2,1)}, bf16[128,512]{1,0:T(8,128)(2,1)S(1)}, u32[]{:S(2)}, u32[]{:S(2)}) collective-permute-start(bf16[128,512]{1,0:T(8,128)(2,1)} %get-tuple-element.73), channel_id=1, source_target_pairs={{0,8},{2,10},{4,12},{6,14},{8,0},{10,2},{12,4},{14,6},{1,9},{3,11}... | collective-permute-start | bytes 393224 | tf_op jit(solution)/shard_map/ppermute | solution.py:536
  116.5 8.1 %copy-start.11 = (bf16[128,512]{1,0:T(8,128)(2,1)S(1)}, bf16[128,512]{1,0:T(8,128)(2,1)}, u32[]{:S(2)}) copy-start(bf16[128,512]{1,0:T(8,128)(2,1)} %get-tuple-element.76) | copy-start | bytes 393220
  116.5 8.4 %copy-start.13 = (f32[128,512]{1,0:T(8,128)S(1)}, f32[128,512]{1,0:T(8,128)}, u32[]{:S(2)}) copy-start(f32[128,512]{1,0:T(8,128)} %get-tuple-element.83) | copy-start | bytes 786436
  116.5 8.4 %collective-permute-start.21 = (bf16[128,512]{1,0:T(8,128)(2,1)}, bf16[128,512]{1,0:T(8,128)(2,1)S(1)}, u32[]{:S(2)}, u32[]{:S(2)}) collective-permute-start(bf16[128,512]{1,0:T(8,128)(2,1)} %get-tuple-element.74), channel_id=1, source_target_pairs={{0,12},{2,14},{4,8},{6,10},{8,4},{10,6},{12,0},{14,2},{1,13},{3,15... | collective-permute-start | bytes 393224 | tf_op jit(solution)/shard_map/ppermute | solution.py:536
  116.6 0.7 copy-start.16
  119.5 5.5 %copy-start.15 = (f32[112,512]{1,0:T(8,128)S(1)}, f32[112,512]{1,0:T(8,128)}, u32[]{:S(2)}) copy-start(f32[112,512]{1,0:T(8,128)} %get-tuple-element.80) | copy-start | bytes 688132
  119.5 5.5 %collective-permute-start.18 = (bf16[64,512]{1,0:T(8,128)(2,1)}, bf16[64,512]{1,0:T(8,128)(2,1)S(1)}, u32[]{:S(2)}, u32[]{:S(2)}) collective-permute-start(bf16[64,512]{1,0:T(8,128)(2,1)} %get-tuple-element.82), channel_id=1, source_target_pairs={{0,1},{1,0},{2,3},{3,2},{4,5},{5,4},{6,7},{7,6},{8,9},{9,8},{10,11... | collective-permute-start | bytes 196616 | tf_op jit(solution)/shard_map/ppermute | solution.py:534
  120.1 4.9 %collective-permute-start.17 = (bf16[48,512]{1,0:T(8,128)(2,1)}, bf16[48,512]{1,0:T(8,128)(2,1)S(1)}, u32[]{:S(2)}, u32[]{:S(2)}) collective-permute-start(bf16[48,512]{1,0:T(8,128)(2,1)} %get-tuple-element.81), channel_id=1, source_target_pairs={{0,2},{2,0},{4,6},{6,4},{8,10},{10,8},{12,14},{14,12},{1,3},{3,1},... | collective-permute-start | bytes 147464 | tf_op jit(solution)/shard_map/ppermute | solution.py:536
  122.0 0.7 copy-start.12
  124.6 1.5 %copy-start.10 = (bf16[128,512]{1,0:T(8,128)(2,1)S(1)}, bf16[128,512]{1,0:T(8,128)(2,1)}, u32[]{:S(2)}) copy-start(bf16[128,512]{1,0:T(8,128)(2,1)} %shard_map.195) | copy-start | bytes 393220
  124.6 1.4 %collective-permute-start.14 = (bf16[128,512]{1,0:T(8,128)(2,1)S(1)}, bf16[128,512]{1,0:T(8,128)(2,1)S(1)}, u32[]{:S(2)}, u32[]{:S(2)}) collective-permute-start(bf16[128,512]{1,0:T(8,128)(2,1)S(1)} %broadcast_select_fusion.1), channel_id=1, source_target_pairs={{0,16},{16,0},{1,17},{17,1},{2,18},{18,2},{3,19},{19,3},{4,20},{20... | collective-permute-start | bytes 393224 | tf_op jit(solution)/shard_map/ppermute | solution.py:529
  125.1 2.3 %collective-permute-start.22 = (f32[112,512]{1,0:T(8,128)S(1)}, f32[112,512]{1,0:T(8,128)S(1)}, u32[]{:S(2)}, u32[]{:S(2)}) collective-permute-start(f32[112,512]{1,0:T(8,128)S(1)} %get-tuple-element.88), channel_id=1, source_target_pairs={{0,16},{16,0},{1,17},{17,1},{2,18},{18,2},{3,19},{19,3},{4,20},{20... | collective-permute-start | bytes 688136 | tf_op jit(solution)/shard_map/ppermute | solution.py:529

commit v4 on v3

--- a/solution.py
+++ b/solution.py
@@ -18,7 +18,7 @@
 F32 = jnp.float32
 GAINS = 16
 VMEM_LIMIT = 63 * 1024 * 1024
-SMALL_LIMIT = 62 * 1024 * 1024
+SMALL_LIMIT = 59 * 1024 * 1024
 
 ROWS = {"ein": 3 * D, "eout": D, "nin": 2 * D, "nout": D}
 GROUPS = {"node": ("nin", "nout"), "edge": ("ein", "eout")}
@@ -137,8 +137,11 @@
                 self.inner[name] = at
                 at += self.half[name]
 
-    def span(self, group):
-        return slice(self.base[group], self.base[group] + self.shards * self.size[group])
+    def parcel(self, group):
+        return slice(0, self.gains) if group == "node" else slice(self.gains, self.rows)
+
+    def extent(self, group):
+        return (0 if group == "node" else GAINS), self.shards * self.size[group]
 
 
 def emit(value, name, first_row, layout, group, store, core, slots):
@@ -374,14 +377,14 @@
 
 
 def back_outs(copies, layout, store, outs, work):
-    d_own, d_edges, sent, keep, send = outs
+    d_own, d_edges, sent, *ends = outs
     d_own_s, d_edges_s, room = work
 
     def ready(group):
-        first = layout.base[group] if group == "node" else layout.gains
-        rows = pl.ds(first, layout.span(group).stop - first)
-        copies.send(store.at[1, rows], send.at[rows])
-        copies.send(store.at[0, rows], keep.at[rows])
+        i, rows = list(GROUPS).index(group), layout.parcel(group)
+        rows = pl.ds(rows.start, rows.stop - rows.start)
+        copies.send(store.at[1, rows], ends[2 + i])
+        copies.send(store.at[0, rows], ends[i])
 
     def finish():
         copies.send(room, sent)
@@ -395,7 +398,7 @@
 def second_kernel(shards, count, src, dst, lists, g_mine, g_other, nodes, latents, cots, *rest):
     halo, mine, other, rest = rest[0], rest[1:5], rest[5:9], rest[9:]
     (node_out, edge_out, gain_out), rest = rest[:3], rest[3:]
-    outs, rest = rest[:5], rest[5:]
+    outs, rest = rest[:7], rest[7:]
     held, rest = rest[:4], rest[4:]
     table, edges, saved, rates, room, node_new, edge_new, cot, rest = *rest[:8], rest[8:]
     d_outer, d_pre, store, *work, sems = rest
@@ -440,7 +443,7 @@
     d_edges_in, saved_in, rate_in, *rest
 ):
     halo, back, mine, other, rest = rest[0], rest[1], rest[2:6], rest[6:10], rest[10:]
-    outs, rest = rest[:5], rest[5:]
+    outs, rest = rest[:7], rest[7:]
     held, rest = rest[:4], rest[4:]
     table, edges, saved, rates, room, cot_own, cot_edge, got, rest = *rest[:8], rest[8:]
     d_outer, d_pre, store, *work, sems = rest
@@ -720,17 +723,16 @@
     layout = Layout(shards)
 
     def group_rows(values):
-        return [
-            Rows(layout.base[g], shards * layout.size[g], values) for g in GROUPS
-        ]
-
-    share = shape((layout.rows, D), BF)
+        return [Rows(*layout.extent(g), v) for g, v in zip(GROUPS, values)]
+
+    parcels = [layout.parcel(g) for g in GROUPS]
+    share = [shape((p.stop - p.start, D), BF) for p in parcels]
     back_shapes = [
         shape((NODE_DEV, D), F32),
         shape((rows, D), BF),
         halo_shape,
-        share,
-        share,
+        *share,
+        *share,
     ]
     back_s = [
         edge_s,
@@ -750,16 +752,16 @@
         44 * 10**6,
         VMEM_LIMIT,
     )(*small, node_one, edge_one, node_cot, halo_one, *mine, *other)
-    d_own, d_edges, sent, keep_one, send_one = done
+    d_own, d_edges, sent, *ends = done
     back = exchange(sent)
-    one = keep_one, other_core(send_one)
+    one = [(k, other_core(v)) for k, v in zip(ends[:2], ends[2:])]
     if shards > 1:
         one = group_rows(one)
         gone = [summed(*p.upper()) for p in one]
         (back,) = tied([back], gone)
         got = [receive([p], across(v, a)) for p, v, a in zip(one, gone, (1, 2))]
 
-    d_own, d_edges, sent, keep_zero, send_zero = call(
+    d_own, d_edges, sent, *ends = call(
         functools.partial(third_kernel, shards),
         small_specs + [VMEM] + [ANY] * (6 + 2 + 8),
         back_shapes,
@@ -773,69 +775,77 @@
         back, *mine, *other,
     )
 
-    if shards > 1:
-        (send_zero,) = tied([send_zero], got)
-        zero = keep_zero, other_core(send_zero)
-        sums = Rows(layout.gains, GAINS, zero)
-        nodes, edges = group_rows(zero)
-        gone = combine(
-            [sent_parts(one), (BF, [edges.upper()]), (BF, [nodes.upper(), sums.whole()])]
-        )
-        receive(one, across(gone[0], 4))
-        receive([edges], across(gone[1], 2))
-        receive([nodes, sums], across(gone[2], 1))
-        gone = combine(
-            [(BF, [edges.upper()]), (BF, [nodes.upper(), sums.whole()]), sent_parts(one)]
-        )
-        (sent,) = tied([sent], gone)
-        back = exchange(sent)
-        receive([edges], across(gone[0], 1))
-        receive([nodes, sums], across(gone[1], 2))
-        receive(one, across(gone[2], 8))
-        zero = [sums, nodes, edges]
-        far = [
-            [p.quarter(i) if p.rows > GAINS else p.whole() for p in zero] for i in range(4)
-        ]
-        *far, stay = combine([*[(BF, v) for v in far[1:]], (F32, far[0])])
-        got = [across(v, 4 * i) for i, v in enumerate(far, 1)]
-        got_one = tied([one[1].terms.pop()[0]], far)[0]
-        one[0].terms.pop()
-        receive(one, got_one)
-        near = [p.upper() for p in one]
-        near_n, near_e, stay_one = combine(
-            [*[(BF, [v]) for v in near], (F32, [p.whole() for p in one])]
-        )
-        near = [across(near_n, 2), across(near_e, 1)]
-        zero = added([stay, *got])
-        one = added([stay_one, jnp.concatenate(near, axis=0)])
-        sums, zero = zero[:GAINS], zero[GAINS:]
-        (back,) = tied([back], far)
-    else:
-        back = exchange(sent)
-        zero = keep_zero, other_core(send_zero)
-        rows = slice(layout.gains, layout.gains + GAINS)
-        sums = lax.psum(added([v[rows] for v in zero]), ("dom", "rep"))
-        one, zero = (
-            jnp.concatenate([added([v[layout.span(g)] for v in x]) for g in GROUPS], axis=0)
-            for x in (one, zero)
-        )
-
-    d_nodes = call(
-        last_kernel,
-        [VMEM] * 3,
-        shape((NODE_DEV, D), BF),
-        VMEM,
-        [],
-        10**7,
-        7 * 10**6,
-    )(send_index, d_own, back)
-
     def paired(gradient, latent):
         got = other_core(jnp.where(first, latent, gradient))
         low = jnp.where(first, gradient, got)
         high = jnp.where(first, got, latent)
         return jnp.stack([low, high])[None]
 
+    def own_gradient(back):
+        return call(
+            last_kernel,
+            [VMEM] * 3,
+            shape((NODE_DEV, D), BF),
+            VMEM,
+            [],
+            10**7,
+            7 * 10**6,
+        )(send_index, d_own, back)
+
+    if shards > 1:
+        send_e, send_n = tied([ends[3], ends[2]], got)
+        one_gone = jnp.concatenate([summed(*p.upper()) for p in one], axis=0)
+        receive(one, across(one_gone, 4))
+        got_e, got_n = other_core(send_e), other_core(send_n)
+        (got_e,) = tied([got_e], [one_gone])
+        sums = Rows(0, GAINS, (ends[1], got_e))
+        nodes, edges = group_rows([(ends[0], got_n), (ends[1], got_e)])
+        gone = summed(*edges.upper())
+        receive([edges], across(gone, 2))
+        nodes.terms[-1] = (tied([got_n], [gone])[0], 0)
+        gone = jnp.concatenate([summed(*nodes.upper()), summed(*sums.whole())], axis=0)
+        got = receive([nodes, sums], across(gone, 1))
+        d_edges, edge_two = tied([d_edges, edge_two], [gone])
+        one_gone = jnp.concatenate([summed(*p.upper()) for p in one], axis=0)
+        receive(one, across(one_gone, 8))
+        (got,) = tied([got], [one_gone])
+        nodes.terms[-1], sums.terms[-1] = (got, 0), (got, nodes.rows)
+        gone = combine([(BF, [edges.upper()]), (BF, [nodes.upper(), sums.whole()])])
+        (sent,) = tied([sent], gone)
+        back = exchange(sent)
+        receive([edges], across(gone[0], 1))
+        receive([nodes, sums], across(gone[1], 2))
+        zero = [sums, nodes, edges]
+        far = [
+            [p.quarter(i) if p.rows > GAINS else p.whole() for p in zero] for i in range(4)
+        ]
+        near = [p.upper() for p in one]
+        *far, stay, near_n, near_e, stay_one = combine(
+            [
+                *[(BF, v) for v in far[1:]],
+                (F32, far[0]),
+                *[(BF, [v]) for v in near],
+                (F32, [p.whole() for p in one]),
+            ]
+        )
+        got = [across(v, 4 * i) for i, v in enumerate(far, 1)]
+        near = [across(near_n, 2), across(near_e, 1)]
+        zero = added([stay, *got])
+        (back,) = tied([back], far)
+        node_pair = paired(own_gradient(back), node_two)
+        one = added([stay_one, jnp.concatenate(near, axis=0)])
+        sums, zero = zero[:GAINS], zero[GAINS:]
+    else:
+        node_pair = paired(own_gradient(exchange(sent)), node_two)
+        zero = [(k, other_core(v)) for k, v in zip(ends[:2], ends[2:])]
+        sums = lax.psum(added([v[:GAINS] for v in zero[1]]), ("dom", "rep"))
+        one, zero = (
+            jnp.concatenate([added([v[-layout.extent(g)[1] :] for v in y]) for g, y in zip(GROUPS, x)])
+            for x in (one, zero)
+        )
+
+
+    edge_pair = paired(d_edges, edge_two)
     factor = float(micro * reps * NODE_DEV * doms) ** (-0.5)
     got = other_core(jnp.where(first, one, zero))
     at, places = 0, {}
@@ -873,8 +883,8 @@
     width = D // (doms * reps)
     sums = lax.dynamic_slice_in_dim(sums[:2], (part * reps + rep) * width, width, axis=1) * factor
     return (
-        paired(d_nodes, node_two),
-        paired(d_edges, edge_two),
+        node_pair,
+        edge_pair,
         grads["ein"][None],
         grads["eout"][None],
         grads["nin"][None],

time: 129 us -> 124 us (0.961)
  Pallas kernels: 40.9 us -> 36 us
  waiting for transfers between devices: 18.5 us -> 15.5 us
  other arithmetic: 9.83 us -> 12.8 us
  local copies, waits for them, and re-layouts: 10.3 us -> 8.87 us
    ppermute x9, waiting for transfers between devices: 1.06 us -> 11.2 us  [across(): lax.ppermute(value, 'dom', [(p, p ^ step) for p in range(lax.axis_size('d...]
    ppermute x4, waiting for transfers between devices: 9.02 us -> 0.08 us  [across(): return lax.ppermute(value, 'rep', [(0, 1), (1, 0)])]
    pallas_call x4 -> x2, Pallas kernels: 10.5 us -> 5.66 us  [combine(): call(kernel, [ANY] * len(arrays), [shape(*s) for s in shapes], [ANY] * le...]
    ppermute x10 -> x12, waiting for transfers between devices: 4.61 us -> 0.03 us  [other_core(): return lax.ppermute(value, 'segment', [(0, 1), (1, 0)])]
    convert_element_type x2 -> x9, other arithmetic: 4.2 us -> 8.2 us  [summed(): return added([a[first:first + rows] for a, first in terms]).astype(BF)]
    unnamed x40 -> x54, local copies, waits for them, and re-layouts: 7.28 us -> 5.82 us
  transfers between devices with their start and end apart: 26 -> 28, of which waited for: 8 -> 6; matrix products, arithmetic and copies ran while one was open for 10% -> 13% of each run, Pallas kernels for 16% -> 15%
where the time goes in v4:
time: 124 us; the launch traced here: 123 us
  starting transfers between devices  36.7 us (30%)
  Pallas kernels  36 us (29%)
  waiting for transfers between devices  15.5 us (12%)
  other arithmetic  12.8 us (10%)
  blocking collectives  11.3 us (9%)
  local copies, waits for them, and re-layouts  8.87 us (7%)
  between operations  1.72 us (1%)
    ppermute x9, starting transfers between devices, across(): lax.ppermute(value, 'dom', [(p, p ^ step) for p in range(lax.axis_size('d...  14.9 us
    all_to_all x3, starting transfers between devices, exchange(): return lax.all_to_all(rows, 'dom', 0, 0, tiled=True)  14 us
    all_to_all x1, blocking collectives, exchange(): return lax.all_to_all(rows, 'dom', 0, 0, tiled=True)  11.3 us
    ppermute x9, waiting for transfers between devices, across(): lax.ppermute(value, 'dom', [(p, p ^ step) for p in range(lax.axis_size('d...  11.2 us
    pallas_call x1, Pallas kernels, body(): call(functools.partial(second_kernel, shards), small_specs + [ANY] * (3 +...  10.8 us
    convert_element_type x9, other arithmetic, summed(): return added([a[first:first + rows] for a, first in terms]).astype(BF)  8.2 us
    pallas_call x1, Pallas kernels, body(): call(functools.partial(third_kernel, shards), small_specs + [VMEM] + [ANY...  8.06 us
    pallas_call x1, Pallas kernels, body(): call(first_kernel, small_specs + [ANY] * (2 + 1 + 8), [shape((NODE_DEV, D...  6.3 us
  transfers between devices with their start and end apart: 28, of which 6 were waited for; matrix products, arithmetic and copies ran while one was open for 13% of the time, Pallas kernels for 15%

profile of v4, /device:TPU:0, one launch (start us, length us, event | category | flops | bytes accessed | tf_op | source)
XLA Modules:
  0.0 122.9 jit_solution(3719517044321730732)
XLA Ops:
  1.7 2.5 %shard_map.188 = bf16[128,512]{1,0:T(8,128)(2,1)} custom-call(s32[1,4,16]{2,1,0:T(4,128)} %lists.9, bf16[2,128,512]{2,1,0:T(8,128)(2,1)} %nodes.5), custom_call_target="tpu_custom_call" | custom-call | flops 10000000 | bytes 7000000 | tf_op jit(solution)/shard_map/pallas_call | solution.py:679
  4.2 7.3 %all-to-all-start = ((bf16[8,16,512]{2,1,0:T(8,128)(2,1)}), bf16[8,16,512]{2,1,0:T(8,128)(2,1)S(1)}, u32[]{:S(2)}, u32[]{:S(2)}) async-start(bf16[8,16,512]{2,1,0:T(8,128)(2,1)} %bitcast.27), calls=%async_computation | async-start | bytes 262144 | tf_op jit(solution)/shard_map/all_to_all | solution.py:528
  11.5 0.7 pad_maximum_fusion.3.g_mine
  12.9 1.3 %broadcast_in_dim.24.src = s32[1,384]{1,0:T(1,128)} reshape(s32[384]{0:T(512)} %param.16) | data formatting | bytes 3072 | tf_op jit(solution)/shard_map/broadcast_in_dim | solution.py:673
  14.2 1.3 %broadcast_in_dim.25.dst = s32[1,384]{1,0:T(1,128)} reshape(s32[384]{0:T(512)} %param.17) | data formatting | bytes 3072 | tf_op jit(solution)/shard_map/broadcast_in_dim | solution.py:673
  15.5 3.4 %all-to-all-done = bf16[8,16,512]{2,1,0:T(8,128)(2,1)S(1)} async-done(((bf16[8,16,512]{2,1,0:T(8,128)(2,1)}), bf16[8,16,512]{2,1,0:T(8,128)(2,1)S(1)}, u32[]{:S(2)}, u32[]{:S(2)}) %all-to-all-start) | async-done | bytes 131104 | tf_op jit(solution)/shard_map/all_to_all | solution.py:528
  19.7 6.3 %shard_map.189 = (bf16[128,512]{1,0:T(8,128)(2,1)}, bf16[384,512]{1,0:T(8,128)(2,1)}, bf16[1664,512]{1,0:T(8,128)(2,1)}, f32[512,128]{1,0:T(8,128)}, bf16[128,512]{1,0:T(8,128)(2,1)}) custom-call(s32[1]{0:T(128)S(6)} %copy.21.count, s32[1,384]{1,0:T(1,128)} %broadcast_in_dim.24.src, s32[1,384]{1,0:T(1,128)} %broadcast_in_dim.25.dst, s32[1,4,16]{2,1,0:T(4,128)} %lists.9, ...), custom_call_target="tpu_custom_call" | custom-call | flops 1100000000 | bytes 26000000 | tf_op jit(solution)/shard_map/pallas_call | solution.py:705
  26.0 11.3 %all_to_all.46 = bf16[8,16,512]{2,1,0:T(8,128)(2,1)} all-to-all(bf16[8,16,512]{2,1,0:T(8,128)(2,1)} %bitcast.31), channel_id=1, replica_groups=mesh['segment'=2,'dom'=8,'rep'=2] {'dom'}, dimensions={0} | all-to-all | bytes 262144 | tf_op jit(solution)/shard_map/all_to_all | solution.py:528
  37.4 10.8 %shard_map.190 = (bf16[128,512]{1,0:T(8,128)(2,1)}, bf16[384,512]{1,0:T(8,128)(2,1)}, f32[16,512]{1,0:T(8,128)}, f32[128,512]{1,0:T(8,128)}, bf16[384,512]{1,0:T...) custom-call(s32[1]{0:T(128)S(6)} %copy.21.count, ...), custom_call_target="tpu_custom_call" | custom-call | flops 2800000000 | bytes 44000000 | tf_op jit(solution)/shard_map/pallas_call | solution.py:745
  48.8 3.4 %all-to-all-start.2 = ((bf16[8,16,512]{2,1,0:T(8,128)(2,1)}), bf16[8,16,512]{2,1,0:T(8,128)(2,1)S(1)}, u32[]{:S(2)}, u32[]{:S(2)}) async-start(bf16[8,16,512]{2,1,0:T(8,128)(2,1)} %bitcast.29), calls=%async_computation.2 | async-start | bytes 262144 | tf_op jit(solution)/shard_map/all_to_all | solution.py:528
  52.2 2.3 %add_convert_fusion.1 = bf16[512,512]{1,0:T(8,128)(2,1)} fusion(bf16[1040,512]{1,0:T(8,128)(2,1)S(1)} %collective-permute-done.6.refs_14_, bf16[1040,512]{1,0:T(8,128)(2,1)} %get-tuple-element.64.refs_13_), kind=kLoop, calls=%fused_computation.1 | loop fusion | flops 1048576 | bytes 1572864 | tf_op jit(solution)/shard_map/convert_element_type | solution.py:635
  54.5 1.9 %collective-permute-start.8 = (bf16[512,512]{1,0:T(8,128)(2,1)}, bf16[512,512]{1,0:T(8,128)(2,1)}, u32[]{:S(2)}, u32[]{:S(2)}) collective-permute-start(bf16[512,512]{1,0:T(8,128)(2,1)} %add_convert_fusion.1), channel_id=1, source_target_pairs={{0,2},{2,0},{4,6},{6,4},{8,10},{10,8},{12,14},{14,12},{1,3},{3,1},... | collective-permute-start | bytes 1572872 | tf_op jit(solution)/shard_map/ppermute | solution.py:539
  56.4 1.0 add_convert_fusion.3
  57.4 1.5 %collective-permute-start.7 = (bf16[384,512]{1,0:T(8,128)(2,1)}, bf16[384,512]{1,0:T(8,128)(2,1)}, u32[]{:S(2)}, u32[]{:S(2)}) collective-permute-start(bf16[384,512]{1,0:T(8,128)(2,1)} %add_convert_fusion.3), channel_id=1, source_target_pairs={{0,1},{1,0},{2,3},{3,2},{4,5},{5,4},{6,7},{7,6},{8,9},{9,8},{10,11... | collective-permute-start | bytes 1179656 | tf_op jit(solution)/shard_map/ppermute | solution.py:537
  58.9 0.8 all-to-all-done.2
  59.7 0.7 copy-done.17
  60.4 8.1 %shard_map.191 = (f32[128,512]{1,0:T(8,128)}, bf16[384,512]{1,0:T(8,128)(2,1)}, bf16[128,512]{1,0:T(8,128)(2,1)}, bf16[768,512]{1,0:T(8,128)(2,1)}, bf16[1040,51...) custom-call(s32[1]{0:T(128)S(6)} %copy.21.count, s32[1,384]{1,0:T(1,128)} %broadcast_in_dim.24.src, ...), custom_call_target="tpu_custom_call" | custom-call | flops 1800000000 | bytes 37000000 | tf_op jit(solution)/shard_map/pallas_call | solution.py:764
  68.4 0.8 collective-permute-done.8.refs_15_
  69.8 1.1 add_convert_fusion.5
  70.9 1.3 %add_convert_fusion.4 = bf16[256,512]{1,0:T(8,128)(2,1)S(1)} fusion(bf16[512,512]{1,0:T(8,128)(2,1)} %collective-permute-done.8.refs_15_, bf16[1040,512]{1,0:T(8,128)(2,1)} %copy-done.4, bf16[1040,512]{1,0:T(8,128)(2,1)} %get-tuple-element.64.refs_13_), kind=kLoop, calls=%fused_computation.5 | loop fusion | flops 786432 | bytes 1048576 | tf_op jit(solution)/shard_map/convert_element_type | solution.py:635
  72.2 1.5 %collective-permute-start.13 = (bf16[448,512]{1,0:T(8,128)(2,1)S(1)}, bf16[448,512]{1,0:T(8,128)(2,1)S(1)}, u32[]{:S(2)}, u32[]{:S(2)}) collective-permute-start(bf16[448,512]{1,0:T(8,128)(2,1)S(1)} %pad_maximum_fusion), channel_id=1, source_target_pairs={{0,4},{2,6},{4,0},{6,2},{8,12},{10,14},{12,8},{14,10},{1,5},{3,7},... | collective-permute-start | bytes 1376264 | tf_op jit(solution)/shard_map/ppermute | solution.py:539
  73.9 1.4 %collective-permute-start.10 = (bf16[512,512]{1,0:T(8,128)(2,1)S(1)}, bf16[512,512]{1,0:T(8,128)(2,1)S(1)}, u32[]{:S(2)}, u32[]{:S(2)}) collective-permute-start(bf16[512,512]{1,0:T(8,128)(2,1)S(1)} %add_convert_fusion), channel_id=1, source_target_pairs={{0,2},{2,0},{4,6},{6,4},{8,10},{10,8},{12,14},{14,12},{1,3},{3,1},... | collective-permute-start | bytes 1572872 | tf_op jit(solution)/shard_map/ppermute | solution.py:539
  75.4 1.6 %collective-permute-start.12 = (bf16[400,512]{1,0:T(8,128)(2,1)S(1)}, bf16[400,512]{1,0:T(8,128)(2,1)S(1)}, u32[]{:S(2)}, u32[]{:S(2)}) collective-permute-start(bf16[400,512]{1,0:T(8,128)(2,1)S(1)} %pad_maximum_fusion.1), channel_id=1, source_target_pairs={{0,1},{1,0},{2,3},{3,2},{4,5},{5,4},{6,7},{7,6},{8,9},{9,8},{10,11... | collective-permute-start | bytes 1228808 | tf_op jit(solution)/shard_map/ppermute | solution.py:537
  77.0 0.8 broadcast_select_fusion
  77.8 6.9 %collective-permute-done.13.refs_11_ = bf16[448,512]{1,0:T(8,128)(2,1)S(1)} collective-permute-done((bf16[448,512]{1,0:T(8,128)(2,1)S(1)}, bf16[448,512]{1,0:T(8,128)(2,1)S(1)}, u32[]{:S(2)}, u32[]{:S(2)}) %collective-permute-start.13) | collective-permute-done | bytes 458784 | tf_op jit(solution)/shard_map/ppermute | solution.py:539
  84.7 1.2 add_convert_fusion.7
  85.9 1.1 add_convert_fusion.6
  87.0 2.2 %collective-permute-start.16 = (bf16[224,512]{1,0:T(8,128)(2,1)S(1)}, bf16[224,512]{1,0:T(8,128)(2,1)S(1)}, u32[]{:S(2)}, u32[]{:S(2)}) collective-permute-start(bf16[224,512]{1,0:T(8,128)(2,1)S(1)} %pad_maximum_fusion.2), channel_id=1, source_target_pairs={{0,8},{2,10},{4,12},{6,14},{8,0},{10,2},{12,4},{14,6},{1,9},{3,11}... | collective-permute-start | bytes 688136 | tf_op jit(solution)/shard_map/ppermute | solution.py:539
  89.3 0.7 copy-done.9
  90.0 0.9 copy-done.8
  90.9 2.1 %shard_map.192 = (bf16[256,512]{1,0:T(8,128)(2,1)}, bf16[208,512]{1,0:T(8,128)(2,1)}) custom-call(bf16[1040,512]{1,0:T(8,128)(2,1)} %get-tuple-element.69.refs_0_, bf16[1040,512]{1,0:T(8,128)(2,1)} %copy-done.1, bf16[512,512]{1,0:T(8,128)(2,1)} %copy-done.8, bf16[768,512]{1,0:T(8,128)(2,1)} %get-tuple-element.74.refs_3_.refs_4_, bf16[768,512]{1,0:T(8,128)(2,1)} %copy-done.3, ...), custom_call_target="tpu_custom_call" | custom-call | flops 1000000 | bytes 8000000 | tf_op jit(solution)/shard_map/pallas_call | solution.py:618
  93.0 1.4 %collective-permute-start.14 = (bf16[208,512]{1,0:T(8,128)(2,1)}, bf16[208,512]{1,0:T(8,128)(2,1)S(1)}, u32[]{:S(2)}, u32[]{:S(2)}) collective-permute-start(bf16[208,512]{1,0:T(8,128)(2,1)} %get-tuple-element.79), channel_id=1, source_target_pairs={{0,2},{2,0},{4,6},{6,4},{8,10},{10,8},{12,14},{14,12},{1,3},{3,1},... | collective-permute-start | bytes 638984 | tf_op jit(solution)/shard_map/ppermute | solution.py:539
  94.4 1.5 %collective-permute-start.15 = (bf16[256,512]{1,0:T(8,128)(2,1)}, bf16[256,512]{1,0:T(8,128)(2,1)S(1)}, u32[]{:S(2)}, u32[]{:S(2)}) collective-permute-start(bf16[256,512]{1,0:T(8,128)(2,1)} %get-tuple-element.78), channel_id=1, source_target_pairs={{0,1},{1,0},{2,3},{3,2},{4,5},{5,4},{6,7},{7,6},{8,9},{9,8},{10,11... | collective-permute-start | bytes 786440 | tf_op jit(solution)/shard_map/ppermute | solution.py:537
  95.9 3.4 %all-to-all-start.3 = ((bf16[8,16,512]{2,1,0:T(8,128)(2,1)}), bf16[8,16,512]{2,1,0:T(8,128)(2,1)S(1)}, u32[]{:S(2)}, u32[]{:S(2)}) async-start(bf16[8,16,512]{2,1,0:T(8,128)(2,1)} %bitcast.6), calls=%async_computation.3 | async-start | bytes 262144 | tf_op jit(solution)/shard_map/all_to_all | solution.py:528
  99.3 1.1 select_bitcast_fusion.1
  100.4 0.9 maximum_bitcast_fusion
  102.1 0.7 copy-done.21
  102.8 3.5 %shard_map.193 = (bf16[128,512]{1,0:T(8,128)(2,1)}, bf16[128,512]{1,0:T(8,128)(2,1)}, bf16[128,512]{1,0:T(8,128)(2,1)}, f32[128,512]{1,0:T(8,128)}, bf16[48,512]...) custom-call(bf16[1040,512]{1,0:T(8,128)(2,1)} %get-tuple-element.69.refs_0_, ...), custom_call_target="tpu_custom_call" | custom-call | flops 1000000 | bytes 8000000 | tf_op jit(solution)/shard_map/pallas_call | solution.py:618
  106.4 3.8 %collective-permute-start.23 = (bf16[128,512]{1,0:T(8,128)(2,1)}, bf16[128,512]{1,0:T(8,128)(2,1)S(1)}, u32[]{:S(2)}, u32[]{:S(2)}) collective-permute-start(bf16[128,512]{1,0:T(8,128)(2,1)} %get-tuple-element.83), channel_id=1, source_target_pairs={{0,12},{2,14},{4,8},{6,10},{8,4},{10,6},{12,0},{14,2},{1,13},{3,15... | collective-permute-start | bytes 393224 | tf_op jit(solution)/shard_map/ppermute | solution.py:539
  110.2 0.6 collective-permute-start.21
  110.8 0.7 copy-done.19
  111.5 1.9 %shard_map.194 = bf16[128,512]{1,0:T(8,128)(2,1)} custom-call(s32[1,4,16]{2,1,0:T(4,128)} %lists.9, f32[128,512]{1,0:T(8,128)} %get-tuple-element.67.d_own, bf16[128,512]{1,0:T(8,128)(2,1)} %bitcast.28), custom_call_target="tpu_custom_call" | custom-call | flops 10000000 | bytes 7000000 | tf_op jit(solution)/shard_map/pallas_call | solution.py:785
  113.5 0.9 collective-permute-start.20
  114.4 2.0 %collective-permute-start.19 = (bf16[48,512]{1,0:T(8,128)(2,1)}, bf16[48,512]{1,0:T(8,128)(2,1)S(1)}, u32[]{:S(2)}, u32[]{:S(2)}) collective-permute-start(bf16[48,512]{1,0:T(8,128)(2,1)} %get-tuple-element.91), channel_id=1, source_target_pairs={{0,2},{2,0},{4,6},{6,4},{8,10},{10,8},{12,14},{14,12},{1,3},{3,1},... | collective-permute-start | bytes 147464 | tf_op jit(solution)/shard_map/ppermute | solution.py:539
  116.5 3.4 %collective-permute-done.22 = bf16[128,512]{1,0:T(8,128)(2,1)S(1)} collective-permute-done((bf16[128,512]{1,0:T(8,128)(2,1)}, bf16[128,512]{1,0:T(8,128)(2,1)S(1)}, u32[]{:S(2)}, u32[]{:S(2)}) %collective-permute-start.22) | collective-permute-done | bytes 131104 | tf_op jit(solution)/shard_map/ppermute | solution.py:539
  120.1 0.6 copy-done.15
  120.8 0.7 maximum_bitcast_fusion.1
  122.1 0.8 shard_map.195
  (97 shorter events, 5.3 us)
Async XLA Ops:
  0.6 18.2 %collective-permute-start.1 = (bf16[1,1536,512]{2,1,0:T(8,128)(2,1)}, bf16[1,1536,512]{2,1,0:T(8,128)(2,1)}, u32[]{:S(2)}, u32[]{:S(2)}) collective-permute-start(bf16[1,1536,512]{2,1,0:T(8,128)(2,1)} %rest_2_.5), channel_id=1, source_target_pairs={{0,16},{16,0},{1,17},{17,1},{2,18},{18,2},{3,19},{19,3},{4,20},{20... | collective-permute-start | bytes 4718600 | tf_op jit(solution)/shard_map/ppermute | solution.py:532
  1.1 17.7 %collective-permute-start.3 = (bf16[1,1024,512]{2,1,0:T(8,128)(2,1)}, bf16[1,1024,512]{2,1,0:T(8,128)(2,1)}, u32[]{:S(2)}, u32[]{:S(2)}) collective-permute-start(bf16[1,1024,512]{2,1,0:T(8,128)(2,1)} %rest_4_.5), channel_id=1, source_target_pairs={{0,16},{16,0},{1,17},{17,1},{2,18},{18,2},{3,19},{19,3},{4,20},{20... | collective-permute-start | bytes 3145736 | tf_op jit(solution)/shard_map/ppermute | solution.py:532
  1.2 17.6 %collective-permute-start.2 = (bf16[1,512,512]{2,1,0:T(8,128)(2,1)}, bf16[1,512,512]{2,1,0:T(8,128)(2,1)S(1)}, u32[]{:S(2)}, u32[]{:S(2)}) collective-permute-start(bf16[1,512,512]{2,1,0:T(8,128)(2,1)} %rest_3_.5), channel_id=1, source_target_pairs={{0,16},{16,0},{1,17},{17,1},{2,18},{18,2},{3,19},{19,3},{4,20},{20... | collective-permute-start | bytes 1572872 | tf_op jit(solution)/shard_map/ppermute | solution.py:532
  1.7 17.2 %collective-permute-start.4 = (bf16[1,512,512]{2,1,0:T(8,128)(2,1)}, bf16[1,512,512]{2,1,0:T(8,128)(2,1)}, u32[]{:S(2)}, u32[]{:S(2)}) collective-permute-start(bf16[1,512,512]{2,1,0:T(8,128)(2,1)} %rest_5_.1), channel_id=1, source_target_pairs={{0,16},{16,0},{1,17},{17,1},{2,18},{18,2},{3,19},{19,3},{4,20},{20... | collective-permute-start | bytes 1572872 | tf_op jit(solution)/shard_map/ppermute | solution.py:532
  4.2 14.6 %all-to-all-start = ((bf16[8,16,512]{2,1,0:T(8,128)(2,1)}), bf16[8,16,512]{2,1,0:T(8,128)(2,1)S(1)}, u32[]{:S(2)}, u32[]{:S(2)}) async-start(bf16[8,16,512]{2,1,0:T(8,128)(2,1)} %bitcast.27), calls=%async_computation | async-start | bytes 262144 | tf_op jit(solution)/shard_map/all_to_all | solution.py:528
  12.2 6.7 %copy-start.25 = (f32[2,512]{1,0:T(2,128)}, f32[2,512]{1,0:T(2,128)S(1)}, u32[]{:S(2)}) copy-start(f32[2,512]{1,0:T(2,128)S(1)} %pad_maximum_fusion.3.g_mine) | copy-start | bytes 12292
  12.2 3.3 %collective-permute-start = (f32[2,512]{1,0:T(2,128)S(1)}, f32[2,512]{1,0:T(2,128)S(1)}, u32[]{:S(2)}, u32[]{:S(2)}) collective-permute-start(f32[2,512]{1,0:T(2,128)S(1)} %pad_maximum_fusion.3.g_mine), channel_id=1, source_target_pairs={{0,16},{16,0},{1,17},{17,1},{2,18},{18,2},{3,19},{19,3},{4,20},{20... | collective-permute-start | bytes 12296 | tf_op jit(solution)/shard_map/ppermute | solution.py:532
  15.5 3.4 %copy-start.26 = (f32[2,512]{1,0:T(2,128)}, f32[2,512]{1,0:T(2,128)S(1)}, u32[]{:S(2)}) copy-start(f32[2,512]{1,0:T(2,128)S(1)} %collective-permute-done.g_other) | copy-start | bytes 12292
  18.9 0.9 copy-start.7
  48.2 8.2 %copy-start.5 = (bf16[768,512]{1,0:T(8,128)(2,1)S(1)}, bf16[768,512]{1,0:T(8,128)(2,1)}, u32[]{:S(2)}) copy-start(bf16[768,512]{1,0:T(8,128)(2,1)} %get-tuple-element.62.refs_8_) | copy-start | bytes 2359300
  48.2 4.0 %collective-permute-start.6 = (bf16[1040,512]{1,0:T(8,128)(2,1)}, bf16[1040,512]{1,0:T(8,128)(2,1)S(1)}, u32[]{:S(2)}, u32[]{:S(2)}) collective-permute-start(bf16[1040,512]{1,0:T(8,128)(2,1)} %get-tuple-element.65), channel_id=1, source_target_pairs={{0,16},{16,0},{1,17},{17,1},{2,18},{18,2},{3,19},{19,3},{4,20},{20... | collective-permute-start | bytes 3194888 | tf_op jit(solution)/shard_map/ppermute | solution.py:532
  48.3 8.1 %collective-permute-start.5 = (bf16[768,512]{1,0:T(8,128)(2,1)}, bf16[768,512]{1,0:T(8,128)(2,1)S(1)}, u32[]{:S(2)}, u32[]{:S(2)}) collective-permute-start(bf16[768,512]{1,0:T(8,128)(2,1)} %get-tuple-element.63), channel_id=1, source_target_pairs={{0,16},{16,0},{1,17},{17,1},{2,18},{18,2},{3,19},{19,3},{4,20},{20... | collective-permute-start | bytes 2359304 | tf_op jit(solution)/shard_map/ppermute | solution.py:532
  48.8 10.9 %all-to-all-start.2 = ((bf16[8,16,512]{2,1,0:T(8,128)(2,1)}), bf16[8,16,512]{2,1,0:T(8,128)(2,1)S(1)}, u32[]{:S(2)}, u32[]{:S(2)}) async-start(bf16[8,16,512]{2,1,0:T(8,128)(2,1)} %bitcast.29), calls=%async_computation.2 | async-start | bytes 262144 | tf_op jit(solution)/shard_map/all_to_all | solution.py:528
  52.2 5.2 %copy-start.4 = (bf16[1040,512]{1,0:T(8,128)(2,1)}, bf16[1040,512]{1,0:T(8,128)(2,1)S(1)}, u32[]{:S(2)}) copy-start(bf16[1040,512]{1,0:T(8,128)(2,1)S(1)} %collective-permute-done.6.refs_14_) | copy-start | bytes 3194884
  54.5 14.7 %collective-permute-start.8 = (bf16[512,512]{1,0:T(8,128)(2,1)}, bf16[512,512]{1,0:T(8,128)(2,1)}, u32[]{:S(2)}, u32[]{:S(2)}) collective-permute-start(bf16[512,512]{1,0:T(8,128)(2,1)} %add_convert_fusion.1), channel_id=1, source_target_pairs={{0,2},{2,0},{4,6},{6,4},{8,10},{10,8},{12,14},{14,12},{1,3},{3,1},... | collective-permute-start | bytes 1572872 | tf_op jit(solution)/shard_map/ppermute | solution.py:539
  56.4 2.5 %copy-start.6 = (bf16[768,512]{1,0:T(8,128)(2,1)}, bf16[768,512]{1,0:T(8,128)(2,1)S(1)}, u32[]{:S(2)}) copy-start(bf16[768,512]{1,0:T(8,128)(2,1)S(1)} %collective-permute-done.5.refs_9_) | copy-start | bytes 2359300
  57.4 11.0 %collective-permute-start.7 = (bf16[384,512]{1,0:T(8,128)(2,1)}, bf16[384,512]{1,0:T(8,128)(2,1)}, u32[]{:S(2)}, u32[]{:S(2)}) collective-permute-start(bf16[384,512]{1,0:T(8,128)(2,1)} %add_convert_fusion.3), channel_id=1, source_target_pairs={{0,1},{1,0},{2,3},{3,2},{4,5},{5,4},{6,7},{7,6},{8,9},{9,8},{10,11... | collective-permute-start | bytes 1179656 | tf_op jit(solution)/shard_map/ppermute | solution.py:537
  69.3 4.5 %collective-permute-start.9 = (bf16[1040,512]{1,0:T(8,128)(2,1)}, bf16[1040,512]{1,0:T(8,128)(2,1)S(1)}, u32[]{:S(2)}, u32[]{:S(2)}) collective-permute-start(bf16[1040,512]{1,0:T(8,128)(2,1)} %get-tuple-element.72), channel_id=1, source_target_pairs={{0,16},{16,0},{1,17},{17,1},{2,18},{18,2},{3,19},{19,3},{4,20},{20... | collective-permute-start | bytes 3194888 | tf_op jit(solution)/shard_map/ppermute | solution.py:532
  69.3 6.0 %collective-permute-start.11 = (bf16[768,512]{1,0:T(8,128)(2,1)}, bf16[768,512]{1,0:T(8,128)(2,1)S(1)}, u32[]{:S(2)}, u32[]{:S(2)}) collective-permute-start(bf16[768,512]{1,0:T(8,128)(2,1)} %get-tuple-element.75), channel_id=1, source_target_pairs={{0,16},{16,0},{1,17},{17,1},{2,18},{18,2},{3,19},{19,3},{4,20},{20... | collective-permute-start | bytes 2359304 | tf_op jit(solution)/shard_map/ppermute | solution.py:532
  70.9 2.9 %copy-start = (bf16[1040,512]{1,0:T(8,128)(2,1)S(1)}, bf16[1040,512]{1,0:T(8,128)(2,1)}, u32[]{:S(2)}) copy-start(bf16[1040,512]{1,0:T(8,128)(2,1)} %get-tuple-element.69.refs_0_) | copy-start | bytes 3194884
  72.2 3.1 %copy-start.2 = (bf16[768,512]{1,0:T(8,128)(2,1)S(1)}, bf16[768,512]{1,0:T(8,128)(2,1)}, u32[]{:S(2)}) copy-start(bf16[768,512]{1,0:T(8,128)(2,1)} %get-tuple-element.74.refs_3_.refs_4_) | copy-start | bytes 2359300
  72.2 12.5 %collective-permute-start.13 = (bf16[448,512]{1,0:T(8,128)(2,1)S(1)}, bf16[448,512]{1,0:T(8,128)(2,1)S(1)}, u32[]{:S(2)}, u32[]{:S(2)}) collective-permute-start(bf16[448,512]{1,0:T(8,128)(2,1)S(1)} %pad_maximum_fusion), channel_id=1, source_target_pairs={{0,4},{2,6},{4,0},{6,2},{8,12},{10,14},{12,8},{14,10},{1,5},{3,7},... | collective-permute-start | bytes 1376264 | tf_op jit(solution)/shard_map/ppermute | solution.py:539
  73.7 1.7 %copy-start.1 = (bf16[1040,512]{1,0:T(8,128)(2,1)}, bf16[1040,512]{1,0:T(8,128)(2,1)S(1)}, u32[]{:S(2)}) copy-start(bf16[1040,512]{1,0:T(8,128)(2,1)S(1)} %collective-permute-done.9.refs_1_) | copy-start | bytes 3194884
  73.9 3.1 %copy-start.10 = (bf16[384,512]{1,0:T(8,128)(2,1)S(1)}, bf16[384,512]{1,0:T(8,128)(2,1)}, u32[]{:S(2)}) copy-start(bf16[384,512]{1,0:T(8,128)(2,1)} %get-tuple-element.89) | copy-start | bytes 1179652
  73.9 3.1 %copy-start.12 = (bf16[384,512]{1,0:T(8,128)(2,1)S(1)}, bf16[384,512]{1,0:T(8,128)(2,1)}, u32[]{:S(2)}) copy-start(bf16[384,512]{1,0:T(8,128)(2,1)} %get-tuple-element.88) | copy-start | bytes 1179652
  73.9 15.4 %collective-permute-start.10 = (bf16[512,512]{1,0:T(8,128)(2,1)S(1)}, bf16[512,512]{1,0:T(8,128)(2,1)S(1)}, u32[]{:S(2)}, u32[]{:S(2)}) collective-permute-start(bf16[512,512]{1,0:T(8,128)(2,1)S(1)} %add_convert_fusion), channel_id=1, source_target_pairs={{0,2},{2,0},{4,6},{6,4},{8,10},{10,8},{12,14},{14,12},{1,3},{3,1},... | collective-permute-start | bytes 1572872 | tf_op jit(solution)/shard_map/ppermute | solution.py:539
  75.3 2.5 %copy-start.3 = (bf16[768,512]{1,0:T(8,128)(2,1)}, bf16[768,512]{1,0:T(8,128)(2,1)S(1)}, u32[]{:S(2)}) copy-start(bf16[768,512]{1,0:T(8,128)(2,1)S(1)} %collective-permute-done.11.refs_4_.refs_5_) | copy-start | bytes 2359300
  75.4 13.8 %collective-permute-start.12 = (bf16[400,512]{1,0:T(8,128)(2,1)S(1)}, bf16[400,512]{1,0:T(8,128)(2,1)S(1)}, u32[]{:S(2)}, u32[]{:S(2)}) collective-permute-start(bf16[400,512]{1,0:T(8,128)(2,1)S(1)} %pad_maximum_fusion.1), channel_id=1, source_target_pairs={{0,1},{1,0},{2,3},{3,2},{4,5},{5,4},{6,7},{7,6},{8,9},{9,8},{10,11... | collective-permute-start | bytes 1228808 | tf_op jit(solution)/shard_map/ppermute | solution.py:537
  77.8 21.5 %collective-permute-start.18 = (bf16[384,512]{1,0:T(8,128)(2,1)}, bf16[384,512]{1,0:T(8,128)(2,1)}, u32[]{:S(2)}, u32[]{:S(2)}) collective-permute-start(bf16[384,512]{1,0:T(8,128)(2,1)} %broadcast_select_fusion), channel_id=1, source_target_pairs={{0,16},{16,0},{1,17},{17,1},{2,18},{18,2},{3,19},{19,3},{4,20},{20... | collective-permute-start | bytes 1179656 | tf_op jit(solution)/shard_map/ppermute | solution.py:532
  84.7 4.6 %copy-start.16 = (bf16[448,512]{1,0:T(8,128)(2,1)}, bf16[448,512]{1,0:T(8,128)(2,1)S(1)}, u32[]{:S(2)}) copy-start(bf16[448,512]{1,0:T(8,128)(2,1)S(1)} %collective-permute-done.13.refs_11_) | copy-start | bytes 1376260
  87.0 12.3 %copy-start.11 = (bf16[384,512]{1,0:T(8,128)(2,1)S(1)}, bf16[384,512]{1,0:T(8,128)(2,1)}, u32[]{:S(2)}) copy-start(bf16[384,512]{1,0:T(8,128)(2,1)} %get-tuple-element.89) | copy-start | bytes 1179652
  87.0 12.3 %copy-start.13 = (bf16[384,512]{1,0:T(8,128)(2,1)S(1)}, bf16[384,512]{1,0:T(8,128)(2,1)}, u32[]{:S(2)}) copy-start(bf16[384,512]{1,0:T(8,128)(2,1)} %get-tuple-element.88) | copy-start | bytes 1179652
  87.0 14.3 %collective-permute-start.16 = (bf16[224,512]{1,0:T(8,128)(2,1)S(1)}, bf16[224,512]{1,0:T(8,128)(2,1)S(1)}, u32[]{:S(2)}, u32[]{:S(2)}) collective-permute-start(bf16[224,512]{1,0:T(8,128)(2,1)S(1)} %pad_maximum_fusion.2), channel_id=1, source_target_pairs={{0,8},{2,10},{4,12},{6,14},{8,0},{10,2},{12,4},{14,6},{1,9},{3,11}... | collective-permute-start | bytes 688136 | tf_op jit(solution)/shard_map/ppermute | solution.py:539
  90.0 0.9 copy-start.8
  93.0 8.3 %collective-permute-start.14 = (bf16[208,512]{1,0:T(8,128)(2,1)}, bf16[208,512]{1,0:T(8,128)(2,1)S(1)}, u32[]{:S(2)}, u32[]{:S(2)}) collective-permute-start(bf16[208,512]{1,0:T(8,128)(2,1)} %get-tuple-element.79), channel_id=1, source_target_pairs={{0,2},{2,0},{4,6},{6,4},{8,10},{10,8},{12,14},{14,12},{1,3},{3,1},... | collective-permute-start | bytes 638984 | tf_op jit(solution)/shard_map/ppermute | solution.py:539
  94.4 7.0 %collective-permute-start.15 = (bf16[256,512]{1,0:T(8,128)(2,1)}, bf16[256,512]{1,0:T(8,128)(2,1)S(1)}, u32[]{:S(2)}, u32[]{:S(2)}) collective-permute-start(bf16[256,512]{1,0:T(8,128)(2,1)} %get-tuple-element.78), channel_id=1, source_target_pairs={{0,1},{1,0},{2,3},{3,2},{4,5},{5,4},{6,7},{7,6},{8,9},{9,8},{10,11... | collective-permute-start | bytes 786440 | tf_op jit(solution)/shard_map/ppermute | solution.py:537
  95.9 14.9 %all-to-all-start.3 = ((bf16[8,16,512]{2,1,0:T(8,128)(2,1)}), bf16[8,16,512]{2,1,0:T(8,128)(2,1)S(1)}, u32[]{:S(2)}, u32[]{:S(2)}) async-start(bf16[8,16,512]{2,1,0:T(8,128)(2,1)} %bitcast.6), calls=%async_computation.3 | async-start | bytes 262144 | tf_op jit(solution)/shard_map/all_to_all | solution.py:528
  101.3 12.1 %copy-start.18 = (bf16[128,512]{1,0:T(8,128)(2,1)S(1)}, bf16[128,512]{1,0:T(8,128)(2,1)}, u32[]{:S(2)}) copy-start(bf16[128,512]{1,0:T(8,128)(2,1)} %get-tuple-element.85) | copy-start | bytes 393220
  106.3 13.5 %copy-start.20 = (f32[128,512]{1,0:T(8,128)S(1)}, f32[128,512]{1,0:T(8,128)}, u32[]{:S(2)}) copy-start(f32[128,512]{1,0:T(8,128)} %get-tuple-element.93) | copy-start | bytes 786436
  106.4 13.6 %copy-start.22 = (f32[112,512]{1,0:T(8,128)S(1)}, f32[112,512]{1,0:T(8,128)}, u32[]{:S(2)}) copy-start(f32[112,512]{1,0:T(8,128)} %get-tuple-element.90) | copy-start | bytes 688132
  106.4 8.1 %collective-permute-start.23 = (bf16[128,512]{1,0:T(8,128)(2,1)}, bf16[128,512]{1,0:T(8,128)(2,1)S(1)}, u32[]{:S(2)}, u32[]{:S(2)}) collective-permute-start(bf16[128,512]{1,0:T(8,128)(2,1)} %get-tuple-element.83), channel_id=1, source_target_pairs={{0,12},{2,14},{4,8},{6,10},{8,4},{10,6},{12,0},{14,2},{1,13},{3,15... | collective-permute-start | bytes 393224 | tf_op jit(solution)/shard_map/ppermute | solution.py:539
  110.2 9.7 %collective-permute-start.22 = (bf16[128,512]{1,0:T(8,128)(2,1)}, bf16[128,512]{1,0:T(8,128)(2,1)S(1)}, u32[]{:S(2)}, u32[]{:S(2)}) collective-permute-start(bf16[128,512]{1,0:T(8,128)(2,1)} %get-tuple-element.82), channel_id=1, source_target_pairs={{0,8},{2,10},{4,12},{6,14},{8,0},{10,2},{12,4},{14,6},{1,9},{3,11}... | collective-permute-start | bytes 393224 | tf_op jit(solution)/shard_map/ppermute | solution.py:539
  110.2 9.7 %collective-permute-start.21 = (bf16[128,512]{1,0:T(8,128)(2,1)}, bf16[128,512]{1,0:T(8,128)(2,1)S(1)}, u32[]{:S(2)}, u32[]{:S(2)}) collective-permute-start(bf16[128,512]{1,0:T(8,128)(2,1)} %get-tuple-element.81), channel_id=1, source_target_pairs={{0,4},{2,6},{4,0},{6,2},{8,12},{10,14},{12,8},{14,10},{1,5},{3,7},... | collective-permute-start | bytes 393224 | tf_op jit(solution)/shard_map/ppermute | solution.py:539
  113.4 6.7 %collective-permute-start.17 = (bf16[128,512]{1,0:T(8,128)(2,1)S(1)}, bf16[128,512]{1,0:T(8,128)(2,1)S(1)}, u32[]{:S(2)}, u32[]{:S(2)}) collective-permute-start(bf16[128,512]{1,0:T(8,128)(2,1)S(1)} %broadcast_select_fusion.1), channel_id=1, source_target_pairs={{0,16},{16,0},{1,17},{17,1},{2,18},{18,2},{3,19},{19,3},{4,20},{20... | collective-permute-start | bytes 393224 | tf_op jit(solution)/shard_map/ppermute | solution.py:532
  113.5 6.4 %collective-permute-start.20 = (bf16[64,512]{1,0:T(8,128)(2,1)}, bf16[64,512]{1,0:T(8,128)(2,1)S(1)}, u32[]{:S(2)}, u32[]{:S(2)}) collective-permute-start(bf16[64,512]{1,0:T(8,128)(2,1)} %get-tuple-element.92), channel_id=1, source_target_pairs={{0,1},{1,0},{2,3},{3,2},{4,5},{5,4},{6,7},{7,6},{8,9},{9,8},{10,11... | collective-permute-start | bytes 196616 | tf_op jit(solution)/shard_map/ppermute | solution.py:537
  114.4 5.5 %collective-permute-start.19 = (bf16[48,512]{1,0:T(8,128)(2,1)}, bf16[48,512]{1,0:T(8,128)(2,1)S(1)}, u32[]{:S(2)}, u32[]{:S(2)}) collective-permute-start(bf16[48,512]{1,0:T(8,128)(2,1)} %get-tuple-element.91), channel_id=1, source_target_pairs={{0,2},{2,0},{4,6},{6,4},{8,10},{10,8},{12,14},{14,12},{1,3},{3,1},... | collective-permute-start | bytes 147464 | tf_op jit(solution)/shard_map/ppermute | solution.py:539
  119.9 0.9 copy-start.15
  120.1 2.1 %collective-permute-start.24 = (f32[112,512]{1,0:T(8,128)S(1)}, f32[112,512]{1,0:T(8,128)S(1)}, u32[]{:S(2)}, u32[]{:S(2)}) collective-permute-start(f32[112,512]{1,0:T(8,128)S(1)} %get-tuple-element.98), channel_id=1, source_target_pairs={{0,16},{16,0},{1,17},{17,1},{2,18},{18,2},{3,19},{19,3},{4,20},{20... | collective-permute-start | bytes 688136 | tf_op jit(solution)/shard_map/ppermute | solution.py:532
  (7 other events, 4.9 us)

commit v5 on v4

--- a/solution.py
+++ b/solution.py
@@ -18,7 +18,7 @@
 F32 = jnp.float32
 GAINS = 16
 VMEM_LIMIT = 63 * 1024 * 1024
-SMALL_LIMIT = 59 * 1024 * 1024
+SMALL_LIMIT = 52 * 1024 * 1024
 
 ROWS = {"ein": 3 * D, "eout": D, "nin": 2 * D, "nout": D}
 GROUPS = {"node": ("nin", "nout"), "edge": ("ein", "eout")}

time: 124 us -> 122 us (0.984)
  Pallas kernels: 36 us -> 32.6 us
  local copies, waits for them, and re-layouts: 8.87 us -> 6.23 us
  waiting for transfers between devices: 15.5 us -> 17.3 us
  starting transfers between devices: 36.7 us -> 38 us
    unnamed x54 -> x48, local copies, waits for them, and re-layouts: 5.82 us -> 3.17 us
    ppermute x9, waiting for transfers between devices: 11.2 us -> 13 us  [across(): lax.ppermute(value, 'dom', [(p, p ^ step) for p in range(lax.axis_size('d...]
    pallas_call x1, Pallas kernels: 1.93 us -> 0.28 us  [own_gradient(): call(last_kernel, [VMEM] * 3, shape((NODE_DEV, D), BF), VMEM, [], 10 ** 7...]
    pallas_call x1, Pallas kernels: 2.48 us -> 1.05 us  [body(): call(pick_kernel, [VMEM, ANY], halo_shape, ANY, [node_s, room_s, dma((2,)...]
    ppermute x4, starting transfers between devices: 5.39 us -> 6.74 us  [across(): return lax.ppermute(value, 'rep', [(0, 1), (1, 0)])]
  transfers between devices with their start and end apart: 28 -> 28, of which waited for: 6 -> 8; matrix products, arithmetic and copies ran while one was open for 13% -> 13% of each run, Pallas kernels for 15% -> 12%
where the time goes in v5:
time: 122 us; the launch traced here: 120 us
  starting transfers between devices  38 us (31%)
  Pallas kernels  32.6 us (27%)
  waiting for transfers between devices  17.3 us (14%)
  other arithmetic  12.8 us (10%)
  blocking collectives  11.3 us (9%)
  local copies, waits for them, and re-layouts  6.23 us (5%)
  between operations  1.73 us (1%)
    ppermute x9, starting transfers between devices, across(): lax.ppermute(value, 'dom', [(p, p ^ step) for p in range(lax.axis_size('d...  14.8 us
    all_to_all x3, starting transfers between devices, exchange(): return lax.all_to_all(rows, 'dom', 0, 0, tiled=True)  14 us
    ppermute x9, waiting for transfers between devices, across(): lax.ppermute(value, 'dom', [(p, p ^ step) for p in range(lax.axis_size('d...  13 us
    all_to_all x1, blocking collectives, exchange(): return lax.all_to_all(rows, 'dom', 0, 0, tiled=True)  11.3 us
    pallas_call x1, Pallas kernels, body(): call(functools.partial(second_kernel, shards), small_specs + [ANY] * (3 +...  10.8 us
    convert_element_type x9, other arithmetic, summed(): return added([a[first:first + rows] for a, first in terms]).astype(BF)  8.22 us
    pallas_call x1, Pallas kernels, body(): call(functools.partial(third_kernel, shards), small_specs + [VMEM] + [ANY...  8.04 us
    ppermute x4, starting transfers between devices, across(): return lax.ppermute(value, 'rep', [(0, 1), (1, 0)])  6.74 us
  transfers between devices with their start and end apart: 28, of which 8 were waited for; matrix products, arithmetic and copies ran while one was open for 13% of the time, Pallas kernels for 12%

profile of v5, /device:TPU:0, one launch (start us, length us, event | category | flops | bytes accessed | tf_op | source)
XLA Modules:
  0.0 120.0 jit_solution(6058648023752232425)
XLA Ops:
  0.6 0.5 collective-permute-start.1
  1.7 0.9 copy-done
  2.7 0.7 copy-done.4
  3.4 1.0 shard_map.188
  4.4 7.3 %all-to-all-start = ((bf16[8,16,512]{2,1,0:T(8,128)(2,1)}), bf16[8,16,512]{2,1,0:T(8,128)(2,1)S(1)}, u32[]{:S(2)}, u32[]{:S(2)}) async-start(bf16[8,16,512]{2,1,0:T(8,128)(2,1)} %bitcast), calls=%async_computation | async-start | bytes 262144 | tf_op jit(solution)/shard_map/all_to_all | solution.py:528
  11.7 0.7 pad_maximum_fusion.3.g_mine
  13.1 1.3 %broadcast_in_dim.24.src = s32[1,384]{1,0:T(1,128)} reshape(s32[384]{0:T(512)} %param.16) | data formatting | bytes 3072 | tf_op jit(solution)/shard_map/broadcast_in_dim | solution.py:673
  14.4 1.3 %broadcast_in_dim.25.dst = s32[1,384]{1,0:T(1,128)} reshape(s32[384]{0:T(512)} %param.17) | data formatting | bytes 3072 | tf_op jit(solution)/shard_map/broadcast_in_dim | solution.py:673
  15.7 3.4 %all-to-all-done = bf16[8,16,512]{2,1,0:T(8,128)(2,1)S(1)} async-done(((bf16[8,16,512]{2,1,0:T(8,128)(2,1)}), bf16[8,16,512]{2,1,0:T(8,128)(2,1)S(1)}, u32[]{:S(2)}, u32[]{:S(2)}) %all-to-all-start) | async-done | bytes 131104 | tf_op jit(solution)/shard_map/all_to_all | solution.py:528
  19.1 0.6 copy-done.18
  19.9 6.3 %shard_map.189 = (bf16[128,512]{1,0:T(8,128)(2,1)}, bf16[384,512]{1,0:T(8,128)(2,1)}, bf16[1664,512]{1,0:T(8,128)(2,1)}, f32[512,128]{1,0:T(8,128)}, bf16[128,512]{1,0:T(8,128)(2,1)}) custom-call(s32[1]{0:T(128)S(6)} %copy.21.count, s32[1,384]{1,0:T(1,128)} %broadcast_in_dim.24.src, s32[1,384]{1,0:T(1,128)} %broadcast_in_dim.25.dst, s32[1,4,16]{2,1,0:T(4,128)} %lists.9, ...), custom_call_target="tpu_custom_call" | custom-call | flops 1100000000 | bytes 26000000 | tf_op jit(solution)/shard_map/pallas_call | solution.py:705
  26.2 11.3 %all_to_all.46 = bf16[8,16,512]{2,1,0:T(8,128)(2,1)} all-to-all(bf16[8,16,512]{2,1,0:T(8,128)(2,1)} %bitcast.30), channel_id=1, replica_groups=mesh['segment'=2,'dom'=8,'rep'=2] {'dom'}, dimensions={0} | all-to-all | bytes 262144 | tf_op jit(solution)/shard_map/all_to_all | solution.py:528
  37.6 10.8 %shard_map.190 = (bf16[128,512]{1,0:T(8,128)(2,1)}, bf16[384,512]{1,0:T(8,128)(2,1)}, f32[16,512]{1,0:T(8,128)}, f32[128,512]{1,0:T(8,128)}, bf16[384,512]{1,0:T...) custom-call(s32[1]{0:T(128)S(6)} %copy.21.count, ...), custom_call_target="tpu_custom_call" | custom-call | flops 2800000000 | bytes 44000000 | tf_op jit(solution)/shard_map/pallas_call | solution.py:745
  49.0 3.4 %all-to-all-start.2 = ((bf16[8,16,512]{2,1,0:T(8,128)(2,1)}), bf16[8,16,512]{2,1,0:T(8,128)(2,1)S(1)}, u32[]{:S(2)}, u32[]{:S(2)}) async-start(bf16[8,16,512]{2,1,0:T(8,128)(2,1)} %bitcast.28), calls=%async_computation.2 | async-start | bytes 262144 | tf_op jit(solution)/shard_map/all_to_all | solution.py:528
  52.4 2.4 %add_convert_fusion.1 = bf16[512,512]{1,0:T(8,128)(2,1)} fusion(bf16[1040,512]{1,0:T(8,128)(2,1)S(1)} %collective-permute-done.6.refs_14_, bf16[1040,512]{1,0:T(8,128)(2,1)} %get-tuple-element.64.refs_13_), kind=kLoop, calls=%fused_computation.1 | loop fusion | flops 1048576 | bytes 1572864 | tf_op jit(solution)/shard_map/convert_element_type | solution.py:635
  54.7 1.9 %collective-permute-start.8 = (bf16[512,512]{1,0:T(8,128)(2,1)}, bf16[512,512]{1,0:T(8,128)(2,1)}, u32[]{:S(2)}, u32[]{:S(2)}) collective-permute-start(bf16[512,512]{1,0:T(8,128)(2,1)} %add_convert_fusion.1), channel_id=1, source_target_pairs={{0,2},{2,0},{4,6},{6,4},{8,10},{10,8},{12,14},{14,12},{1,3},{3,1},... | collective-permute-start | bytes 1572872 | tf_op jit(solution)/shard_map/ppermute | solution.py:539
  56.6 1.0 add_convert_fusion.3
  57.6 1.5 %collective-permute-start.7 = (bf16[384,512]{1,0:T(8,128)(2,1)}, bf16[384,512]{1,0:T(8,128)(2,1)}, u32[]{:S(2)}, u32[]{:S(2)}) collective-permute-start(bf16[384,512]{1,0:T(8,128)(2,1)} %add_convert_fusion.3), channel_id=1, source_target_pairs={{0,1},{1,0},{2,3},{3,2},{4,5},{5,4},{6,7},{7,6},{8,9},{9,8},{10,11... | collective-permute-start | bytes 1179656 | tf_op jit(solution)/shard_map/ppermute | solution.py:537
  59.1 0.8 all-to-all-done.2
  59.9 0.7 copy-done.20
  60.5 8.0 %shard_map.191 = (f32[128,512]{1,0:T(8,128)}, bf16[384,512]{1,0:T(8,128)(2,1)}, bf16[128,512]{1,0:T(8,128)(2,1)}, bf16[768,512]{1,0:T(8,128)(2,1)}, bf16[1040,51...) custom-call(s32[1]{0:T(128)S(6)} %copy.21.count, s32[1,384]{1,0:T(1,128)} %broadcast_in_dim.24.src, ...), custom_call_target="tpu_custom_call" | custom-call | flops 1800000000 | bytes 37000000 | tf_op jit(solution)/shard_map/pallas_call | solution.py:764
  68.6 0.9 collective-permute-done.8.refs_15_
  70.0 1.1 add_convert_fusion.5
  71.1 1.3 %add_convert_fusion.4 = bf16[256,512]{1,0:T(8,128)(2,1)S(1)} fusion(bf16[512,512]{1,0:T(8,128)(2,1)} %collective-permute-done.8.refs_15_, bf16[1040,512]{1,0:T(8,128)(2,1)} %copy-done.10, bf16[1040,512]{1,0:T(8,128)(2,1)} %get-tuple-element.64.refs_13_), kind=kLoop, calls=%fused_computation.5 | loop fusion | flops 786432 | bytes 1048576 | tf_op jit(solution)/shard_map/convert_element_type | solution.py:635
  72.4 1.5 %collective-permute-start.13 = (bf16[448,512]{1,0:T(8,128)(2,1)S(1)}, bf16[448,512]{1,0:T(8,128)(2,1)S(1)}, u32[]{:S(2)}, u32[]{:S(2)}) collective-permute-start(bf16[448,512]{1,0:T(8,128)(2,1)S(1)} %pad_maximum_fusion), channel_id=1, source_target_pairs={{0,4},{2,6},{4,0},{6,2},{8,12},{10,14},{12,8},{14,10},{1,5},{3,7},... | collective-permute-start | bytes 1376264 | tf_op jit(solution)/shard_map/ppermute | solution.py:539
  74.1 1.4 %collective-permute-start.10 = (bf16[512,512]{1,0:T(8,128)(2,1)S(1)}, bf16[512,512]{1,0:T(8,128)(2,1)S(1)}, u32[]{:S(2)}, u32[]{:S(2)}) collective-permute-start(bf16[512,512]{1,0:T(8,128)(2,1)S(1)} %add_convert_fusion), channel_id=1, source_target_pairs={{0,2},{2,0},{4,6},{6,4},{8,10},{10,8},{12,14},{14,12},{1,3},{3,1},... | collective-permute-start | bytes 1572872 | tf_op jit(solution)/shard_map/ppermute | solution.py:539
  75.7 1.6 %collective-permute-start.12 = (bf16[400,512]{1,0:T(8,128)(2,1)S(1)}, bf16[400,512]{1,0:T(8,128)(2,1)S(1)}, u32[]{:S(2)}, u32[]{:S(2)}) collective-permute-start(bf16[400,512]{1,0:T(8,128)(2,1)S(1)} %pad_maximum_fusion.1), channel_id=1, source_target_pairs={{0,1},{1,0},{2,3},{3,2},{4,5},{5,4},{6,7},{7,6},{8,9},{9,8},{10,11... | collective-permute-start | bytes 1228808 | tf_op jit(solution)/shard_map/ppermute | solution.py:537
  77.2 0.8 broadcast_select_fusion
  78.0 6.9 %collective-permute-done.13.refs_11_ = bf16[448,512]{1,0:T(8,128)(2,1)S(1)} collective-permute-done((bf16[448,512]{1,0:T(8,128)(2,1)S(1)}, bf16[448,512]{1,0:T(8,128)(2,1)S(1)}, u32[]{:S(2)}, u32[]{:S(2)}) %collective-permute-start.13) | collective-permute-done | bytes 458784 | tf_op jit(solution)/shard_map/ppermute | solution.py:539
  84.9 1.2 add_convert_fusion.7
  86.1 1.1 add_convert_fusion.6
  87.2 2.2 %collective-permute-start.16 = (bf16[224,512]{1,0:T(8,128)(2,1)S(1)}, bf16[224,512]{1,0:T(8,128)(2,1)S(1)}, u32[]{:S(2)}, u32[]{:S(2)}) collective-permute-start(bf16[224,512]{1,0:T(8,128)(2,1)S(1)} %pad_maximum_fusion.2), channel_id=1, source_target_pairs={{0,8},{2,10},{4,12},{6,14},{8,0},{10,2},{12,4},{14,6},{1,9},{3,11}... | collective-permute-start | bytes 688136 | tf_op jit(solution)/shard_map/ppermute | solution.py:539
  89.5 1.9 %shard_map.192 = (bf16[256,512]{1,0:T(8,128)(2,1)S(1)}, bf16[208,512]{1,0:T(8,128)(2,1)S(1)}) custom-call(bf16[1040,512]{1,0:T(8,128)(2,1)} %get-tuple-element.69.refs_0_, bf16[1040,512]{1,0:T(8,128)(2,1)} %copy-done.7, bf16[512,512]{1,0:T(8,128)(2,1)S(1)} %collective-permute-done.10.refs_2_.refs_6_, bf16[768,512]{1,0:T(8,128)(2,1)} %get-tuple-element.74.refs_3_.refs_4_, ...), custom_call_target="tpu_custom_call" | custom-call | flops 1000000 | bytes 8000000 | tf_op jit(solution)/shard_map/pallas_call | solution.py:618
  91.5 1.4 %collective-permute-start.14 = (bf16[208,512]{1,0:T(8,128)(2,1)S(1)}, bf16[208,512]{1,0:T(8,128)(2,1)S(1)}, u32[]{:S(2)}, u32[]{:S(2)}) collective-permute-start(bf16[208,512]{1,0:T(8,128)(2,1)S(1)} %get-tuple-element.79), channel_id=1, source_target_pairs={{0,2},{2,0},{4,6},{6,4},{8,10},{10,8},{12,14},{14,12},{1,3},{3,1},... | collective-permute-start | bytes 638984 | tf_op jit(solution)/shard_map/ppermute | solution.py:539
  92.9 1.5 %collective-permute-start.15 = (bf16[256,512]{1,0:T(8,128)(2,1)S(1)}, bf16[256,512]{1,0:T(8,128)(2,1)S(1)}, u32[]{:S(2)}, u32[]{:S(2)}) collective-permute-start(bf16[256,512]{1,0:T(8,128)(2,1)S(1)} %get-tuple-element.78), channel_id=1, source_target_pairs={{0,1},{1,0},{2,3},{3,2},{4,5},{5,4},{6,7},{7,6},{8,9},{9,8},{10,11... | collective-permute-start | bytes 786440 | tf_op jit(solution)/shard_map/ppermute | solution.py:537
  94.4 3.4 %all-to-all-start.3 = ((bf16[8,16,512]{2,1,0:T(8,128)(2,1)}), bf16[8,16,512]{2,1,0:T(8,128)(2,1)S(1)}, u32[]{:S(2)}, u32[]{:S(2)}) async-start(bf16[8,16,512]{2,1,0:T(8,128)(2,1)} %bitcast.6), calls=%async_computation.3 | async-start | bytes 262144 | tf_op jit(solution)/shard_map/all_to_all | solution.py:528
  97.8 1.1 select_bitcast_fusion.1
  98.8 0.9 maximum_bitcast_fusion
  99.9 3.4 %shard_map.193 = (bf16[128,512]{1,0:T(8,128)(2,1)S(1)}, bf16[128,512]{1,0:T(8,128)(2,1)S(1)}, bf16[128,512]{1,0:T(8,128)(2,1)S(1)}, f32[128,512]{1,0:T(8,128)S(1...) custom-call(bf16[1040,512]{1,0:T(8,128)(2,1)} %get-tuple-element.69.refs_0_, ...), custom_call_target="tpu_custom_call" | custom-call | flops 1000000 | bytes 8000000 | tf_op jit(solution)/shard_map/pallas_call | solution.py:618
  103.3 4.5 %collective-permute-start.23 = (bf16[128,512]{1,0:T(8,128)(2,1)S(1)}, bf16[128,512]{1,0:T(8,128)(2,1)S(1)}, u32[]{:S(2)}, u32[]{:S(2)}) collective-permute-start(bf16[128,512]{1,0:T(8,128)(2,1)S(1)} %get-tuple-element.83), channel_id=1, source_target_pairs={{0,12},{2,14},{4,8},{6,10},{8,4},{10,6},{12,0},{14,2},{1,13},{3,15... | collective-permute-start | bytes 393224 | tf_op jit(solution)/shard_map/ppermute | solution.py:539
  107.8 0.6 collective-permute-start.21
  108.9 2.2 %collective-permute-start.20 = (bf16[64,512]{1,0:T(8,128)(2,1)S(1)}, bf16[64,512]{1,0:T(8,128)(2,1)S(1)}, u32[]{:S(2)}, u32[]{:S(2)}) collective-permute-start(bf16[64,512]{1,0:T(8,128)(2,1)S(1)} %get-tuple-element.92), channel_id=1, source_target_pairs={{0,1},{1,0},{2,3},{3,2},{4,5},{5,4},{6,7},{7,6},{8,9},{9,8},{10,11... | collective-permute-start | bytes 196616 | tf_op jit(solution)/shard_map/ppermute | solution.py:537
  111.1 1.2 collective-permute-done.23
  112.3 1.3 %collective-permute-start.19 = (bf16[48,512]{1,0:T(8,128)(2,1)S(1)}, bf16[48,512]{1,0:T(8,128)(2,1)S(1)}, u32[]{:S(2)}, u32[]{:S(2)}) collective-permute-start(bf16[48,512]{1,0:T(8,128)(2,1)S(1)} %get-tuple-element.91), channel_id=1, source_target_pairs={{0,2},{2,0},{4,6},{6,4},{8,10},{10,8},{12,14},{14,12},{1,3},{3,1},... | collective-permute-start | bytes 147464 | tf_op jit(solution)/shard_map/ppermute | solution.py:539
  113.5 3.9 %collective-permute-done.22 = bf16[128,512]{1,0:T(8,128)(2,1)S(1)} collective-permute-done((bf16[128,512]{1,0:T(8,128)(2,1)S(1)}, bf16[128,512]{1,0:T(8,128)(2,1)S(1)}, u32[]{:S(2)}, u32[]{:S(2)}) %collective-permute-start.22) | collective-permute-done | bytes 131104 | tf_op jit(solution)/shard_map/ppermute | solution.py:539
  117.8 0.7 maximum_bitcast_fusion.1
  118.6 0.5 fusion
  119.2 0.8 shard_map.195
  (91 shorter events, 3.3 us)
Async XLA Ops:
  0.6 18.4 %collective-permute-start.1 = (bf16[1,1536,512]{2,1,0:T(8,128)(2,1)}, bf16[1,1536,512]{2,1,0:T(8,128)(2,1)}, u32[]{:S(2)}, u32[]{:S(2)}) collective-permute-start(bf16[1,1536,512]{2,1,0:T(8,128)(2,1)} %rest_2_.5), channel_id=1, source_target_pairs={{0,16},{16,0},{1,17},{17,1},{2,18},{18,2},{3,19},{19,3},{4,20},{20... | collective-permute-start | bytes 4718600 | tf_op jit(solution)/shard_map/ppermute | solution.py:532
  1.1 17.9 %collective-permute-start.3 = (bf16[1,1024,512]{2,1,0:T(8,128)(2,1)}, bf16[1,1024,512]{2,1,0:T(8,128)(2,1)}, u32[]{:S(2)}, u32[]{:S(2)}) collective-permute-start(bf16[1,1024,512]{2,1,0:T(8,128)(2,1)} %rest_4_.5), channel_id=1, source_target_pairs={{0,16},{16,0},{1,17},{17,1},{2,18},{18,2},{3,19},{19,3},{4,20},{20... | collective-permute-start | bytes 3145736 | tf_op jit(solution)/shard_map/ppermute | solution.py:532
  1.2 17.8 %collective-permute-start.2 = (bf16[1,512,512]{2,1,0:T(8,128)(2,1)}, bf16[1,512,512]{2,1,0:T(8,128)(2,1)S(1)}, u32[]{:S(2)}, u32[]{:S(2)}) collective-permute-start(bf16[1,512,512]{2,1,0:T(8,128)(2,1)} %rest_3_.5), channel_id=1, source_target_pairs={{0,16},{16,0},{1,17},{17,1},{2,18},{18,2},{3,19},{19,3},{4,20},{20... | collective-permute-start | bytes 1572872 | tf_op jit(solution)/shard_map/ppermute | solution.py:532
  1.7 17.4 %collective-permute-start.4 = (bf16[1,512,512]{2,1,0:T(8,128)(2,1)}, bf16[1,512,512]{2,1,0:T(8,128)(2,1)}, u32[]{:S(2)}, u32[]{:S(2)}) collective-permute-start(bf16[1,512,512]{2,1,0:T(8,128)(2,1)} %rest_5_.1), channel_id=1, source_target_pairs={{0,16},{16,0},{1,17},{17,1},{2,18},{18,2},{3,19},{19,3},{4,20},{20... | collective-permute-start | bytes 1572872 | tf_op jit(solution)/shard_map/ppermute | solution.py:532
  1.7 0.9 copy-start
  4.4 14.6 %all-to-all-start = ((bf16[8,16,512]{2,1,0:T(8,128)(2,1)}), bf16[8,16,512]{2,1,0:T(8,128)(2,1)S(1)}, u32[]{:S(2)}, u32[]{:S(2)}) async-start(bf16[8,16,512]{2,1,0:T(8,128)(2,1)} %bitcast), calls=%async_computation | async-start | bytes 262144 | tf_op jit(solution)/shard_map/all_to_all | solution.py:528
  12.4 6.7 %copy-start.22 = (f32[2,512]{1,0:T(2,128)}, f32[2,512]{1,0:T(2,128)S(1)}, u32[]{:S(2)}) copy-start(f32[2,512]{1,0:T(2,128)S(1)} %pad_maximum_fusion.3.g_mine) | copy-start | bytes 12292
  12.4 3.3 %collective-permute-start = (f32[2,512]{1,0:T(2,128)S(1)}, f32[2,512]{1,0:T(2,128)S(1)}, u32[]{:S(2)}, u32[]{:S(2)}) collective-permute-start(f32[2,512]{1,0:T(2,128)S(1)} %pad_maximum_fusion.3.g_mine), channel_id=1, source_target_pairs={{0,16},{16,0},{1,17},{17,1},{2,18},{18,2},{3,19},{19,3},{4,20},{20... | collective-permute-start | bytes 12296 | tf_op jit(solution)/shard_map/ppermute | solution.py:532
  15.7 3.4 %copy-start.23 = (f32[2,512]{1,0:T(2,128)}, f32[2,512]{1,0:T(2,128)S(1)}, u32[]{:S(2)}) copy-start(f32[2,512]{1,0:T(2,128)S(1)} %collective-permute-done.g_other) | copy-start | bytes 12292
  48.4 8.3 %copy-start.11 = (bf16[768,512]{1,0:T(8,128)(2,1)S(1)}, bf16[768,512]{1,0:T(8,128)(2,1)}, u32[]{:S(2)}) copy-start(bf16[768,512]{1,0:T(8,128)(2,1)} %get-tuple-element.62.refs_8_) | copy-start | bytes 2359300
  48.4 4.0 %collective-permute-start.6 = (bf16[1040,512]{1,0:T(8,128)(2,1)}, bf16[1040,512]{1,0:T(8,128)(2,1)S(1)}, u32[]{:S(2)}, u32[]{:S(2)}) collective-permute-start(bf16[1040,512]{1,0:T(8,128)(2,1)} %get-tuple-element.65), channel_id=1, source_target_pairs={{0,16},{16,0},{1,17},{17,1},{2,18},{18,2},{3,19},{19,3},{4,20},{20... | collective-permute-start | bytes 3194888 | tf_op jit(solution)/shard_map/ppermute | solution.py:532
  48.5 8.2 %collective-permute-start.5 = (bf16[768,512]{1,0:T(8,128)(2,1)}, bf16[768,512]{1,0:T(8,128)(2,1)S(1)}, u32[]{:S(2)}, u32[]{:S(2)}) collective-permute-start(bf16[768,512]{1,0:T(8,128)(2,1)} %get-tuple-element.63), channel_id=1, source_target_pairs={{0,16},{16,0},{1,17},{17,1},{2,18},{18,2},{3,19},{19,3},{4,20},{20... | collective-permute-start | bytes 2359304 | tf_op jit(solution)/shard_map/ppermute | solution.py:532
  49.0 10.9 %all-to-all-start.2 = ((bf16[8,16,512]{2,1,0:T(8,128)(2,1)}), bf16[8,16,512]{2,1,0:T(8,128)(2,1)S(1)}, u32[]{:S(2)}, u32[]{:S(2)}) async-start(bf16[8,16,512]{2,1,0:T(8,128)(2,1)} %bitcast.28), calls=%async_computation.2 | async-start | bytes 262144 | tf_op jit(solution)/shard_map/all_to_all | solution.py:528
  52.4 5.3 %copy-start.10 = (bf16[1040,512]{1,0:T(8,128)(2,1)}, bf16[1040,512]{1,0:T(8,128)(2,1)S(1)}, u32[]{:S(2)}) copy-start(bf16[1040,512]{1,0:T(8,128)(2,1)S(1)} %collective-permute-done.6.refs_14_) | copy-start | bytes 3194884
  54.7 14.7 %collective-permute-start.8 = (bf16[512,512]{1,0:T(8,128)(2,1)}, bf16[512,512]{1,0:T(8,128)(2,1)}, u32[]{:S(2)}, u32[]{:S(2)}) collective-permute-start(bf16[512,512]{1,0:T(8,128)(2,1)} %add_convert_fusion.1), channel_id=1, source_target_pairs={{0,2},{2,0},{4,6},{6,4},{8,10},{10,8},{12,14},{14,12},{1,3},{3,1},... | collective-permute-start | bytes 1572872 | tf_op jit(solution)/shard_map/ppermute | solution.py:539
  56.6 2.5 %copy-start.12 = (bf16[768,512]{1,0:T(8,128)(2,1)}, bf16[768,512]{1,0:T(8,128)(2,1)S(1)}, u32[]{:S(2)}) copy-start(bf16[768,512]{1,0:T(8,128)(2,1)S(1)} %collective-permute-done.5.refs_9_) | copy-start | bytes 2359300
  57.6 11.0 %collective-permute-start.7 = (bf16[384,512]{1,0:T(8,128)(2,1)}, bf16[384,512]{1,0:T(8,128)(2,1)}, u32[]{:S(2)}, u32[]{:S(2)}) collective-permute-start(bf16[384,512]{1,0:T(8,128)(2,1)} %add_convert_fusion.3), channel_id=1, source_target_pairs={{0,1},{1,0},{2,3},{3,2},{4,5},{5,4},{6,7},{7,6},{8,9},{9,8},{10,11... | collective-permute-start | bytes 1179656 | tf_op jit(solution)/shard_map/ppermute | solution.py:537
  69.5 4.5 %collective-permute-start.9 = (bf16[1040,512]{1,0:T(8,128)(2,1)}, bf16[1040,512]{1,0:T(8,128)(2,1)S(1)}, u32[]{:S(2)}, u32[]{:S(2)}) collective-permute-start(bf16[1040,512]{1,0:T(8,128)(2,1)} %get-tuple-element.72), channel_id=1, source_target_pairs={{0,16},{16,0},{1,17},{17,1},{2,18},{18,2},{3,19},{19,3},{4,20},{20... | collective-permute-start | bytes 3194888 | tf_op jit(solution)/shard_map/ppermute | solution.py:532
  69.5 6.0 %collective-permute-start.11 = (bf16[768,512]{1,0:T(8,128)(2,1)}, bf16[768,512]{1,0:T(8,128)(2,1)S(1)}, u32[]{:S(2)}, u32[]{:S(2)}) collective-permute-start(bf16[768,512]{1,0:T(8,128)(2,1)} %get-tuple-element.75), channel_id=1, source_target_pairs={{0,16},{16,0},{1,17},{17,1},{2,18},{18,2},{3,19},{19,3},{4,20},{20... | collective-permute-start | bytes 2359304 | tf_op jit(solution)/shard_map/ppermute | solution.py:532
  71.1 2.9 %copy-start.6 = (bf16[1040,512]{1,0:T(8,128)(2,1)S(1)}, bf16[1040,512]{1,0:T(8,128)(2,1)}, u32[]{:S(2)}) copy-start(bf16[1040,512]{1,0:T(8,128)(2,1)} %get-tuple-element.69.refs_0_) | copy-start | bytes 3194884
  72.4 3.1 %copy-start.8 = (bf16[768,512]{1,0:T(8,128)(2,1)S(1)}, bf16[768,512]{1,0:T(8,128)(2,1)}, u32[]{:S(2)}) copy-start(bf16[768,512]{1,0:T(8,128)(2,1)} %get-tuple-element.74.refs_3_.refs_4_) | copy-start | bytes 2359300
  72.4 12.5 %collective-permute-start.13 = (bf16[448,512]{1,0:T(8,128)(2,1)S(1)}, bf16[448,512]{1,0:T(8,128)(2,1)S(1)}, u32[]{:S(2)}, u32[]{:S(2)}) collective-permute-start(bf16[448,512]{1,0:T(8,128)(2,1)S(1)} %pad_maximum_fusion), channel_id=1, source_target_pairs={{0,4},{2,6},{4,0},{6,2},{8,12},{10,14},{12,8},{14,10},{1,5},{3,7},... | collective-permute-start | bytes 1376264 | tf_op jit(solution)/shard_map/ppermute | solution.py:539
  73.9 1.7 %copy-start.7 = (bf16[1040,512]{1,0:T(8,128)(2,1)}, bf16[1040,512]{1,0:T(8,128)(2,1)S(1)}, u32[]{:S(2)}) copy-start(bf16[1040,512]{1,0:T(8,128)(2,1)S(1)} %collective-permute-done.9.refs_1_) | copy-start | bytes 3194884
  74.1 3.1 %copy-start.14 = (bf16[384,512]{1,0:T(8,128)(2,1)S(1)}, bf16[384,512]{1,0:T(8,128)(2,1)}, u32[]{:S(2)}) copy-start(bf16[384,512]{1,0:T(8,128)(2,1)} %get-tuple-element.89) | copy-start | bytes 1179652
  74.1 3.1 %copy-start.16 = (bf16[384,512]{1,0:T(8,128)(2,1)S(1)}, bf16[384,512]{1,0:T(8,128)(2,1)}, u32[]{:S(2)}) copy-start(bf16[384,512]{1,0:T(8,128)(2,1)} %get-tuple-element.88) | copy-start | bytes 1179652
  74.1 15.4 %collective-permute-start.10 = (bf16[512,512]{1,0:T(8,128)(2,1)S(1)}, bf16[512,512]{1,0:T(8,128)(2,1)S(1)}, u32[]{:S(2)}, u32[]{:S(2)}) collective-permute-start(bf16[512,512]{1,0:T(8,128)(2,1)S(1)} %add_convert_fusion), channel_id=1, source_target_pairs={{0,2},{2,0},{4,6},{6,4},{8,10},{10,8},{12,14},{14,12},{1,3},{3,1},... | collective-permute-start | bytes 1572872 | tf_op jit(solution)/shard_map/ppermute | solution.py:539
  75.5 2.5 %copy-start.9 = (bf16[768,512]{1,0:T(8,128)(2,1)}, bf16[768,512]{1,0:T(8,128)(2,1)S(1)}, u32[]{:S(2)}) copy-start(bf16[768,512]{1,0:T(8,128)(2,1)S(1)} %collective-permute-done.11.refs_4_.refs_5_) | copy-start | bytes 2359300
  75.7 13.8 %collective-permute-start.12 = (bf16[400,512]{1,0:T(8,128)(2,1)S(1)}, bf16[400,512]{1,0:T(8,128)(2,1)S(1)}, u32[]{:S(2)}, u32[]{:S(2)}) collective-permute-start(bf16[400,512]{1,0:T(8,128)(2,1)S(1)} %pad_maximum_fusion.1), channel_id=1, source_target_pairs={{0,1},{1,0},{2,3},{3,2},{4,5},{5,4},{6,7},{7,6},{8,9},{9,8},{10,11... | collective-permute-start | bytes 1228808 | tf_op jit(solution)/shard_map/ppermute | solution.py:537
  78.0 19.7 %collective-permute-start.18 = (bf16[384,512]{1,0:T(8,128)(2,1)}, bf16[384,512]{1,0:T(8,128)(2,1)}, u32[]{:S(2)}, u32[]{:S(2)}) collective-permute-start(bf16[384,512]{1,0:T(8,128)(2,1)} %broadcast_select_fusion), channel_id=1, source_target_pairs={{0,16},{16,0},{1,17},{17,1},{2,18},{18,2},{3,19},{19,3},{4,20},{20... | collective-permute-start | bytes 1179656 | tf_op jit(solution)/shard_map/ppermute | solution.py:532
  84.9 6.5 %copy-start.19 = (bf16[448,512]{1,0:T(8,128)(2,1)}, bf16[448,512]{1,0:T(8,128)(2,1)S(1)}, u32[]{:S(2)}) copy-start(bf16[448,512]{1,0:T(8,128)(2,1)S(1)} %collective-permute-done.13.refs_11_) | copy-start | bytes 1376260
  87.2 10.5 %copy-start.15 = (bf16[384,512]{1,0:T(8,128)(2,1)S(1)}, bf16[384,512]{1,0:T(8,128)(2,1)}, u32[]{:S(2)}) copy-start(bf16[384,512]{1,0:T(8,128)(2,1)} %get-tuple-element.89) | copy-start | bytes 1179652
  87.2 10.5 %copy-start.17 = (bf16[384,512]{1,0:T(8,128)(2,1)S(1)}, bf16[384,512]{1,0:T(8,128)(2,1)}, u32[]{:S(2)}) copy-start(bf16[384,512]{1,0:T(8,128)(2,1)} %get-tuple-element.88) | copy-start | bytes 1179652
  87.2 12.6 %collective-permute-start.16 = (bf16[224,512]{1,0:T(8,128)(2,1)S(1)}, bf16[224,512]{1,0:T(8,128)(2,1)S(1)}, u32[]{:S(2)}, u32[]{:S(2)}) collective-permute-start(bf16[224,512]{1,0:T(8,128)(2,1)S(1)} %pad_maximum_fusion.2), channel_id=1, source_target_pairs={{0,8},{2,10},{4,12},{6,14},{8,0},{10,2},{12,4},{14,6},{1,9},{3,11}... | collective-permute-start | bytes 688136 | tf_op jit(solution)/shard_map/ppermute | solution.py:539
  89.5 2.0 %copy-start.2 = (bf16[400,512]{1,0:T(8,128)(2,1)}, bf16[400,512]{1,0:T(8,128)(2,1)S(1)}, u32[]{:S(2)}) copy-start(bf16[400,512]{1,0:T(8,128)(2,1)S(1)} %collective-permute-done.12.refs_5_.refs_2_) | copy-start | bytes 1228804
  89.5 2.0 %copy-start.1 = (bf16[512,512]{1,0:T(8,128)(2,1)}, bf16[512,512]{1,0:T(8,128)(2,1)S(1)}, u32[]{:S(2)}) copy-start(bf16[512,512]{1,0:T(8,128)(2,1)S(1)} %collective-permute-done.10.refs_2_.refs_6_) | copy-start | bytes 1572868
  91.5 8.4 %collective-permute-start.14 = (bf16[208,512]{1,0:T(8,128)(2,1)S(1)}, bf16[208,512]{1,0:T(8,128)(2,1)S(1)}, u32[]{:S(2)}, u32[]{:S(2)}) collective-permute-start(bf16[208,512]{1,0:T(8,128)(2,1)S(1)} %get-tuple-element.79), channel_id=1, source_target_pairs={{0,2},{2,0},{4,6},{6,4},{8,10},{10,8},{12,14},{14,12},{1,3},{3,1},... | collective-permute-start | bytes 638984 | tf_op jit(solution)/shard_map/ppermute | solution.py:539
  92.9 7.0 %collective-permute-start.15 = (bf16[256,512]{1,0:T(8,128)(2,1)S(1)}, bf16[256,512]{1,0:T(8,128)(2,1)S(1)}, u32[]{:S(2)}, u32[]{:S(2)}) collective-permute-start(bf16[256,512]{1,0:T(8,128)(2,1)S(1)} %get-tuple-element.78), channel_id=1, source_target_pairs={{0,1},{1,0},{2,3},{3,2},{4,5},{5,4},{6,7},{7,6},{8,9},{9,8},{10,11... | collective-permute-start | bytes 786440 | tf_op jit(solution)/shard_map/ppermute | solution.py:537
  94.4 14.1 %all-to-all-start.3 = ((bf16[8,16,512]{2,1,0:T(8,128)(2,1)}), bf16[8,16,512]{2,1,0:T(8,128)(2,1)S(1)}, u32[]{:S(2)}, u32[]{:S(2)}) async-start(bf16[8,16,512]{2,1,0:T(8,128)(2,1)} %bitcast.6), calls=%async_computation.3 | async-start | bytes 262144 | tf_op jit(solution)/shard_map/all_to_all | solution.py:528
  99.8 8.7 %copy-start.3 = (f32[128,512]{1,0:T(8,128)S(1)}, f32[128,512]{1,0:T(8,128)}, u32[]{:S(2)}) copy-start(f32[128,512]{1,0:T(8,128)} %get-tuple-element.67.d_own) | copy-start | bytes 786436
  99.8 8.7 %copy-start.5 = (s32[1,4,16]{2,1,0:T(4,128)S(1)}, s32[1,4,16]{2,1,0:T(4,128)}, u32[]{:S(2)}) copy-start(s32[1,4,16]{2,1,0:T(4,128)} %lists.9) | copy-start | bytes 772
  99.8 9.0 %copy-start.21 = (bf16[128,512]{1,0:T(8,128)(2,1)S(1)}, bf16[128,512]{1,0:T(8,128)(2,1)}, u32[]{:S(2)}) copy-start(bf16[128,512]{1,0:T(8,128)(2,1)} %get-tuple-element.85) | copy-start | bytes 393220
  103.3 9.0 %collective-permute-start.23 = (bf16[128,512]{1,0:T(8,128)(2,1)S(1)}, bf16[128,512]{1,0:T(8,128)(2,1)S(1)}, u32[]{:S(2)}, u32[]{:S(2)}) collective-permute-start(bf16[128,512]{1,0:T(8,128)(2,1)S(1)} %get-tuple-element.83), channel_id=1, source_target_pairs={{0,12},{2,14},{4,8},{6,10},{8,4},{10,6},{12,0},{14,2},{1,13},{3,15... | collective-permute-start | bytes 393224 | tf_op jit(solution)/shard_map/ppermute | solution.py:539
  107.8 9.7 %collective-permute-start.22 = (bf16[128,512]{1,0:T(8,128)(2,1)S(1)}, bf16[128,512]{1,0:T(8,128)(2,1)S(1)}, u32[]{:S(2)}, u32[]{:S(2)}) collective-permute-start(bf16[128,512]{1,0:T(8,128)(2,1)S(1)} %get-tuple-element.82), channel_id=1, source_target_pairs={{0,8},{2,10},{4,12},{6,14},{8,0},{10,2},{12,4},{14,6},{1,9},{3,11}... | collective-permute-start | bytes 393224 | tf_op jit(solution)/shard_map/ppermute | solution.py:539
  107.8 9.7 %collective-permute-start.21 = (bf16[128,512]{1,0:T(8,128)(2,1)S(1)}, bf16[128,512]{1,0:T(8,128)(2,1)S(1)}, u32[]{:S(2)}, u32[]{:S(2)}) collective-permute-start(bf16[128,512]{1,0:T(8,128)(2,1)S(1)} %get-tuple-element.81), channel_id=1, source_target_pairs={{0,4},{2,6},{4,0},{6,2},{8,12},{10,14},{12,8},{14,10},{1,5},{3,7},... | collective-permute-start | bytes 393224 | tf_op jit(solution)/shard_map/ppermute | solution.py:539
  108.8 8.9 %collective-permute-start.17 = (bf16[128,512]{1,0:T(8,128)(2,1)S(1)}, bf16[128,512]{1,0:T(8,128)(2,1)S(1)}, u32[]{:S(2)}, u32[]{:S(2)}) collective-permute-start(bf16[128,512]{1,0:T(8,128)(2,1)S(1)} %broadcast_select_fusion.1), channel_id=1, source_target_pairs={{0,16},{16,0},{1,17},{17,1},{2,18},{18,2},{3,19},{19,3},{4,20},{20... | collective-permute-start | bytes 393224 | tf_op jit(solution)/shard_map/ppermute | solution.py:532
  108.9 8.7 %collective-permute-start.20 = (bf16[64,512]{1,0:T(8,128)(2,1)S(1)}, bf16[64,512]{1,0:T(8,128)(2,1)S(1)}, u32[]{:S(2)}, u32[]{:S(2)}) collective-permute-start(bf16[64,512]{1,0:T(8,128)(2,1)S(1)} %get-tuple-element.92), channel_id=1, source_target_pairs={{0,1},{1,0},{2,3},{3,2},{4,5},{5,4},{6,7},{7,6},{8,9},{9,8},{10,11... | collective-permute-start | bytes 196616 | tf_op jit(solution)/shard_map/ppermute | solution.py:537
  112.3 5.3 %collective-permute-start.19 = (bf16[48,512]{1,0:T(8,128)(2,1)S(1)}, bf16[48,512]{1,0:T(8,128)(2,1)S(1)}, u32[]{:S(2)}, u32[]{:S(2)}) collective-permute-start(bf16[48,512]{1,0:T(8,128)(2,1)S(1)} %get-tuple-element.91), channel_id=1, source_target_pairs={{0,2},{2,0},{4,6},{6,4},{8,10},{10,8},{12,14},{14,12},{1,3},{3,1},... | collective-permute-start | bytes 147464 | tf_op jit(solution)/shard_map/ppermute | solution.py:539
  117.6 1.6 %collective-permute-start.24 = (f32[112,512]{1,0:T(8,128)S(1)}, f32[112,512]{1,0:T(8,128)S(1)}, u32[]{:S(2)}, u32[]{:S(2)}) collective-permute-start(f32[112,512]{1,0:T(8,128)S(1)} %get-tuple-element.98), channel_id=1, source_target_pairs={{0,16},{16,0},{1,17},{17,1},{2,18},{18,2},{3,19},{19,3},{4,20},{20... | collective-permute-start | bytes 688136 | tf_op jit(solution)/shard_map/ppermute | solution.py:532
  (4 other events, 2.8 us)

commit v6 on v5

--- a/solution.py
+++ b/solution.py
@@ -70,20 +70,28 @@
     return rate * (scaled - first - hat * second)
 
 
-def forward(own, edges, table, src, dst, count, weights, waits, gains, res, edges_done):
+def forward(own, edges, table, src, dst, count, weights, waits, gains, res, edges_done, here):
     w_ein, w_eout, w_nin, w_nout = weights
     g_edge, g_node = gains
     rows = edges.shape[0]
+    edges_here, table_here = here
     hot_src = one_hot(table.shape[0], src)
     hot_dst = one_hot(NODE_DEV, dst)
+    table_here()
+    edges_here()
     waits[0]()
-    waits[1]()
     for at in range(0, rows, CHUNK):
         part = slice(at, at + CHUNK)
         edge = edges[part]
+        pre = mm(edge, w_ein[:D])
+        if at == 0:
+            waits[1]()
+            waits[2]()
         sender = t_mm(hot_src[:, part], table[...]).astype(BF)
         receiver = t_mm(hot_dst[:, part], own[...]).astype(BF)
-        pre = mm(edge, w_ein[:D]) + mm(sender, w_ein[D : 2 * D]) + mm(receiver, w_ein[2 * D :])
+        pre = pre + mm(sender, w_ein[D : 2 * D]) + mm(receiver, w_ein[2 * D :])
+        if at == 0:
+            waits[3]()
         middle, slope = silu_pair(pre)
         middle = middle.astype(BF)
         center, rate = normed(mm(middle, w_eout[...]))
@@ -97,8 +105,8 @@
         res["edge_rate"][part] = jnp.broadcast_to(rate, (CHUNK, 128))
     agg = mm(incidence(dst, count), res["edge_new"][...]).astype(BF)
     edges_done()
-    waits[2]()
-    waits[3]()
+    waits[4]()
+    waits[5]()
     pre = mm(own[...], w_nin[:D]) + mm(agg, w_nin[D:])
     middle, slope = silu_pair(pre)
     middle = middle.astype(BF)
@@ -337,6 +345,26 @@
     copies.finish()
 
 
+def weight_parts(weights):
+    first, *others = weights
+    return [first.at[:D], first.at[D : 2 * D], first.at[2 * D :], *others]
+
+
+def arrivals(copies, nodes, own, latents, edges, halo, room, table, core, section, weights):
+    late = copies.start(latents, edges)
+    parts = [weight_parts(v) for v in weights]
+    waits = copies.either(core == section, *[p[:1] for p in parts])
+    coming = [copies.start(nodes, own), copies.start(halo, room)]
+    waits += copies.either(core == section, *[p[1:] for p in parts])
+
+    def table_here():
+        for copy in coming:
+            copy.wait()
+        fill_halo(table, room)
+
+    return waits, (late.wait, table_here)
+
+
 def first_kernel(count, src, dst, lists, g_mine, g_other, nodes, latents, *rest):
     halo, mine, other, rest = rest[0], rest[1:5], rest[5:9], rest[9:]
     (node_out, edge_out, saved_out, rate_out, sent), rest = rest[:5], rest[5:]
@@ -345,16 +373,14 @@
     core = lax.axis_index("segment")
     own = table.at[:NODE_DEV]
     copies = Copies(sems)
-    coming = [copies.start(nodes.at[core], own), copies.start(latents.at[core], edges)]
-    coming += [copies.start(halo, room)]
-    waits = copies.either(core == 0, first_rows(mine), first_rows(other), held)
+    waits, here = arrivals(
+        copies, nodes.at[core], own, latents.at[core], edges, halo, room, table, core, 0,
+        (first_rows(mine), first_rows(other), held),
+    )
     src, dst = src[...], dst[...]
     gains = jnp.where(core == 0, g_mine[...], g_other[...])
     res = views(edges.shape[0], saved, rates)
     res.update(node_new=node_new, edge_new=edge_new)
-    for copy in coming:
-        copy.wait()
-    fill_halo(table, room)
     tall = 3 * edges.shape[0]
 
     def edges_done():
@@ -363,7 +389,7 @@
 
     forward(
         own, edges, table, src, dst, count[0], held, waits, (gains[:1], gains[1:2]), res,
-        edges_done,
+        edges_done, here,
     )
     place(1, pick(one_hots(lists), node_new[...]), room)
     for source, target in (
@@ -406,21 +432,19 @@
     core, me = lax.axis_index("segment"), shard_number(shards)
     own = table.at[:NODE_DEV]
     copies = Copies(sems)
-    coming = [copies.start(nodes, own), copies.start(latents, edges)]
-    coming += [copies.start(halo, room)]
-    waits = copies.either(core == 1, first_rows(mine), first_rows(other), held)
+    waits, here = arrivals(
+        copies, nodes, own, latents, edges, halo, room, table, core, 1,
+        (first_rows(mine), first_rows(other), held),
+    )
     cot_copy = copies.start(cots.at[core], cot)
     src, dst = src[...], dst[...]
     gains = jnp.where(core == 1, g_mine[...], g_other[...])
     gains = (gains[:1], gains[1:2])
     res = views(edges.shape[0], saved, rates)
     res.update(node_new=node_new, edge_new=edge_new)
-    for copy in coming:
-        copy.wait()
-    fill_halo(table, room)
     forward(
         own, edges, table, src, dst, count[0], held, waits, gains, res,
-        lambda: copies.send(edge_new, edge_out),
+        lambda: copies.send(edge_new, edge_out), here,
     )
     copies.send(node_new, node_out)
     cot_copy.wait()

time: 122 us -> 122 us (level)
  no operation moved by 1% of the time
where the time goes in v6:
time: 122 us; the launch traced here: 120 us
  starting transfers between devices  38 us (31%)
  Pallas kernels  32.3 us (26%)
  waiting for transfers between devices  17.3 us (14%)
  other arithmetic  12.8 us (10%)
  blocking collectives  11.3 us (9%)
  local copies, waits for them, and re-layouts  6.23 us (5%)
  between operations  1.73 us (1%)
    ppermute x9, starting transfers between devices, across(): lax.ppermute(value, 'dom', [(p, p ^ step) for p in range(lax.axis_size('d...  14.8 us
    all_to_all x3, starting transfers between devices, exchange(): return lax.all_to_all(rows, 'dom', 0, 0, tiled=True)  14 us
    ppermute x9, waiting for transfers between devices, across(): lax.ppermute(value, 'dom', [(p, p ^ step) for p in range(lax.axis_size('d...  13 us
    all_to_all x1, blocking collectives, exchange(): return lax.all_to_all(rows, 'dom', 0, 0, tiled=True)  11.3 us
    pallas_call x1, Pallas kernels, body(): call(functools.partial(second_kernel, shards), small_specs + [ANY] * (3 +...  10.7 us
    convert_element_type x9, other arithmetic, summed(): return added([a[first:first + rows] for a, first in terms]).astype(BF)  8.22 us
    pallas_call x1, Pallas kernels, body(): call(functools.partial(third_kernel, shards), small_specs + [VMEM] + [ANY...  8.04 us
    ppermute x4, starting transfers between devices, across(): return lax.ppermute(value, 'rep', [(0, 1), (1, 0)])  6.77 us
  transfers between devices with their start and end apart: 28, of which 8 were waited for; matrix products, arithmetic and copies ran while one was open for 13% of the time, Pallas kernels for 12%

profile of v6, /device:TPU:0, one launch (start us, length us, event | category | flops | bytes accessed | tf_op | source)
XLA Modules:
  0.0 119.7 jit_solution(3924739445553937818)
XLA Ops:
  0.6 0.5 collective-permute-start.1
  1.7 0.9 copy-done
  2.7 0.7 copy-done.4
  3.4 1.0 shard_map.188
  4.4 7.3 %all-to-all-start = ((bf16[8,16,512]{2,1,0:T(8,128)(2,1)}), bf16[8,16,512]{2,1,0:T(8,128)(2,1)S(1)}, u32[]{:S(2)}, u32[]{:S(2)}) async-start(bf16[8,16,512]{2,1,0:T(8,128)(2,1)} %bitcast), calls=%async_computation | async-start | bytes 262144 | tf_op jit(solution)/shard_map/all_to_all | solution.py:552
  11.7 0.7 pad_maximum_fusion.3.g_mine
  13.1 1.3 %broadcast_in_dim.24.src = s32[1,384]{1,0:T(1,128)} reshape(s32[384]{0:T(512)} %param.16) | data formatting | bytes 3072 | tf_op jit(solution)/shard_map/broadcast_in_dim | solution.py:697
  14.4 1.3 %broadcast_in_dim.25.dst = s32[1,384]{1,0:T(1,128)} reshape(s32[384]{0:T(512)} %param.17) | data formatting | bytes 3072 | tf_op jit(solution)/shard_map/broadcast_in_dim | solution.py:697
  15.7 3.4 %all-to-all-done = bf16[8,16,512]{2,1,0:T(8,128)(2,1)S(1)} async-done(((bf16[8,16,512]{2,1,0:T(8,128)(2,1)}), bf16[8,16,512]{2,1,0:T(8,128)(2,1)S(1)}, u32[]{:S(2)}, u32[]{:S(2)}) %all-to-all-start) | async-done | bytes 131104 | tf_op jit(solution)/shard_map/all_to_all | solution.py:552
  19.1 0.6 copy-done.18
  19.9 6.1 %shard_map.189 = (bf16[128,512]{1,0:T(8,128)(2,1)}, bf16[384,512]{1,0:T(8,128)(2,1)}, bf16[1664,512]{1,0:T(8,128)(2,1)}, f32[512,128]{1,0:T(8,128)}, bf16[128,512]{1,0:T(8,128)(2,1)}) custom-call(s32[1]{0:T(128)S(6)} %copy.21.count, s32[1,384]{1,0:T(1,128)} %broadcast_in_dim.24.src, s32[1,384]{1,0:T(1,128)} %broadcast_in_dim.25.dst, s32[1,4,16]{2,1,0:T(4,128)} %lists.9, ...), custom_call_target="tpu_custom_call" | custom-call | flops 1100000000 | bytes 26000000 | tf_op jit(solution)/shard_map/pallas_call | solution.py:729
  26.0 11.3 %all_to_all.46 = bf16[8,16,512]{2,1,0:T(8,128)(2,1)} all-to-all(bf16[8,16,512]{2,1,0:T(8,128)(2,1)} %bitcast.30), channel_id=1, replica_groups=mesh['segment'=2,'dom'=8,'rep'=2] {'dom'}, dimensions={0} | all-to-all | bytes 262144 | tf_op jit(solution)/shard_map/all_to_all | solution.py:552
  37.4 10.7 %shard_map.190 = (bf16[128,512]{1,0:T(8,128)(2,1)}, bf16[384,512]{1,0:T(8,128)(2,1)}, f32[16,512]{1,0:T(8,128)}, f32[128,512]{1,0:T(8,128)}, bf16[384,512]{1,0:T...) custom-call(s32[1]{0:T(128)S(6)} %copy.21.count, ...), custom_call_target="tpu_custom_call" | custom-call | flops 2800000000 | bytes 44000000 | tf_op jit(solution)/shard_map/pallas_call | solution.py:769
  48.7 3.4 %all-to-all-start.2 = ((bf16[8,16,512]{2,1,0:T(8,128)(2,1)}), bf16[8,16,512]{2,1,0:T(8,128)(2,1)S(1)}, u32[]{:S(2)}, u32[]{:S(2)}) async-start(bf16[8,16,512]{2,1,0:T(8,128)(2,1)} %bitcast.28), calls=%async_computation.2 | async-start | bytes 262144 | tf_op jit(solution)/shard_map/all_to_all | solution.py:552
  52.0 2.4 %add_convert_fusion.1 = bf16[512,512]{1,0:T(8,128)(2,1)} fusion(bf16[1040,512]{1,0:T(8,128)(2,1)S(1)} %collective-permute-done.6.refs_14_, bf16[1040,512]{1,0:T(8,128)(2,1)} %get-tuple-element.64.refs_13_), kind=kLoop, calls=%fused_computation.1 | loop fusion | flops 1048576 | bytes 1572864 | tf_op jit(solution)/shard_map/convert_element_type | solution.py:659
  54.4 1.9 %collective-permute-start.8 = (bf16[512,512]{1,0:T(8,128)(2,1)}, bf16[512,512]{1,0:T(8,128)(2,1)}, u32[]{:S(2)}, u32[]{:S(2)}) collective-permute-start(bf16[512,512]{1,0:T(8,128)(2,1)} %add_convert_fusion.1), channel_id=1, source_target_pairs={{0,2},{2,0},{4,6},{6,4},{8,10},{10,8},{12,14},{14,12},{1,3},{3,1},... | collective-permute-start | bytes 1572872 | tf_op jit(solution)/shard_map/ppermute | solution.py:563
  56.3 1.0 add_convert_fusion.3
  57.3 1.5 %collective-permute-start.7 = (bf16[384,512]{1,0:T(8,128)(2,1)}, bf16[384,512]{1,0:T(8,128)(2,1)}, u32[]{:S(2)}, u32[]{:S(2)}) collective-permute-start(bf16[384,512]{1,0:T(8,128)(2,1)} %add_convert_fusion.3), channel_id=1, source_target_pairs={{0,1},{1,0},{2,3},{3,2},{4,5},{5,4},{6,7},{7,6},{8,9},{9,8},{10,11... | collective-permute-start | bytes 1179656 | tf_op jit(solution)/shard_map/ppermute | solution.py:561
  58.8 0.8 all-to-all-done.2
  59.6 0.7 copy-done.20
  60.2 8.0 %shard_map.191 = (f32[128,512]{1,0:T(8,128)}, bf16[384,512]{1,0:T(8,128)(2,1)}, bf16[128,512]{1,0:T(8,128)(2,1)}, bf16[768,512]{1,0:T(8,128)(2,1)}, bf16[1040,51...) custom-call(s32[1]{0:T(128)S(6)} %copy.21.count, s32[1,384]{1,0:T(1,128)} %broadcast_in_dim.24.src, ...), custom_call_target="tpu_custom_call" | custom-call | flops 1800000000 | bytes 37000000 | tf_op jit(solution)/shard_map/pallas_call | solution.py:788
  68.3 0.9 collective-permute-done.8.refs_15_
  69.7 1.1 add_convert_fusion.5
  70.8 1.3 %add_convert_fusion.4 = bf16[256,512]{1,0:T(8,128)(2,1)S(1)} fusion(bf16[512,512]{1,0:T(8,128)(2,1)} %collective-permute-done.8.refs_15_, bf16[1040,512]{1,0:T(8,128)(2,1)} %copy-done.10, bf16[1040,512]{1,0:T(8,128)(2,1)} %get-tuple-element.64.refs_13_), kind=kLoop, calls=%fused_computation.5 | loop fusion | flops 786432 | bytes 1048576 | tf_op jit(solution)/shard_map/convert_element_type | solution.py:659
  72.1 1.5 %collective-permute-start.13 = (bf16[448,512]{1,0:T(8,128)(2,1)S(1)}, bf16[448,512]{1,0:T(8,128)(2,1)S(1)}, u32[]{:S(2)}, u32[]{:S(2)}) collective-permute-start(bf16[448,512]{1,0:T(8,128)(2,1)S(1)} %pad_maximum_fusion), channel_id=1, source_target_pairs={{0,4},{2,6},{4,0},{6,2},{8,12},{10,14},{12,8},{14,10},{1,5},{3,7},... | collective-permute-start | bytes 1376264 | tf_op jit(solution)/shard_map/ppermute | solution.py:563
  73.8 1.4 %collective-permute-start.10 = (bf16[512,512]{1,0:T(8,128)(2,1)S(1)}, bf16[512,512]{1,0:T(8,128)(2,1)S(1)}, u32[]{:S(2)}, u32[]{:S(2)}) collective-permute-start(bf16[512,512]{1,0:T(8,128)(2,1)S(1)} %add_convert_fusion), channel_id=1, source_target_pairs={{0,2},{2,0},{4,6},{6,4},{8,10},{10,8},{12,14},{14,12},{1,3},{3,1},... | collective-permute-start | bytes 1572872 | tf_op jit(solution)/shard_map/ppermute | solution.py:563
  75.3 1.6 %collective-permute-start.12 = (bf16[400,512]{1,0:T(8,128)(2,1)S(1)}, bf16[400,512]{1,0:T(8,128)(2,1)S(1)}, u32[]{:S(2)}, u32[]{:S(2)}) collective-permute-start(bf16[400,512]{1,0:T(8,128)(2,1)S(1)} %pad_maximum_fusion.1), channel_id=1, source_target_pairs={{0,1},{1,0},{2,3},{3,2},{4,5},{5,4},{6,7},{7,6},{8,9},{9,8},{10,11... | collective-permute-start | bytes 1228808 | tf_op jit(solution)/shard_map/ppermute | solution.py:561
  76.9 0.8 broadcast_select_fusion
  77.7 6.9 %collective-permute-done.13.refs_11_ = bf16[448,512]{1,0:T(8,128)(2,1)S(1)} collective-permute-done((bf16[448,512]{1,0:T(8,128)(2,1)S(1)}, bf16[448,512]{1,0:T(8,128)(2,1)S(1)}, u32[]{:S(2)}, u32[]{:S(2)}) %collective-permute-start.13) | collective-permute-done | bytes 458784 | tf_op jit(solution)/shard_map/ppermute | solution.py:563
  84.6 1.2 add_convert_fusion.7
  85.8 1.1 add_convert_fusion.6
  86.9 2.2 %collective-permute-start.16 = (bf16[224,512]{1,0:T(8,128)(2,1)S(1)}, bf16[224,512]{1,0:T(8,128)(2,1)S(1)}, u32[]{:S(2)}, u32[]{:S(2)}) collective-permute-start(bf16[224,512]{1,0:T(8,128)(2,1)S(1)} %pad_maximum_fusion.2), channel_id=1, source_target_pairs={{0,8},{2,10},{4,12},{6,14},{8,0},{10,2},{12,4},{14,6},{1,9},{3,11}... | collective-permute-start | bytes 688136 | tf_op jit(solution)/shard_map/ppermute | solution.py:563
  89.2 1.9 %shard_map.192 = (bf16[256,512]{1,0:T(8,128)(2,1)S(1)}, bf16[208,512]{1,0:T(8,128)(2,1)S(1)}) custom-call(bf16[1040,512]{1,0:T(8,128)(2,1)} %get-tuple-element.69.refs_0_, bf16[1040,512]{1,0:T(8,128)(2,1)} %copy-done.7, bf16[512,512]{1,0:T(8,128)(2,1)S(1)} %collective-permute-done.10.refs_2_.refs_6_, bf16[768,512]{1,0:T(8,128)(2,1)} %get-tuple-element.74.refs_3_.refs_4_, ...), custom_call_target="tpu_custom_call" | custom-call | flops 1000000 | bytes 8000000 | tf_op jit(solution)/shard_map/pallas_call | solution.py:642
  91.2 1.4 %collective-permute-start.14 = (bf16[208,512]{1,0:T(8,128)(2,1)S(1)}, bf16[208,512]{1,0:T(8,128)(2,1)S(1)}, u32[]{:S(2)}, u32[]{:S(2)}) collective-permute-start(bf16[208,512]{1,0:T(8,128)(2,1)S(1)} %get-tuple-element.79), channel_id=1, source_target_pairs={{0,2},{2,0},{4,6},{6,4},{8,10},{10,8},{12,14},{14,12},{1,3},{3,1},... | collective-permute-start | bytes 638984 | tf_op jit(solution)/shard_map/ppermute | solution.py:563
  92.6 1.5 %collective-permute-start.15 = (bf16[256,512]{1,0:T(8,128)(2,1)S(1)}, bf16[256,512]{1,0:T(8,128)(2,1)S(1)}, u32[]{:S(2)}, u32[]{:S(2)}) collective-permute-start(bf16[256,512]{1,0:T(8,128)(2,1)S(1)} %get-tuple-element.78), channel_id=1, source_target_pairs={{0,1},{1,0},{2,3},{3,2},{4,5},{5,4},{6,7},{7,6},{8,9},{9,8},{10,11... | collective-permute-start | bytes 786440 | tf_op jit(solution)/shard_map/ppermute | solution.py:561
  94.1 3.4 %all-to-all-start.3 = ((bf16[8,16,512]{2,1,0:T(8,128)(2,1)}), bf16[8,16,512]{2,1,0:T(8,128)(2,1)S(1)}, u32[]{:S(2)}, u32[]{:S(2)}) async-start(bf16[8,16,512]{2,1,0:T(8,128)(2,1)} %bitcast.6), calls=%async_computation.3 | async-start | bytes 262144 | tf_op jit(solution)/shard_map/all_to_all | solution.py:552
  97.5 1.1 select_bitcast_fusion.1
  98.5 0.9 maximum_bitcast_fusion
  99.6 3.4 %shard_map.193 = (bf16[128,512]{1,0:T(8,128)(2,1)S(1)}, bf16[128,512]{1,0:T(8,128)(2,1)S(1)}, bf16[128,512]{1,0:T(8,128)(2,1)S(1)}, f32[128,512]{1,0:T(8,128)S(1...) custom-call(bf16[1040,512]{1,0:T(8,128)(2,1)} %get-tuple-element.69.refs_0_, ...), custom_call_target="tpu_custom_call" | custom-call | flops 1000000 | bytes 8000000 | tf_op jit(solution)/shard_map/pallas_call | solution.py:642
  103.0 4.5 %collective-permute-start.23 = (bf16[128,512]{1,0:T(8,128)(2,1)S(1)}, bf16[128,512]{1,0:T(8,128)(2,1)S(1)}, u32[]{:S(2)}, u32[]{:S(2)}) collective-permute-start(bf16[128,512]{1,0:T(8,128)(2,1)S(1)} %get-tuple-element.83), channel_id=1, source_target_pairs={{0,12},{2,14},{4,8},{6,10},{8,4},{10,6},{12,0},{14,2},{1,13},{3,15... | collective-permute-start | bytes 393224 | tf_op jit(solution)/shard_map/ppermute | solution.py:563
  107.5 0.6 collective-permute-start.21
  108.6 2.2 %collective-permute-start.20 = (bf16[64,512]{1,0:T(8,128)(2,1)S(1)}, bf16[64,512]{1,0:T(8,128)(2,1)S(1)}, u32[]{:S(2)}, u32[]{:S(2)}) collective-permute-start(bf16[64,512]{1,0:T(8,128)(2,1)S(1)} %get-tuple-element.92), channel_id=1, source_target_pairs={{0,1},{1,0},{2,3},{3,2},{4,5},{5,4},{6,7},{7,6},{8,9},{9,8},{10,11... | collective-permute-start | bytes 196616 | tf_op jit(solution)/shard_map/ppermute | solution.py:561
  110.8 1.2 collective-permute-done.23
  112.0 1.3 %collective-permute-start.19 = (bf16[48,512]{1,0:T(8,128)(2,1)S(1)}, bf16[48,512]{1,0:T(8,128)(2,1)S(1)}, u32[]{:S(2)}, u32[]{:S(2)}) collective-permute-start(bf16[48,512]{1,0:T(8,128)(2,1)S(1)} %get-tuple-element.91), channel_id=1, source_target_pairs={{0,2},{2,0},{4,6},{6,4},{8,10},{10,8},{12,14},{14,12},{1,3},{3,1},... | collective-permute-start | bytes 147464 | tf_op jit(solution)/shard_map/ppermute | solution.py:563
  113.2 3.9 %collective-permute-done.22 = bf16[128,512]{1,0:T(8,128)(2,1)S(1)} collective-permute-done((bf16[128,512]{1,0:T(8,128)(2,1)S(1)}, bf16[128,512]{1,0:T(8,128)(2,1)S(1)}, u32[]{:S(2)}, u32[]{:S(2)}) %collective-permute-start.22) | collective-permute-done | bytes 131104 | tf_op jit(solution)/shard_map/ppermute | solution.py:563
  117.5 0.7 maximum_bitcast_fusion.1
  118.3 0.5 fusion
  118.9 0.8 shard_map.195
  (91 shorter events, 3.3 us)
Async XLA Ops:
  0.6 18.4 %collective-permute-start.1 = (bf16[1,1536,512]{2,1,0:T(8,128)(2,1)}, bf16[1,1536,512]{2,1,0:T(8,128)(2,1)}, u32[]{:S(2)}, u32[]{:S(2)}) collective-permute-start(bf16[1,1536,512]{2,1,0:T(8,128)(2,1)} %rest_2_.5), channel_id=1, source_target_pairs={{0,16},{16,0},{1,17},{17,1},{2,18},{18,2},{3,19},{19,3},{4,20},{20... | collective-permute-start | bytes 4718600 | tf_op jit(solution)/shard_map/ppermute | solution.py:556
  1.1 17.9 %collective-permute-start.3 = (bf16[1,1024,512]{2,1,0:T(8,128)(2,1)}, bf16[1,1024,512]{2,1,0:T(8,128)(2,1)}, u32[]{:S(2)}, u32[]{:S(2)}) collective-permute-start(bf16[1,1024,512]{2,1,0:T(8,128)(2,1)} %rest_4_.5), channel_id=1, source_target_pairs={{0,16},{16,0},{1,17},{17,1},{2,18},{18,2},{3,19},{19,3},{4,20},{20... | collective-permute-start | bytes 3145736 | tf_op jit(solution)/shard_map/ppermute | solution.py:556
  1.2 17.8 %collective-permute-start.2 = (bf16[1,512,512]{2,1,0:T(8,128)(2,1)}, bf16[1,512,512]{2,1,0:T(8,128)(2,1)S(1)}, u32[]{:S(2)}, u32[]{:S(2)}) collective-permute-start(bf16[1,512,512]{2,1,0:T(8,128)(2,1)} %rest_3_.5), channel_id=1, source_target_pairs={{0,16},{16,0},{1,17},{17,1},{2,18},{18,2},{3,19},{19,3},{4,20},{20... | collective-permute-start | bytes 1572872 | tf_op jit(solution)/shard_map/ppermute | solution.py:556
  1.7 17.4 %collective-permute-start.4 = (bf16[1,512,512]{2,1,0:T(8,128)(2,1)}, bf16[1,512,512]{2,1,0:T(8,128)(2,1)}, u32[]{:S(2)}, u32[]{:S(2)}) collective-permute-start(bf16[1,512,512]{2,1,0:T(8,128)(2,1)} %rest_5_.1), channel_id=1, source_target_pairs={{0,16},{16,0},{1,17},{17,1},{2,18},{18,2},{3,19},{19,3},{4,20},{20... | collective-permute-start | bytes 1572872 | tf_op jit(solution)/shard_map/ppermute | solution.py:556
  1.7 0.9 copy-start
  4.4 14.6 %all-to-all-start = ((bf16[8,16,512]{2,1,0:T(8,128)(2,1)}), bf16[8,16,512]{2,1,0:T(8,128)(2,1)S(1)}, u32[]{:S(2)}, u32[]{:S(2)}) async-start(bf16[8,16,512]{2,1,0:T(8,128)(2,1)} %bitcast), calls=%async_computation | async-start | bytes 262144 | tf_op jit(solution)/shard_map/all_to_all | solution.py:552
  12.4 6.7 %copy-start.22 = (f32[2,512]{1,0:T(2,128)}, f32[2,512]{1,0:T(2,128)S(1)}, u32[]{:S(2)}) copy-start(f32[2,512]{1,0:T(2,128)S(1)} %pad_maximum_fusion.3.g_mine) | copy-start | bytes 12292
  12.4 3.3 %collective-permute-start = (f32[2,512]{1,0:T(2,128)S(1)}, f32[2,512]{1,0:T(2,128)S(1)}, u32[]{:S(2)}, u32[]{:S(2)}) collective-permute-start(f32[2,512]{1,0:T(2,128)S(1)} %pad_maximum_fusion.3.g_mine), channel_id=1, source_target_pairs={{0,16},{16,0},{1,17},{17,1},{2,18},{18,2},{3,19},{19,3},{4,20},{20... | collective-permute-start | bytes 12296 | tf_op jit(solution)/shard_map/ppermute | solution.py:556
  15.7 3.4 %copy-start.23 = (f32[2,512]{1,0:T(2,128)}, f32[2,512]{1,0:T(2,128)S(1)}, u32[]{:S(2)}) copy-start(f32[2,512]{1,0:T(2,128)S(1)} %collective-permute-done.g_other) | copy-start | bytes 12292
  48.1 8.3 %copy-start.11 = (bf16[768,512]{1,0:T(8,128)(2,1)S(1)}, bf16[768,512]{1,0:T(8,128)(2,1)}, u32[]{:S(2)}) copy-start(bf16[768,512]{1,0:T(8,128)(2,1)} %get-tuple-element.62.refs_8_) | copy-start | bytes 2359300
  48.1 4.0 %collective-permute-start.6 = (bf16[1040,512]{1,0:T(8,128)(2,1)}, bf16[1040,512]{1,0:T(8,128)(2,1)S(1)}, u32[]{:S(2)}, u32[]{:S(2)}) collective-permute-start(bf16[1040,512]{1,0:T(8,128)(2,1)} %get-tuple-element.65), channel_id=1, source_target_pairs={{0,16},{16,0},{1,17},{17,1},{2,18},{18,2},{3,19},{19,3},{4,20},{20... | collective-permute-start | bytes 3194888 | tf_op jit(solution)/shard_map/ppermute | solution.py:556
  48.2 8.2 %collective-permute-start.5 = (bf16[768,512]{1,0:T(8,128)(2,1)}, bf16[768,512]{1,0:T(8,128)(2,1)S(1)}, u32[]{:S(2)}, u32[]{:S(2)}) collective-permute-start(bf16[768,512]{1,0:T(8,128)(2,1)} %get-tuple-element.63), channel_id=1, source_target_pairs={{0,16},{16,0},{1,17},{17,1},{2,18},{18,2},{3,19},{19,3},{4,20},{20... | collective-permute-start | bytes 2359304 | tf_op jit(solution)/shard_map/ppermute | solution.py:556
  48.7 10.9 %all-to-all-start.2 = ((bf16[8,16,512]{2,1,0:T(8,128)(2,1)}), bf16[8,16,512]{2,1,0:T(8,128)(2,1)S(1)}, u32[]{:S(2)}, u32[]{:S(2)}) async-start(bf16[8,16,512]{2,1,0:T(8,128)(2,1)} %bitcast.28), calls=%async_computation.2 | async-start | bytes 262144 | tf_op jit(solution)/shard_map/all_to_all | solution.py:552
  52.0 5.3 %copy-start.10 = (bf16[1040,512]{1,0:T(8,128)(2,1)}, bf16[1040,512]{1,0:T(8,128)(2,1)S(1)}, u32[]{:S(2)}) copy-start(bf16[1040,512]{1,0:T(8,128)(2,1)S(1)} %collective-permute-done.6.refs_14_) | copy-start | bytes 3194884
  54.4 14.7 %collective-permute-start.8 = (bf16[512,512]{1,0:T(8,128)(2,1)}, bf16[512,512]{1,0:T(8,128)(2,1)}, u32[]{:S(2)}, u32[]{:S(2)}) collective-permute-start(bf16[512,512]{1,0:T(8,128)(2,1)} %add_convert_fusion.1), channel_id=1, source_target_pairs={{0,2},{2,0},{4,6},{6,4},{8,10},{10,8},{12,14},{14,12},{1,3},{3,1},... | collective-permute-start | bytes 1572872 | tf_op jit(solution)/shard_map/ppermute | solution.py:563
  56.3 2.5 %copy-start.12 = (bf16[768,512]{1,0:T(8,128)(2,1)}, bf16[768,512]{1,0:T(8,128)(2,1)S(1)}, u32[]{:S(2)}) copy-start(bf16[768,512]{1,0:T(8,128)(2,1)S(1)} %collective-permute-done.5.refs_9_) | copy-start | bytes 2359300
  57.3 11.0 %collective-permute-start.7 = (bf16[384,512]{1,0:T(8,128)(2,1)}, bf16[384,512]{1,0:T(8,128)(2,1)}, u32[]{:S(2)}, u32[]{:S(2)}) collective-permute-start(bf16[384,512]{1,0:T(8,128)(2,1)} %add_convert_fusion.3), channel_id=1, source_target_pairs={{0,1},{1,0},{2,3},{3,2},{4,5},{5,4},{6,7},{7,6},{8,9},{9,8},{10,11... | collective-permute-start | bytes 1179656 | tf_op jit(solution)/shard_map/ppermute | solution.py:561
  69.2 4.5 %collective-permute-start.9 = (bf16[1040,512]{1,0:T(8,128)(2,1)}, bf16[1040,512]{1,0:T(8,128)(2,1)S(1)}, u32[]{:S(2)}, u32[]{:S(2)}) collective-permute-start(bf16[1040,512]{1,0:T(8,128)(2,1)} %get-tuple-element.72), channel_id=1, source_target_pairs={{0,16},{16,0},{1,17},{17,1},{2,18},{18,2},{3,19},{19,3},{4,20},{20... | collective-permute-start | bytes 3194888 | tf_op jit(solution)/shard_map/ppermute | solution.py:556
  69.2 6.0 %collective-permute-start.11 = (bf16[768,512]{1,0:T(8,128)(2,1)}, bf16[768,512]{1,0:T(8,128)(2,1)S(1)}, u32[]{:S(2)}, u32[]{:S(2)}) collective-permute-start(bf16[768,512]{1,0:T(8,128)(2,1)} %get-tuple-element.75), channel_id=1, source_target_pairs={{0,16},{16,0},{1,17},{17,1},{2,18},{18,2},{3,19},{19,3},{4,20},{20... | collective-permute-start | bytes 2359304 | tf_op jit(solution)/shard_map/ppermute | solution.py:556
  70.8 2.9 %copy-start.6 = (bf16[1040,512]{1,0:T(8,128)(2,1)S(1)}, bf16[1040,512]{1,0:T(8,128)(2,1)}, u32[]{:S(2)}) copy-start(bf16[1040,512]{1,0:T(8,128)(2,1)} %get-tuple-element.69.refs_0_) | copy-start | bytes 3194884
  72.1 3.1 %copy-start.8 = (bf16[768,512]{1,0:T(8,128)(2,1)S(1)}, bf16[768,512]{1,0:T(8,128)(2,1)}, u32[]{:S(2)}) copy-start(bf16[768,512]{1,0:T(8,128)(2,1)} %get-tuple-element.74.refs_3_.refs_4_) | copy-start | bytes 2359300
  72.1 12.5 %collective-permute-start.13 = (bf16[448,512]{1,0:T(8,128)(2,1)S(1)}, bf16[448,512]{1,0:T(8,128)(2,1)S(1)}, u32[]{:S(2)}, u32[]{:S(2)}) collective-permute-start(bf16[448,512]{1,0:T(8,128)(2,1)S(1)} %pad_maximum_fusion), channel_id=1, source_target_pairs={{0,4},{2,6},{4,0},{6,2},{8,12},{10,14},{12,8},{14,10},{1,5},{3,7},... | collective-permute-start | bytes 1376264 | tf_op jit(solution)/shard_map/ppermute | solution.py:563
  73.6 1.7 %copy-start.7 = (bf16[1040,512]{1,0:T(8,128)(2,1)}, bf16[1040,512]{1,0:T(8,128)(2,1)S(1)}, u32[]{:S(2)}) copy-start(bf16[1040,512]{1,0:T(8,128)(2,1)S(1)} %collective-permute-done.9.refs_1_) | copy-start | bytes 3194884
  73.8 3.1 %copy-start.14 = (bf16[384,512]{1,0:T(8,128)(2,1)S(1)}, bf16[384,512]{1,0:T(8,128)(2,1)}, u32[]{:S(2)}) copy-start(bf16[384,512]{1,0:T(8,128)(2,1)} %get-tuple-element.89) | copy-start | bytes 1179652
  73.8 3.1 %copy-start.16 = (bf16[384,512]{1,0:T(8,128)(2,1)S(1)}, bf16[384,512]{1,0:T(8,128)(2,1)}, u32[]{:S(2)}) copy-start(bf16[384,512]{1,0:T(8,128)(2,1)} %get-tuple-element.88) | copy-start | bytes 1179652
  73.8 15.4 %collective-permute-start.10 = (bf16[512,512]{1,0:T(8,128)(2,1)S(1)}, bf16[512,512]{1,0:T(8,128)(2,1)S(1)}, u32[]{:S(2)}, u32[]{:S(2)}) collective-permute-start(bf16[512,512]{1,0:T(8,128)(2,1)S(1)} %add_convert_fusion), channel_id=1, source_target_pairs={{0,2},{2,0},{4,6},{6,4},{8,10},{10,8},{12,14},{14,12},{1,3},{3,1},... | collective-permute-start | bytes 1572872 | tf_op jit(solution)/shard_map/ppermute | solution.py:563
  75.2 2.5 %copy-start.9 = (bf16[768,512]{1,0:T(8,128)(2,1)}, bf16[768,512]{1,0:T(8,128)(2,1)S(1)}, u32[]{:S(2)}) copy-start(bf16[768,512]{1,0:T(8,128)(2,1)S(1)} %collective-permute-done.11.refs_4_.refs_5_) | copy-start | bytes 2359300
  75.3 13.8 %collective-permute-start.12 = (bf16[400,512]{1,0:T(8,128)(2,1)S(1)}, bf16[400,512]{1,0:T(8,128)(2,1)S(1)}, u32[]{:S(2)}, u32[]{:S(2)}) collective-permute-start(bf16[400,512]{1,0:T(8,128)(2,1)S(1)} %pad_maximum_fusion.1), channel_id=1, source_target_pairs={{0,1},{1,0},{2,3},{3,2},{4,5},{5,4},{6,7},{7,6},{8,9},{9,8},{10,11... | collective-permute-start | bytes 1228808 | tf_op jit(solution)/shard_map/ppermute | solution.py:561
  77.7 19.7 %collective-permute-start.18 = (bf16[384,512]{1,0:T(8,128)(2,1)}, bf16[384,512]{1,0:T(8,128)(2,1)}, u32[]{:S(2)}, u32[]{:S(2)}) collective-permute-start(bf16[384,512]{1,0:T(8,128)(2,1)} %broadcast_select_fusion), channel_id=1, source_target_pairs={{0,16},{16,0},{1,17},{17,1},{2,18},{18,2},{3,19},{19,3},{4,20},{20... | collective-permute-start | bytes 1179656 | tf_op jit(solution)/shard_map/ppermute | solution.py:556
  84.6 6.5 %copy-start.19 = (bf16[448,512]{1,0:T(8,128)(2,1)}, bf16[448,512]{1,0:T(8,128)(2,1)S(1)}, u32[]{:S(2)}) copy-start(bf16[448,512]{1,0:T(8,128)(2,1)S(1)} %collective-permute-done.13.refs_11_) | copy-start | bytes 1376260
  86.9 10.5 %copy-start.15 = (bf16[384,512]{1,0:T(8,128)(2,1)S(1)}, bf16[384,512]{1,0:T(8,128)(2,1)}, u32[]{:S(2)}) copy-start(bf16[384,512]{1,0:T(8,128)(2,1)} %get-tuple-element.89) | copy-start | bytes 1179652
  86.9 10.5 %copy-start.17 = (bf16[384,512]{1,0:T(8,128)(2,1)S(1)}, bf16[384,512]{1,0:T(8,128)(2,1)}, u32[]{:S(2)}) copy-start(bf16[384,512]{1,0:T(8,128)(2,1)} %get-tuple-element.88) | copy-start | bytes 1179652
  86.9 12.6 %collective-permute-start.16 = (bf16[224,512]{1,0:T(8,128)(2,1)S(1)}, bf16[224,512]{1,0:T(8,128)(2,1)S(1)}, u32[]{:S(2)}, u32[]{:S(2)}) collective-permute-start(bf16[224,512]{1,0:T(8,128)(2,1)S(1)} %pad_maximum_fusion.2), channel_id=1, source_target_pairs={{0,8},{2,10},{4,12},{6,14},{8,0},{10,2},{12,4},{14,6},{1,9},{3,11}... | collective-permute-start | bytes 688136 | tf_op jit(solution)/shard_map/ppermute | solution.py:563
  89.2 2.0 %copy-start.2 = (bf16[400,512]{1,0:T(8,128)(2,1)}, bf16[400,512]{1,0:T(8,128)(2,1)S(1)}, u32[]{:S(2)}) copy-start(bf16[400,512]{1,0:T(8,128)(2,1)S(1)} %collective-permute-done.12.refs_5_.refs_2_) | copy-start | bytes 1228804
  89.2 2.0 %copy-start.1 = (bf16[512,512]{1,0:T(8,128)(2,1)}, bf16[512,512]{1,0:T(8,128)(2,1)S(1)}, u32[]{:S(2)}) copy-start(bf16[512,512]{1,0:T(8,128)(2,1)S(1)} %collective-permute-done.10.refs_2_.refs_6_) | copy-start | bytes 1572868
  91.2 8.4 %collective-permute-start.14 = (bf16[208,512]{1,0:T(8,128)(2,1)S(1)}, bf16[208,512]{1,0:T(8,128)(2,1)S(1)}, u32[]{:S(2)}, u32[]{:S(2)}) collective-permute-start(bf16[208,512]{1,0:T(8,128)(2,1)S(1)} %get-tuple-element.79), channel_id=1, source_target_pairs={{0,2},{2,0},{4,6},{6,4},{8,10},{10,8},{12,14},{14,12},{1,3},{3,1},... | collective-permute-start | bytes 638984 | tf_op jit(solution)/shard_map/ppermute | solution.py:563
  92.6 7.0 %collective-permute-start.15 = (bf16[256,512]{1,0:T(8,128)(2,1)S(1)}, bf16[256,512]{1,0:T(8,128)(2,1)S(1)}, u32[]{:S(2)}, u32[]{:S(2)}) collective-permute-start(bf16[256,512]{1,0:T(8,128)(2,1)S(1)} %get-tuple-element.78), channel_id=1, source_target_pairs={{0,1},{1,0},{2,3},{3,2},{4,5},{5,4},{6,7},{7,6},{8,9},{9,8},{10,11... | collective-permute-start | bytes 786440 | tf_op jit(solution)/shard_map/ppermute | solution.py:561
  94.1 14.1 %all-to-all-start.3 = ((bf16[8,16,512]{2,1,0:T(8,128)(2,1)}), bf16[8,16,512]{2,1,0:T(8,128)(2,1)S(1)}, u32[]{:S(2)}, u32[]{:S(2)}) async-start(bf16[8,16,512]{2,1,0:T(8,128)(2,1)} %bitcast.6), calls=%async_computation.3 | async-start | bytes 262144 | tf_op jit(solution)/shard_map/all_to_all | solution.py:552
  99.5 8.7 %copy-start.3 = (f32[128,512]{1,0:T(8,128)S(1)}, f32[128,512]{1,0:T(8,128)}, u32[]{:S(2)}) copy-start(f32[128,512]{1,0:T(8,128)} %get-tuple-element.67.d_own) | copy-start | bytes 786436
  99.5 8.7 %copy-start.5 = (s32[1,4,16]{2,1,0:T(4,128)S(1)}, s32[1,4,16]{2,1,0:T(4,128)}, u32[]{:S(2)}) copy-start(s32[1,4,16]{2,1,0:T(4,128)} %lists.9) | copy-start | bytes 772
  99.5 9.0 %copy-start.21 = (bf16[128,512]{1,0:T(8,128)(2,1)S(1)}, bf16[128,512]{1,0:T(8,128)(2,1)}, u32[]{:S(2)}) copy-start(bf16[128,512]{1,0:T(8,128)(2,1)} %get-tuple-element.85) | copy-start | bytes 393220
  103.0 9.0 %collective-permute-start.23 = (bf16[128,512]{1,0:T(8,128)(2,1)S(1)}, bf16[128,512]{1,0:T(8,128)(2,1)S(1)}, u32[]{:S(2)}, u32[]{:S(2)}) collective-permute-start(bf16[128,512]{1,0:T(8,128)(2,1)S(1)} %get-tuple-element.83), channel_id=1, source_target_pairs={{0,12},{2,14},{4,8},{6,10},{8,4},{10,6},{12,0},{14,2},{1,13},{3,15... | collective-permute-start | bytes 393224 | tf_op jit(solution)/shard_map/ppermute | solution.py:563
  107.5 9.7 %collective-permute-start.22 = (bf16[128,512]{1,0:T(8,128)(2,1)S(1)}, bf16[128,512]{1,0:T(8,128)(2,1)S(1)}, u32[]{:S(2)}, u32[]{:S(2)}) collective-permute-start(bf16[128,512]{1,0:T(8,128)(2,1)S(1)} %get-tuple-element.82), channel_id=1, source_target_pairs={{0,8},{2,10},{4,12},{6,14},{8,0},{10,2},{12,4},{14,6},{1,9},{3,11}... | collective-permute-start | bytes 393224 | tf_op jit(solution)/shard_map/ppermute | solution.py:563
  107.5 9.7 %collective-permute-start.21 = (bf16[128,512]{1,0:T(8,128)(2,1)S(1)}, bf16[128,512]{1,0:T(8,128)(2,1)S(1)}, u32[]{:S(2)}, u32[]{:S(2)}) collective-permute-start(bf16[128,512]{1,0:T(8,128)(2,1)S(1)} %get-tuple-element.81), channel_id=1, source_target_pairs={{0,4},{2,6},{4,0},{6,2},{8,12},{10,14},{12,8},{14,10},{1,5},{3,7},... | collective-permute-start | bytes 393224 | tf_op jit(solution)/shard_map/ppermute | solution.py:563
  108.5 8.9 %collective-permute-start.17 = (bf16[128,512]{1,0:T(8,128)(2,1)S(1)}, bf16[128,512]{1,0:T(8,128)(2,1)S(1)}, u32[]{:S(2)}, u32[]{:S(2)}) collective-permute-start(bf16[128,512]{1,0:T(8,128)(2,1)S(1)} %broadcast_select_fusion.1), channel_id=1, source_target_pairs={{0,16},{16,0},{1,17},{17,1},{2,18},{18,2},{3,19},{19,3},{4,20},{20... | collective-permute-start | bytes 393224 | tf_op jit(solution)/shard_map/ppermute | solution.py:556
  108.6 8.7 %collective-permute-start.20 = (bf16[64,512]{1,0:T(8,128)(2,1)S(1)}, bf16[64,512]{1,0:T(8,128)(2,1)S(1)}, u32[]{:S(2)}, u32[]{:S(2)}) collective-permute-start(bf16[64,512]{1,0:T(8,128)(2,1)S(1)} %get-tuple-element.92), channel_id=1, source_target_pairs={{0,1},{1,0},{2,3},{3,2},{4,5},{5,4},{6,7},{7,6},{8,9},{9,8},{10,11... | collective-permute-start | bytes 196616 | tf_op jit(solution)/shard_map/ppermute | solution.py:561
  112.0 5.3 %collective-permute-start.19 = (bf16[48,512]{1,0:T(8,128)(2,1)S(1)}, bf16[48,512]{1,0:T(8,128)(2,1)S(1)}, u32[]{:S(2)}, u32[]{:S(2)}) collective-permute-start(bf16[48,512]{1,0:T(8,128)(2,1)S(1)} %get-tuple-element.91), channel_id=1, source_target_pairs={{0,2},{2,0},{4,6},{6,4},{8,10},{10,8},{12,14},{14,12},{1,3},{3,1},... | collective-permute-start | bytes 147464 | tf_op jit(solution)/shard_map/ppermute | solution.py:563
  117.3 1.6 %collective-permute-start.24 = (f32[112,512]{1,0:T(8,128)S(1)}, f32[112,512]{1,0:T(8,128)S(1)}, u32[]{:S(2)}, u32[]{:S(2)}) collective-permute-start(f32[112,512]{1,0:T(8,128)S(1)} %get-tuple-element.98), channel_id=1, source_target_pairs={{0,16},{16,0},{1,17},{17,1},{2,18},{18,2},{3,19},{19,3},{4,20},{20... | collective-permute-start | bytes 688136 | tf_op jit(solution)/shard_map/ppermute | solution.py:556
  (4 other events, 2.8 us)
